TPU v7x, 32 devices: a whole 2x2x4 slice. The times are simulated.
32 devices in a mesh: row: 8 (over z, x), col: 4 (over y, core).
Axes of the slice: x: 2, y: 2, z: 4, core: 2. Of those that a mesh axis runs over, the one named last changes fastest.
Arguments:
- tile_u: bfloat16 [16, 8, 1024, 128], P('row', 'col'), may hold values from -6 to 6
- tile_v: bfloat16 [16, 8, 128, 1024], P('row', 'col'), may hold values from -0.5 to 0.5
- tile_ranks: int32 [16, 8], P('row', 'col'), may hold values from 32 to 128
- inverses: bfloat16 [2, 1024, 1024], replicated, may hold values from -0.005859375 to 0.005859375
- panel_order: int32 [2, 2], replicated, may hold values from 0 to 15, as said below
Outputs:
- trailing: bfloat16 [16, 8, 1024, 1024], P('row', 'col')
Inputs may be any that keep to these rules, and one draw needn't show every extreme that they name: `panel_order`: column 0 names 2 different tile rows, below 16; column 1 names 2 different tile columns, below 8; the last tile row and the last tile column are always among them.
All inputs are finite; a program needn't handle non-finite values.
Results may differ from a plain program's by a relative error of at most 0.0075.
Values may be sent and summed in bfloat16 or wider, within the bound.
No kernel may reach another device: no remote copies, remote signals or barrier semaphores. Data moves between devices by JAX's collectives and lax.ppermute only.
A program may use at most 128 MiB of HBM per device.

v0:
```python
import functools

import jax
import jax.numpy as jnp
from jax import lax
from jax.experimental import pallas as pl
from jax.experimental.pallas import tpu as pltpu
from jax.sharding import PartitionSpec as P

F32 = jnp.float32
BF16 = jnp.bfloat16
VMEM_BYTES = 48 * 1024 * 1024
WHOLE = pl.BlockSpec(memory_space=pltpu.VMEM)
SCALARS = pl.BlockSpec(memory_space=pltpu.SMEM)


def params():
    return pltpu.CompilerParams(vmem_limit_bytes=VMEM_BYTES)


def dot(a, b):
    return jnp.dot(a, b, preferred_element_type=F32)


def swap(block, axis, n, bit, senders=None):
    senders = range(n) if senders is None else sorted(senders)
    return lax.ppermute(block, axis, [(s, s ^ bit) for s in senders])


def upper_bits(n):
    return [1 << b for b in range(1, n.bit_length() - 1)]


def after(value, *others):
    return lax.optimization_barrier((value,) + others)[0]


class Lane:
    def __init__(self, keep, give, axis, n, root):
        self.mine, self.axis, self.n, self.root = keep, axis, n, root
        self.me = lax.axis_index(axis)
        self.known = isinstance(root, int)
        self.holders = {root} if self.known else None
        self.bits = upper_bits(n)[::-1] if self.known else upper_bits(n)
        self.move(1, give)

    def move(self, bit, value):
        got = swap(value, self.axis, self.n, bit, self.holders)
        if self.known:
            self.holders = self.holders | {h ^ bit for h in self.holders}
        same = ((self.root ^ self.me) & bit) == 0
        if self.known and bit == 1:
            same = self.me != (self.root ^ 1)
        self.mine = jnp.where(same, self.mine, got)

    def step(self, k, *others):
        if others:
            self.mine = after(self.mine, *others)
        self.move(self.bits[k], self.mine)


def prep_kernel(order, ranks, u, v, *refs, last_row, last_col):
    rs_uk, rs_ug, rd_uk, rd_ug, rs_vk, rs_vg, rd_vk, rd_vg, c_k, c_g, held, v_sem, u_sems = refs
    rows, cols = u.shape[:2]
    rank, width = v.shape[2:]
    row_dyn = lax.rem(jnp.where(order[0, 0] == last_row, order[1, 0], order[0, 0]), rows)
    col_dyn = lax.rem(jnp.where(order[0, 1] == last_col, order[1, 1], order[0, 1]), cols)
    row_side = lax.rem(lax.axis_index("row"), 2)
    col_side = lax.rem(lax.axis_index("col"), 2)

    fetch = pltpu.make_async_copy(v, held, v_sem)
    fetch.start()
    copies = []
    for i, outs in ((rows - 1, (rs_uk, rs_ug)), (row_dyn, (rd_uk, rd_ug))):
        for slot, j in enumerate((row_side, 1 - row_side)):
            copies.append((u.at[i, j], outs[slot]))
    for which, j in enumerate((cols - 1, col_dyn)):
        for slot, i in enumerate((col_side, 1 - col_side)):
            copies.append((u.at[i, j], (c_k, c_g)[slot].at[which, 0]))
    copies = [pltpu.make_async_copy(a, b, u_sems.at[k]) for k, (a, b) in enumerate(copies)]
    for copy in copies:
        copy.start()
    fetch.wait()

    def kept(i, j):
        row = lax.broadcasted_iota(jnp.int32, (rank, width), 0)
        return jnp.where(row < ranks[i, j], held[i, j], jnp.zeros((), v.dtype))

    for i, outs in ((rows - 1, (rs_vk, rs_vg)), (row_dyn, (rd_vk, rd_vg))):
        for slot, j in enumerate((row_side, 1 - row_side)):
            outs[slot][...] = kept(i, j)
    for which, j in enumerate((cols - 1, col_dyn)):
        for slot, i in enumerate((col_side, 1 - col_side)):
            value = kept(i, j)
            for k in range(width // rank):
                (c_k, c_g)[slot][which, 1, k * rank:(k + 1) * rank, :] = value[:, k * rank:(k + 1) * rank]
    for copy in copies:
        copy.wait()


def solve_kernel(order, inverses, fixed, moving, out, *, last_row):
    fixed_first = order[0, 0] == last_row
    out[0] = dot(inverses[0], jnp.where(fixed_first, fixed[...], moving[...])).astype(BF16)
    out[1] = dot(inverses[1], jnp.where(fixed_first, moving[...], fixed[...])).astype(BF16)


def core_kernel(order, solved, swapped, first, second, v21, v12, out, edge, *, last_col):
    rank, width = v21.shape
    count = width // rank
    swap_first = lax.rem(lax.axis_index("row"), 2) == 1
    step_of = jnp.where(order[0, 1] == last_col, 0, 1)
    for s, more in enumerate((v21, v12)):
        which = step_of if s == 0 else 1 - step_of
        lines = [jnp.concatenate([tiles[which, 1, k * rank:(k + 1) * rank, :] for k in range(count)], axis=1) for tiles in (first, second)]
        tall = jnp.concatenate(lines + [more[...]], axis=0)
        mine, other = solved[s], swapped[s]
        wide = jnp.concatenate([jnp.where(swap_first, other, mine), jnp.where(swap_first, mine, other)], axis=1)
        got = dot(tall, wide).astype(BF16)
        out[s] = got
        late = lax.rem(order[1 - s, 1], 2) == 1
        pivot = jnp.where(late, got[:, rank:], got[:, :rank])
        if s == 0:
            edge[:2 * rank] = pivot[:2 * rank]
        else:
            edge[2 * rank:] = pivot


def final_kernel(order, ranks, u, v, first, second, vp1, vp2, cores, edge, out, *, last_col):
    i, j = pl.program_id(0), pl.program_id(1)
    rank, width = v.shape[2:]
    row = lax.axis_index("row") * pl.num_programs(0) + i
    col = lax.axis_index("col") * pl.num_programs(1) + j
    open1 = jnp.logical_and(row != order[0, 0], col != order[0, 1])
    open2 = jnp.logical_and(open1, jnp.logical_and(row != order[1, 0], col != order[1, 1]))
    m1 = jnp.where(open1, F32(1), F32(0))
    m2 = jnp.where(open2, F32(1), F32(0))
    foot = (cores.shape[1] // rank - 1) * rank
    top = pl.ds(pl.multiple_of(i * rank, rank), rank)
    below = pl.ds(pl.multiple_of(2 * rank + i * rank, rank), rank)

    def left(s, lines):
        return jnp.where(j == 0, cores[s, lines, :rank], cores[s, lines, rank:])

    c1_ij, c1_iq2, c1_p2j = left(0, top), edge[top], left(0, pl.ds(foot, rank))
    high_a, high_b = left(1, top), edge[below]
    low_a = -dot(c1_iq2, left(1, pl.ds(foot, rank)))
    low_b = -dot(c1_iq2, edge[4 * rank:])
    q1p1 = m2 * dot(low_b.astype(BF16), c1_p2j) - m1 * c1_ij.astype(F32)
    q2p1 = m2 * dot(high_b, c1_p2j)
    mix = jnp.concatenate([
        jnp.concatenate([q1p1, -m2 * low_a], axis=1),
        jnp.concatenate([q2p1, -m2 * high_a.astype(F32)], axis=1)], axis=0).astype(BF16)
    change = dot(mix, jnp.concatenate([vp1[0], vp2[0]], axis=0)).astype(BF16)
    line = lax.broadcasted_iota(jnp.int32, (rank, width), 0)
    own = jnp.where(line < ranks[i, j], v[0, 0], jnp.zeros((), BF16))
    right = jnp.concatenate([own, change], axis=0)
    w1 = jnp.where(order[0, 1] == last_col, 0, 1)
    uq1, uq2 = (jnp.where(i == 0, first[w, 0], second[w, 0]) for w in (w1, 1 - w1))
    out[0, 0] = dot(jnp.concatenate([u[0, 0], uq1, uq2], axis=1), right).astype(BF16)


def make(rows_n, cols_n):
    def on_device(tile_u, tile_v, tile_ranks, inverses, panel_order):
        rows, cols, width, rank = tile_u.shape
        last = dict(last_row=rows_n * rows - 1, last_col=cols_n * cols - 1)
        me_row, me_col = lax.axis_index("row"), lax.axis_index("col")
        q1, q2 = panel_order[0, 1], panel_order[1, 1]
        row_first = panel_order[0, 0] == last["last_row"]
        col_first = q1 == last["last_col"]
        row_root = jnp.where(row_first, panel_order[1, 0], panel_order[0, 0]) // rows
        col_root = jnp.where(col_first, q2, q1) // cols
        side_r, side_c = me_row % 2, me_col % 2

        tall = jax.ShapeDtypeStruct((width, rank), BF16)
        flat = jax.ShapeDtypeStruct((rank, width), BF16)
        quad = jax.ShapeDtypeStruct((2, 2, width, rank), BF16)
        anywhere = pl.BlockSpec(memory_space=pl.ANY)
        cut = pl.pallas_call(
            functools.partial(prep_kernel, **last),
            out_shape=[tall] * 4 + [flat] * 4 + [quad] * 2,
            in_specs=[SCALARS, SCALARS, anywhere, anywhere],
            out_specs=[WHOLE] * 10,
            scratch_shapes=[pltpu.VMEM(tile_v.shape, BF16), pltpu.SemaphoreType.DMA(()), pltpu.SemaphoreType.DMA((8,))],
            compiler_params=params(),
        )(panel_order, tile_ranks, tile_u, tile_v)
        rs_uk, rs_ug, rd_uk, rd_ug, rs_vk, rs_vg, rd_vk, rd_vg, c_k, c_g = cut

        def lanes(fixed_keep, fixed_give, moving_keep, moving_give):
            return (Lane(fixed_keep, fixed_give, "row", rows_n, rows_n - 1),
                    Lane(moving_keep, moving_give, "row", rows_n, row_root))

        def by_col(keep, give, roots):
            lane = Lane(keep, give, "col", cols_n, roots)
            for k in range(len(lane.bits)):
                lane.step(k)
            other = swap(lane.mine, "col", cols_n, 1)
            return jnp.where(side_c == 0, lane.mine, other), jnp.where(side_c == 0, other, lane.mine)

        def cross(one, two):
            shape = one.shape[1:]
            cand = jnp.stack([jnp.where(q1 % cols == 0, two[0], two[1]), jnp.where(q2 % cols == 0, one[0], one[1])])
            cand = cand.reshape(2, 2, shape[0] // 2, shape[1])
            keep = jnp.where(side_c == 0, cand[:, 0], cand[:, 1])
            give = jnp.where(side_c == 0, cand[:, 1], cand[:, 0])
            both = jnp.concatenate(by_col(keep, give, jnp.stack([q1 // cols, q2 // cols])[:, None, None]), axis=1)
            return both[0], both[1]

        v_lanes = lanes(rs_vk, rs_vg, rd_vk, rd_vg)
        arrived = [lane.mine for lane in v_lanes]
        u_lanes = lanes(rs_uk, after(rs_ug, *arrived), rd_uk, after(rd_ug, *arrived))
        first, second = by_col(c_k, after(c_g, arrived[1]), jnp.stack([cols_n - 1, col_root])[:, None, None, None])
        for k in range(len(upper_bits(rows_n))):
            for lane in v_lanes:
                lane.step(k)
            arrived = [lane.mine for lane in v_lanes]
            for lane in u_lanes:
                lane.step(k, *arrived)
        fixed, moving = arrived
        mine = jnp.stack([jnp.where(row_first, fixed, moving), jnp.where(row_first, moving, fixed)])
        other = swap(mine, "row", rows_n, 1)
        vp1, vp2 = (jnp.stack([jnp.where(side_r == 0, mine[s], other[s]), jnp.where(side_r == 0, other[s], mine[s])]) for s in range(2))
        v21, v12 = cross(vp1, vp2)

        solved = pl.pallas_call(
            functools.partial(solve_kernel, last_row=last["last_row"]),
            out_shape=jax.ShapeDtypeStruct((2, width, rank), BF16),
            in_specs=[SCALARS] + [WHOLE] * 3,
            out_specs=WHOLE,
            compiler_params=params(),
        )(panel_order, inverses, u_lanes[0].mine, u_lanes[1].mine)
        swapped = swap(solved, "row", rows_n, 1)
        cores, edge = pl.pallas_call(
            functools.partial(core_kernel, last_col=last["last_col"]),
            out_shape=[jax.ShapeDtypeStruct((2, 3 * rank, 2 * rank), BF16), jax.ShapeDtypeStruct((5 * rank, rank), BF16)],
            in_specs=[SCALARS] + [WHOLE] * 6,
            out_specs=[WHOLE] * 2,
            compiler_params=params(),
        )(panel_order, solved, swapped, first, second, v21, v12)
        edge_root = jnp.where(jnp.arange(5 * rank)[:, None] < 2 * rank, q2 // cols, q1 // cols)
        for bit in [1] + upper_bits(cols_n):
            got = swap(edge, "col", cols_n, bit)
            edge = jnp.where(((edge_root ^ me_col) & bit) == 0, edge, got)

        return pl.pallas_call(
            functools.partial(final_kernel, last_col=last["last_col"]),
            out_shape=jax.ShapeDtypeStruct((rows, cols, width, width), BF16),
            grid=(rows, cols),
            in_specs=[
                SCALARS, SCALARS,
                pl.BlockSpec((1, 1, width, rank), lambda i, j: (i, j, 0, 0)),
                pl.BlockSpec((1, 1, rank, width), lambda i, j: (i, j, 0, 0)),
                WHOLE, WHOLE,
                pl.BlockSpec((1, rank, width), lambda i, j: (j, 0, 0)),
                pl.BlockSpec((1, rank, width), lambda i, j: (j, 0, 0)),
                WHOLE, WHOLE],
            out_specs=pl.BlockSpec((1, 1, width, width), lambda i, j: (i, j, 0, 0)),
            compiler_params=params(),
        )(panel_order, tile_ranks, tile_u, tile_v, first, second, vp1, vp2, cores, edge)

    return on_device


def solution(mesh):
    placed = (P("row", "col", None, None), P("row", "col", None, None), P("row", "col"), P(), P())
    return jax.shard_map(
        make(mesh.shape["row"], mesh.shape["col"]),
        mesh=mesh,
        in_specs=placed,
        out_specs=P("row", "col", None, None),
        check_vma=False,
    )
```

profile of v0, /device:TPU:0, one launch (start us, length us, event | category | flops | bytes accessed | tf_op | source)
XLA Modules:
  0.0 119.6 jit_solution(17403264943817605372)
XLA Ops:
  2.6 3.0 %shard_map.55 = (bf16[1024,128]{1,0:T(8,128)(2,1)S(1)}, bf16[1024,128]{1,0:T(8,128)(2,1)S(1)}, bf16[1024,128]{1,0:T(8,128)(2,1)S(1)}, bf16[1024,128]{1,0:T(8,128...) custom-call(s32[2,2]{1,0:T(2,128)S(1)} %copy-done.4, ...), custom_call_target="tpu_custom_call" | custom-call | tf_op jit(solution)/shard_map/pallas_call | solution.py:178
  6.2 2.9 %collective-permute-start = (bf16[128,1024]{1,0:T(8,128)(2,1)}, bf16[128,1024]{1,0:T(8,128)(2,1)}, u32[]{:S(2)}, u32[]{:S(2)}) collective-permute-start(bf16[128,1024]{1,0:T(8,128)(2,1)} %get-tuple-element.27), channel_id=1, source_target_pairs={{0,4},{4,0},{8,12},{12,8},{16,20},{20,16},{24,28},{28,24},{1,5},{5... | collective-permute-start | bytes 786440 | tf_op jit(solution)/shard_map/ppermute | solution.py:27
  9.2 1.3 %collective-permute-start.4 = (bf16[128,1024]{1,0:T(8,128)(2,1)}, bf16[128,1024]{1,0:T(8,128)(2,1)}, u32[]{:S(2)}, u32[]{:S(2)}) collective-permute-start(bf16[128,1024]{1,0:T(8,128)(2,1)} %get-tuple-element.30), channel_id=1, source_target_pairs={{28,24},{29,25},{30,26},{31,27}} | collective-permute-start | bytes 786440 | tf_op jit(solution)/shard_map/ppermute | solution.py:27
  21.0 1.6 %collective-permute-start.7 = (bf16[128,1024]{1,0:T(8,128)(2,1)}, bf16[128,1024]{1,0:T(8,128)(2,1)}, u32[]{:S(2)}, u32[]{:S(2)}) collective-permute-start(bf16[128,1024]{1,0:T(8,128)(2,1)} %broadcast_select_fusion.26), channel_id=1, source_target_pairs={{0,8},{4,12},{8,0},{12,4},{16,24},{20,28},{24,16},{28,20},{1,9},{5... | collective-permute-start | bytes 786440 | tf_op jit(solution)/shard_map/ppermute | solution.py:27
  22.6 1.4 %collective-permute-start.5 = (bf16[128,1024]{1,0:T(8,128)(2,1)S(1)}, bf16[128,1024]{1,0:T(8,128)(2,1)}, u32[]{:S(2)}, u32[]{:S(2)}) collective-permute-start(bf16[128,1024]{1,0:T(8,128)(2,1)S(1)} %broadcast_select_fusion.17), channel_id=1, source_target_pairs={{24,8},{28,12},{25,9},{29,13},{26,10},{30,14},{27,11},{31,15}} | collective-permute-start | bytes 786440 | tf_op jit(solution)/shard_map/ppermute | solution.py:27
  24.0 1.5 %collective-permute-start.13 = (bf16[1024,128]{1,0:T(8,128)(2,1)}, bf16[1024,128]{1,0:T(8,128)(2,1)}, u32[]{:S(2)}, u32[]{:S(2)}) collective-permute-start(bf16[1024,128]{1,0:T(8,128)(2,1)} %copy-done.8), channel_id=1, source_target_pairs={{0,4},{4,0},{8,12},{12,8},{16,20},{20,16},{24,28},{28,24},{1,5},{5... | collective-permute-start | bytes 786440 | tf_op jit(solution)/shard_map/ppermute | solution.py:27
  25.5 3.5 %collective-permute-done.7 = bf16[128,1024]{1,0:T(8,128)(2,1)} collective-permute-done((bf16[128,1024]{1,0:T(8,128)(2,1)}, bf16[128,1024]{1,0:T(8,128)(2,1)}, u32[]{:S(2)}, u32[]{:S(2)}) %collective-permute-start.7) | collective-permute-done | bytes 262176 | tf_op jit(solution)/shard_map/ppermute | solution.py:27
  30.1 4.1 %collective-permute-start.8 = (bf16[128,1024]{1,0:T(8,128)(2,1)S(1)}, bf16[128,1024]{1,0:T(8,128)(2,1)}, u32[]{:S(2)}, u32[]{:S(2)}) collective-permute-start(bf16[128,1024]{1,0:T(8,128)(2,1)S(1)} %broadcast_select_fusion.15), channel_id=1, source_target_pairs={{0,16},{4,20},{8,24},{12,28},{16,0},{20,4},{24,8},{28,12},{1,17},{... | collective-permute-start | bytes 786440 | tf_op jit(solution)/shard_map/ppermute | solution.py:27
  34.2 1.7 %broadcast_select_fusion.18 = bf16[128,1024]{1,0:T(8,128)(2,1)} fusion(bf16[128,1024]{1,0:T(8,128)(2,1)S(1)} %broadcast_select_fusion.17, bf16[128,1024]{1,0:T(8,128)(2,1)} %collective-permute-done.5, pred[]{:T(512)S(6)} %eq.107), kind=kLoop, calls=%fused_computation.35 | loop fusion | flops 131072 | bytes 786433 | tf_op jit(solution)/shard_map/jit(_where)/select_n | solution.py:54
  38.0 9.9 %collective-permute-done.8 = bf16[128,1024]{1,0:T(8,128)(2,1)} collective-permute-done((bf16[128,1024]{1,0:T(8,128)(2,1)S(1)}, bf16[128,1024]{1,0:T(8,128)(2,1)}, u32[]{:S(2)}, u32[]{:S(2)}) %collective-permute-start.8) | collective-permute-done | bytes 262176 | tf_op jit(solution)/shard_map/ppermute | solution.py:27
  48.0 3.1 %collective-permute-done.6 = bf16[128,1024]{1,0:T(8,128)(2,1)S(1)} collective-permute-done((bf16[128,1024]{1,0:T(8,128)(2,1)}, bf16[128,1024]{1,0:T(8,128)(2,1)S(1)}, u32[]{:S(2)}, u32[]{:S(2)}) %collective-permute-start.6) | collective-permute-done | bytes 262176 | tf_op jit(solution)/shard_map/ppermute | solution.py:27
  51.2 3.8 %collective-permute-start.9 = (bf16[2,128,1024]{2,1,0:T(8,128)(2,1)S(1)}, bf16[2,128,1024]{2,1,0:T(8,128)(2,1)S(1)}, u32[]{:S(2)}, u32[]{:S(2)}) collective-permute-start(bf16[2,128,1024]{2,1,0:T(8,128)(2,1)S(1)} %pad_maximum_fusion), channel_id=1, source_target_pairs={{0,4},{4,0},{8,12},{12,8},{16,20},{20,16},{24,28},{28,24},{1,5},{5... | collective-permute-start | bytes 1572872 | tf_op jit(solution)/shard_map/ppermute | solution.py:27
  57.2 1.6 %collective-permute-start.2 = (bf16[2,2,1024,128]{3,2,1,0:T(8,128)(2,1)S(1)}, bf16[2,2,1024,128]{3,2,1,0:T(8,128)(2,1)S(1)}, u32[]{:S(2)}, u32[]{:S(2)}) collective-permute-start(bf16[2,2,1024,128]{3,2,1,0:T(8,128)(2,1)S(1)} %broadcast_select_fusion), channel_id=1, source_target_pairs={{0,2},{1,3},{2,0},{3,1},{4,6},{5,7},{6,4},{7,5},{8,10},{9,11},{10,... | collective-permute-start | bytes 3145736 | tf_op jit(solution)/shard_map/ppermute | solution.py:27
  58.8 6.1 %collective-permute-done.9 = bf16[2,128,1024]{2,1,0:T(8,128)(2,1)S(1)} collective-permute-done((bf16[2,128,1024]{2,1,0:T(8,128)(2,1)S(1)}, bf16[2,128,1024]{2,1,0:T(8,128)(2,1)S(1)}, u32[]{:S(2)}, u32[]{:S(2)}) %collective-permute-start.9) | collective-permute-done | bytes 524320 | tf_op jit(solution)/shard_map/ppermute | solution.py:27
  65.3 4.6 %collective-permute-start.15 = (bf16[1024,128]{1,0:T(8,128)(2,1)S(1)}, bf16[1024,128]{1,0:T(8,128)(2,1)S(1)}, u32[]{:S(2)}, u32[]{:S(2)}) collective-permute-start(bf16[1024,128]{1,0:T(8,128)(2,1)S(1)} %broadcast_select_fusion.10), channel_id=1, source_target_pairs={{0,16},{4,20},{8,24},{12,28},{16,0},{20,4},{24,8},{28,12},{1,17},{... | collective-permute-start | bytes 786440 | tf_op jit(solution)/shard_map/ppermute | solution.py:27
  71.3 1.6 %collective-permute-start.18 = (bf16[2,64,1024]{2,1,0:T(8,128)(2,1)S(1)}, bf16[2,64,1024]{2,1,0:T(8,128)(2,1)S(1)}, u32[]{:S(2)}, u32[]{:S(2)}) collective-permute-start(bf16[2,64,1024]{2,1,0:T(8,128)(2,1)S(1)} %bitcast_select_fusion), channel_id=1, source_target_pairs={{0,2},{1,3},{2,0},{3,1},{4,6},{5,7},{6,4},{7,5},{8,10},{9,11},{10,... | collective-permute-start | bytes 786440 | tf_op jit(solution)/shard_map/ppermute | solution.py:27
  72.9 9.5 %collective-permute-done.2 = bf16[2,2,1024,128]{3,2,1,0:T(8,128)(2,1)S(1)} collective-permute-done((bf16[2,2,1024,128]{3,2,1,0:T(8,128)(2,1)S(1)}, bf16[2,2,1024,128]{3,2,1,0:T(8,128)(2,1)S(1)}, u32[]{:S(2)}, u32[]{:S(2)}) %collective-permute-start.2) | collective-permute-done | bytes 1048608 | tf_op jit(solution)/shard_map/ppermute | solution.py:27
  82.6 2.6 %collective-permute-done.18 = bf16[2,64,1024]{2,1,0:T(8,128)(2,1)S(1)} collective-permute-done((bf16[2,64,1024]{2,1,0:T(8,128)(2,1)S(1)}, bf16[2,64,1024]{2,1,0:T(8,128)(2,1)S(1)}, u32[]{:S(2)}, u32[]{:S(2)}) %collective-permute-start.18) | collective-permute-done | bytes 262176 | tf_op jit(solution)/shard_map/ppermute | solution.py:27
  85.5 1.8 %shard_map.56.solved = bf16[2,1024,128]{2,1,0:T(8,128)(2,1)S(1)} custom-call(s32[2,2]{1,0:T(2,128)S(1)} %copy-done.5, bf16[2,1024,1024]{2,1,0:T(8,128)(2,1)S(1)} %copy-done, bf16[1024,128]{1,0:T(8,128)(2,1)S(1)} %broadcast_select_fusion.14.fixed, bf16[1024,128]{1,0:T(8,128)(2,1)S(1)} %broadcast_select_fusion.11.moving), custom_call_target="tpu_custom_call" | custom-call | tf_op jit(solution)/shard_map/pallas_call | solution.py:224
  88.2 13.5 %collective-permute-done.16.swapped = bf16[2,1024,128]{2,1,0:T(8,128)(2,1)S(1)} collective-permute-done((bf16[2,1024,128]{2,1,0:T(8,128)(2,1)S(1)}, bf16[2,1024,128]{2,1,0:T(8,128)(2,1)S(1)}, u32[]{:S(2)}, u32[]{:S(2)}) %collective-permute-start.16) | collective-permute-done | bytes 524320 | tf_op jit(solution)/shard_map/ppermute | solution.py:27
  102.9 1.4 %collective-permute-done.20 = bf16[640,128]{1,0:T(8,128)(2,1)S(1)} collective-permute-done((bf16[640,128]{1,0:T(8,128)(2,1)S(1)}, bf16[640,128]{1,0:T(8,128)(2,1)S(1)}, u32[]{:S(2)}, u32[]{:S(2)}) %collective-permute-start.20) | collective-permute-done | bytes 163872 | tf_op jit(solution)/shard_map/ppermute | solution.py:27
  104.5 1.6 %collective-permute-start.21 = (bf16[640,128]{1,0:T(8,128)(2,1)S(1)}, bf16[640,128]{1,0:T(8,128)(2,1)S(1)}, u32[]{:S(2)}, u32[]{:S(2)}) collective-permute-start(bf16[640,128]{1,0:T(8,128)(2,1)S(1)} %broadcast_select_fusion.27), channel_id=1, source_target_pairs={{0,2},{1,3},{2,0},{3,1},{4,6},{5,7},{6,4},{7,5},{8,10},{9,11},{10,... | collective-permute-start | bytes 491528 | tf_op jit(solution)/shard_map/ppermute | solution.py:27
  106.1 4.6 %collective-permute-done.21 = bf16[640,128]{1,0:T(8,128)(2,1)S(1)} collective-permute-done((bf16[640,128]{1,0:T(8,128)(2,1)S(1)}, bf16[640,128]{1,0:T(8,128)(2,1)S(1)}, u32[]{:S(2)}, u32[]{:S(2)}) %collective-permute-start.21) | collective-permute-done | bytes 163872 | tf_op jit(solution)/shard_map/ppermute | solution.py:27
  111.0 8.7 %shard_map.58 = bf16[2,2,1024,1024]{3,2,1,0:T(8,128)(2,1)} custom-call(s32[2,2]{1,0:T(2,128)S(1)} %copy-done.5, s32[2,2]{1,0:T(2,128)S(1)} %copy-done.7, bf16[2,2,1024,128]{3,2,1,0:T(8,128)(2,1)S(1)} %copy-done.2, bf16[2,2,128,1024]{3,2,1,0:T(8,128)(2,1)S(1)} %copy-done.3, bf16[2,2,1024,128]{3,2,1,0:T(8,128)(2,1)S(1)} %get-tuple-element.51.first, ...), custom_call_target="tpu_custom_call" | custom-call | tf_op jit(solution)/shard_map/pallas_call | solution.py:244
  (74 shorter events, 15.0 us)
Async XLA Ops:
  6.2 14.0 %collective-permute-start = (bf16[128,1024]{1,0:T(8,128)(2,1)}, bf16[128,1024]{1,0:T(8,128)(2,1)}, u32[]{:S(2)}, u32[]{:S(2)}) collective-permute-start(bf16[128,1024]{1,0:T(8,128)(2,1)} %get-tuple-element.27), channel_id=1, source_target_pairs={{0,4},{4,0},{8,12},{12,8},{16,20},{20,16},{24,28},{28,24},{1,5},{5... | collective-permute-start | bytes 786440 | tf_op jit(solution)/shard_map/ppermute | solution.py:27
  9.2 13.4 %collective-permute-start.4 = (bf16[128,1024]{1,0:T(8,128)(2,1)}, bf16[128,1024]{1,0:T(8,128)(2,1)}, u32[]{:S(2)}, u32[]{:S(2)}) collective-permute-start(bf16[128,1024]{1,0:T(8,128)(2,1)} %get-tuple-element.30), channel_id=1, source_target_pairs={{28,24},{29,25},{30,26},{31,27}} | collective-permute-start | bytes 786440 | tf_op jit(solution)/shard_map/ppermute | solution.py:27
  21.0 8.1 %collective-permute-start.7 = (bf16[128,1024]{1,0:T(8,128)(2,1)}, bf16[128,1024]{1,0:T(8,128)(2,1)}, u32[]{:S(2)}, u32[]{:S(2)}) collective-permute-start(bf16[128,1024]{1,0:T(8,128)(2,1)} %broadcast_select_fusion.26), channel_id=1, source_target_pairs={{0,8},{4,12},{8,0},{12,4},{16,24},{20,28},{24,16},{28,20},{1,9},{5... | collective-permute-start | bytes 786440 | tf_op jit(solution)/shard_map/ppermute | solution.py:27
  22.6 11.6 %collective-permute-start.5 = (bf16[128,1024]{1,0:T(8,128)(2,1)S(1)}, bf16[128,1024]{1,0:T(8,128)(2,1)}, u32[]{:S(2)}, u32[]{:S(2)}) collective-permute-start(bf16[128,1024]{1,0:T(8,128)(2,1)S(1)} %broadcast_select_fusion.17), channel_id=1, source_target_pairs={{24,8},{28,12},{25,9},{29,13},{26,10},{30,14},{27,11},{31,15}} | collective-permute-start | bytes 786440 | tf_op jit(solution)/shard_map/ppermute | solution.py:27
  24.0 13.9 %collective-permute-start.13 = (bf16[1024,128]{1,0:T(8,128)(2,1)}, bf16[1024,128]{1,0:T(8,128)(2,1)}, u32[]{:S(2)}, u32[]{:S(2)}) collective-permute-start(bf16[1024,128]{1,0:T(8,128)(2,1)} %copy-done.8), channel_id=1, source_target_pairs={{0,4},{4,0},{8,12},{12,8},{16,20},{20,16},{24,28},{28,24},{1,5},{5... | collective-permute-start | bytes 786440 | tf_op jit(solution)/shard_map/ppermute | solution.py:27
  30.1 17.9 %collective-permute-start.8 = (bf16[128,1024]{1,0:T(8,128)(2,1)S(1)}, bf16[128,1024]{1,0:T(8,128)(2,1)}, u32[]{:S(2)}, u32[]{:S(2)}) collective-permute-start(bf16[128,1024]{1,0:T(8,128)(2,1)S(1)} %broadcast_select_fusion.15), channel_id=1, source_target_pairs={{0,16},{4,20},{8,24},{12,28},{16,0},{20,4},{24,8},{28,12},{1,17},{... | collective-permute-start | bytes 786440 | tf_op jit(solution)/shard_map/ppermute | solution.py:27
  35.9 15.1 %collective-permute-start.6 = (bf16[128,1024]{1,0:T(8,128)(2,1)}, bf16[128,1024]{1,0:T(8,128)(2,1)S(1)}, u32[]{:S(2)}, u32[]{:S(2)}) collective-permute-start(bf16[128,1024]{1,0:T(8,128)(2,1)} %broadcast_select_fusion.18), channel_id=1, source_target_pairs={{8,0},{12,4},{24,16},{28,20},{9,1},{13,5},{25,17},{29,21},{10,2},{... | collective-permute-start | bytes 786440 | tf_op jit(solution)/shard_map/ppermute | solution.py:27
  37.2 17.8 %collective-permute-start.10 = (bf16[1024,128]{1,0:T(8,128)(2,1)S(1)}, bf16[1024,128]{1,0:T(8,128)(2,1)S(1)}, u32[]{:S(2)}, u32[]{:S(2)}) collective-permute-start(bf16[1024,128]{1,0:T(8,128)(2,1)S(1)} %get-tuple-element.33), channel_id=1, source_target_pairs={{28,24},{29,25},{30,26},{31,27}} | collective-permute-start | bytes 786440 | tf_op jit(solution)/shard_map/ppermute | solution.py:27
  37.9 19.1 %collective-permute-start.1 = (bf16[2,2,1024,128]{3,2,1,0:T(8,128)(2,1)S(1)}, bf16[2,2,1024,128]{3,2,1,0:T(8,128)(2,1)S(1)}, u32[]{:S(2)}, u32[]{:S(2)}) collective-permute-start(bf16[2,2,1024,128]{3,2,1,0:T(8,128)(2,1)S(1)} %get-tuple-element.28), channel_id=1, source_target_pairs={{0,1},{1,0},{2,3},{3,2},{4,5},{5,4},{6,7},{7,6},{8,9},{9,8},{10,11... | collective-permute-start | bytes 3145736 | tf_op jit(solution)/shard_map/ppermute | solution.py:27
  51.1 34.3 %copy-start = (bf16[2,1024,1024]{2,1,0:T(8,128)(2,1)S(1)}, bf16[2,1024,1024]{2,1,0:T(8,128)(2,1)}, u32[]{:S(2)}) copy-start(bf16[2,1024,1024]{2,1,0:T(8,128)(2,1)} %inverses.1) | copy-start | bytes 12582916
  51.1 34.3 %copy-start.5 = (s32[2,2]{1,0:T(2,128)S(1)}, s32[2,2]{1,0:T(2,128)}, u32[]{:S(2)}) copy-start(s32[2,2]{1,0:T(2,128)} %order.7) | copy-start | bytes 52
  51.2 13.7 %collective-permute-start.9 = (bf16[2,128,1024]{2,1,0:T(8,128)(2,1)S(1)}, bf16[2,128,1024]{2,1,0:T(8,128)(2,1)S(1)}, u32[]{:S(2)}, u32[]{:S(2)}) collective-permute-start(bf16[2,128,1024]{2,1,0:T(8,128)(2,1)S(1)} %pad_maximum_fusion), channel_id=1, source_target_pairs={{0,4},{4,0},{8,12},{12,8},{16,20},{20,16},{24,28},{28,24},{1,5},{5... | collective-permute-start | bytes 1572872 | tf_op jit(solution)/shard_map/ppermute | solution.py:27
  55.0 10.1 %collective-permute-start.11 = (bf16[1024,128]{1,0:T(8,128)(2,1)S(1)}, bf16[1024,128]{1,0:T(8,128)(2,1)S(1)}, u32[]{:S(2)}, u32[]{:S(2)}) collective-permute-start(bf16[1024,128]{1,0:T(8,128)(2,1)S(1)} %broadcast_select_fusion.12), channel_id=1, source_target_pairs={{24,8},{28,12},{25,9},{29,13},{26,10},{30,14},{27,11},{31,15}} | collective-permute-start | bytes 786440 | tf_op jit(solution)/shard_map/ppermute | solution.py:27
  55.7 9.5 %collective-permute-start.14 = (bf16[1024,128]{1,0:T(8,128)(2,1)S(1)}, bf16[1024,128]{1,0:T(8,128)(2,1)S(1)}, u32[]{:S(2)}, u32[]{:S(2)}) collective-permute-start(bf16[1024,128]{1,0:T(8,128)(2,1)S(1)} %broadcast_select_fusion.9), channel_id=1, source_target_pairs={{0,8},{4,12},{8,0},{12,4},{16,24},{20,28},{24,16},{28,20},{1,9},{5... | collective-permute-start | bytes 786440 | tf_op jit(solution)/shard_map/ppermute | solution.py:27
  57.2 25.2 %collective-permute-start.2 = (bf16[2,2,1024,128]{3,2,1,0:T(8,128)(2,1)S(1)}, bf16[2,2,1024,128]{3,2,1,0:T(8,128)(2,1)S(1)}, u32[]{:S(2)}, u32[]{:S(2)}) collective-permute-start(bf16[2,2,1024,128]{3,2,1,0:T(8,128)(2,1)S(1)} %broadcast_select_fusion), channel_id=1, source_target_pairs={{0,2},{1,3},{2,0},{3,1},{4,6},{5,7},{6,4},{7,5},{8,10},{9,11},{10,... | collective-permute-start | bytes 3145736 | tf_op jit(solution)/shard_map/ppermute | solution.py:27
  65.1 6.1 %collective-permute-start.17 = (bf16[2,64,1024]{2,1,0:T(8,128)(2,1)S(1)}, bf16[2,64,1024]{2,1,0:T(8,128)(2,1)S(1)}, u32[]{:S(2)}, u32[]{:S(2)}) collective-permute-start(bf16[2,64,1024]{2,1,0:T(8,128)(2,1)S(1)} %select_bitcast_fusion), channel_id=1, source_target_pairs={{0,1},{1,0},{2,3},{3,2},{4,5},{5,4},{6,7},{7,6},{8,9},{9,8},{10,11... | collective-permute-start | bytes 786440 | tf_op jit(solution)/shard_map/ppermute | solution.py:27
  65.3 20.1 %collective-permute-start.15 = (bf16[1024,128]{1,0:T(8,128)(2,1)S(1)}, bf16[1024,128]{1,0:T(8,128)(2,1)S(1)}, u32[]{:S(2)}, u32[]{:S(2)}) collective-permute-start(bf16[1024,128]{1,0:T(8,128)(2,1)S(1)} %broadcast_select_fusion.10), channel_id=1, source_target_pairs={{0,16},{4,20},{8,24},{12,28},{16,0},{20,4},{24,8},{28,12},{1,17},{... | collective-permute-start | bytes 786440 | tf_op jit(solution)/shard_map/ppermute | solution.py:27
  69.9 15.5 %collective-permute-start.12 = (bf16[1024,128]{1,0:T(8,128)(2,1)S(1)}, bf16[1024,128]{1,0:T(8,128)(2,1)S(1)}, u32[]{:S(2)}, u32[]{:S(2)}) collective-permute-start(bf16[1024,128]{1,0:T(8,128)(2,1)S(1)} %broadcast_select_fusion.13), channel_id=1, source_target_pairs={{8,0},{12,4},{24,16},{28,20},{9,1},{13,5},{25,17},{29,21},{10,2},{... | collective-permute-start | bytes 786440 | tf_op jit(solution)/shard_map/ppermute | solution.py:27
  71.3 13.9 %collective-permute-start.18 = (bf16[2,64,1024]{2,1,0:T(8,128)(2,1)S(1)}, bf16[2,64,1024]{2,1,0:T(8,128)(2,1)S(1)}, u32[]{:S(2)}, u32[]{:S(2)}) collective-permute-start(bf16[2,64,1024]{2,1,0:T(8,128)(2,1)S(1)} %bitcast_select_fusion), channel_id=1, source_target_pairs={{0,2},{1,3},{2,0},{3,1},{4,6},{5,7},{6,4},{7,5},{8,10},{9,11},{10,... | collective-permute-start | bytes 786440 | tf_op jit(solution)/shard_map/ppermute | solution.py:27
  82.5 5.5 %collective-permute-start.3 = (bf16[2,2,1024,128]{3,2,1,0:T(8,128)(2,1)S(1)}, bf16[2,2,1024,128]{3,2,1,0:T(8,128)(2,1)S(1)}, u32[]{:S(2)}, u32[]{:S(2)}) collective-permute-start(bf16[2,2,1024,128]{3,2,1,0:T(8,128)(2,1)S(1)} %broadcast_select_fusion.1), channel_id=1, source_target_pairs={{0,1},{1,0},{2,3},{3,2},{4,5},{5,4},{6,7},{7,6},{8,9},{9,8},{10,11... | collective-permute-start | bytes 3145736 | tf_op jit(solution)/shard_map/ppermute | solution.py:27
  85.3 2.7 %collective-permute-start.19 = (bf16[2,64,1024]{2,1,0:T(8,128)(2,1)S(1)}, bf16[2,64,1024]{2,1,0:T(8,128)(2,1)S(1)}, u32[]{:S(2)}, u32[]{:S(2)}) collective-permute-start(bf16[2,64,1024]{2,1,0:T(8,128)(2,1)S(1)} %broadcast_select_fusion.4), channel_id=1, source_target_pairs={{0,1},{1,0},{2,3},{3,2},{4,5},{5,4},{6,7},{7,6},{8,9},{9,8},{10,11... | collective-permute-start | bytes 786440 | tf_op jit(solution)/shard_map/ppermute | solution.py:27
  87.3 14.4 %collective-permute-start.16 = (bf16[2,1024,128]{2,1,0:T(8,128)(2,1)S(1)}, bf16[2,1024,128]{2,1,0:T(8,128)(2,1)S(1)}, u32[]{:S(2)}, u32[]{:S(2)}) collective-permute-start(bf16[2,1024,128]{2,1,0:T(8,128)(2,1)S(1)} %shard_map.56.solved), channel_id=1, source_target_pairs={{0,4},{4,0},{8,12},{12,8},{16,20},{20,16},{24,28},{28,24},{1,5},{5... | collective-permute-start | bytes 1572872 | tf_op jit(solution)/shard_map/ppermute | solution.py:27
  102.8 1.5 %collective-permute-start.20 = (bf16[640,128]{1,0:T(8,128)(2,1)S(1)}, bf16[640,128]{1,0:T(8,128)(2,1)S(1)}, u32[]{:S(2)}, u32[]{:S(2)}) collective-permute-start(bf16[640,128]{1,0:T(8,128)(2,1)S(1)} %get-tuple-element.42), channel_id=1, source_target_pairs={{0,1},{1,0},{2,3},{3,2},{4,5},{5,4},{6,7},{7,6},{8,9},{9,8},{10,11... | collective-permute-start | bytes 491528 | tf_op jit(solution)/shard_map/ppermute | solution.py:27
  104.5 6.3 %collective-permute-start.21 = (bf16[640,128]{1,0:T(8,128)(2,1)S(1)}, bf16[640,128]{1,0:T(8,128)(2,1)S(1)}, u32[]{:S(2)}, u32[]{:S(2)}) collective-permute-start(bf16[640,128]{1,0:T(8,128)(2,1)S(1)} %broadcast_select_fusion.27), channel_id=1, source_target_pairs={{0,2},{1,3},{2,0},{3,1},{4,6},{5,7},{6,4},{7,5},{8,10},{9,11},{10,... | collective-permute-start | bytes 491528 | tf_op jit(solution)/shard_map/ppermute | solution.py:27
  (7 other events, 79.7 us)
where the time goes:
time: 120 us
  waiting for transfers between devices  54.2 us (45%)
  starting transfers between devices  32.2 us (27%)
  Pallas kernels  14.5 us (12%)
  between operations  9.41 us (8%)
  other arithmetic  5.33 us (4%)
  local copies, waits for them, and re-layouts  3.96 us (3%)
    ppermute x22, waiting for transfers between devices, swap(): return lax.ppermute(block, axis, [(s, s ^ bit) for s in senders])  54.2 us
    ppermute x22, starting transfers between devices, swap(): return lax.ppermute(block, axis, [(s, s ^ bit) for s in senders])  32.2 us
    pallas_call x1, Pallas kernels, on_device(): pl.pallas_call(functools.partial(final_kernel, last_col=last['last_col'])...  8.65 us
    select_n x14, other arithmetic, move(): self.mine = jnp.where(same, self.mine, got)  4.19 us
    unnamed x18, local copies, waits for them, and re-layouts  3.31 us
    pallas_call x1, Pallas kernels, on_device(): pl.pallas_call(functools.partial(prep_kernel, **last), out_shape=[tall] *...  2.95 us
  transfers between devices with their start and end apart: 22, of which 9 were waited for; matrix products, arithmetic and copies ran while one was open for 5% of the time, Pallas kernels for 2%

commit v1 on v0

--- a/solution.py
+++ b/solution.py
@@ -35,23 +35,22 @@
     return lax.optimization_barrier((value,) + others)[0]
 
 
+def all_bits(n):
+    return [1] + upper_bits(n)
+
+
 class Lane:
-    def __init__(self, keep, give, axis, n, root):
-        self.mine, self.axis, self.n, self.root = keep, axis, n, root
-        self.me = lax.axis_index(axis)
-        self.known = isinstance(root, int)
-        self.holders = {root} if self.known else None
-        self.bits = upper_bits(n)[::-1] if self.known else upper_bits(n)
-        self.move(1, give)
-
-    def move(self, bit, value):
-        got = swap(value, self.axis, self.n, bit, self.holders)
-        if self.known:
+    def __init__(self, keep, give, axis, n, same, root=None, got=None):
+        self.mine, self.axis, self.n, self.same = keep, axis, n, same
+        self.holders = None if root is None else {root}
+        self.bits = upper_bits(n) if root is None else upper_bits(n)[::-1]
+        self.move(1, give, got)
+
+    def move(self, bit, value, got=None):
+        got = swap(value, self.axis, self.n, bit, self.holders) if got is None else got
+        if self.holders:
             self.holders = self.holders | {h ^ bit for h in self.holders}
-        same = ((self.root ^ self.me) & bit) == 0
-        if self.known and bit == 1:
-            same = self.me != (self.root ^ 1)
-        self.mine = jnp.where(same, self.mine, got)
+        self.mine = jnp.where(self.same(bit, self.mine), self.mine, got)
 
     def step(self, k, *others):
         if others:
@@ -59,14 +58,23 @@
         self.move(self.bits[k], self.mine)
 
 
-def prep_kernel(order, ranks, u, v, *refs, last_row, last_col):
-    rs_uk, rs_ug, rd_uk, rd_ug, rs_vk, rs_vg, rd_vk, rd_vg, c_k, c_g, held, v_sem, u_sems = refs
+def flag_names(rows_n, cols_n):
+    names = ["row_first", "side_r", "side_c", "q1_low", "q2_low"]
+    names += [(kind, bit) for kind in ("rs", "rd") for bit in all_bits(rows_n)]
+    names += [(kind, bit) for kind in ("cs", "cd", "q1", "q2") for bit in all_bits(cols_n)]
+    return names
+
+
+def prep_kernel(order, ranks, u, v, *refs, rows_n, cols_n):
+    flags, rs_uk, rs_ug, rd_uk, rd_ug, rs_vk, rs_vg, rd_vk, rd_vg, c_k, c_g, held, v_sem, u_sems = refs
     rows, cols = u.shape[:2]
     rank, width = v.shape[2:]
-    row_dyn = lax.rem(jnp.where(order[0, 0] == last_row, order[1, 0], order[0, 0]), rows)
-    col_dyn = lax.rem(jnp.where(order[0, 1] == last_col, order[1, 1], order[0, 1]), cols)
-    row_side = lax.rem(lax.axis_index("row"), 2)
-    col_side = lax.rem(lax.axis_index("col"), 2)
+    me_row, me_col = lax.axis_index("row"), lax.axis_index("col")
+    row_first = order[0, 0] == rows_n * rows - 1
+    row_other = jnp.where(row_first, order[1, 0], order[0, 0])
+    col_other = jnp.where(order[0, 1] == cols_n * cols - 1, order[1, 1], order[0, 1])
+    row_dyn, col_dyn = lax.rem(row_other, rows), lax.rem(col_other, cols)
+    row_side, col_side = lax.rem(me_row, 2), lax.rem(me_col, 2)
 
     fetch = pltpu.make_async_copy(v, held, v_sem)
     fetch.start()
@@ -80,6 +88,21 @@
     copies = [pltpu.make_async_copy(a, b, u_sems.at[k]) for k, (a, b) in enumerate(copies)]
     for copy in copies:
         copy.start()
+
+    q1, q2 = order[0, 1], order[1, 1]
+    truth = {
+        "row_first": row_first, "side_r": row_side == 0, "side_c": col_side == 0,
+        "q1_low": lax.rem(q1, cols) == 0, "q2_low": lax.rem(q2, cols) == 0}
+    for bit in all_bits(rows_n):
+        truth["rs", bit] = (me_row & bit) == (rows_n - 1) & bit
+        truth["rd", bit] = (me_row & bit) == (lax.div(row_other, rows) & bit)
+    truth["rs", 1] = me_row != (rows_n - 1) ^ 1
+    for bit in all_bits(cols_n):
+        truth["cs", bit] = (me_col & bit) == (cols_n - 1) & bit
+        for kind, where in (("cd", col_other), ("q1", q1), ("q2", q2)):
+            truth[kind, bit] = (me_col & bit) == (lax.div(where, cols) & bit)
+    for k, name in enumerate(flag_names(rows_n, cols_n)):
+        flags[k:k + 1, :] = jnp.full((1, width), jnp.where(truth[name], 1, 0), jnp.int32)
     fetch.wait()
 
     def kept(i, j):
@@ -163,63 +186,83 @@
     def on_device(tile_u, tile_v, tile_ranks, inverses, panel_order):
         rows, cols, width, rank = tile_u.shape
         last = dict(last_row=rows_n * rows - 1, last_col=cols_n * cols - 1)
-        me_row, me_col = lax.axis_index("row"), lax.axis_index("col")
-        q1, q2 = panel_order[0, 1], panel_order[1, 1]
-        row_first = panel_order[0, 0] == last["last_row"]
-        col_first = q1 == last["last_col"]
-        row_root = jnp.where(row_first, panel_order[1, 0], panel_order[0, 0]) // rows
-        col_root = jnp.where(col_first, q2, q1) // cols
-        side_r, side_c = me_row % 2, me_col % 2
-
         tall = jax.ShapeDtypeStruct((width, rank), BF16)
         flat = jax.ShapeDtypeStruct((rank, width), BF16)
         quad = jax.ShapeDtypeStruct((2, 2, width, rank), BF16)
         anywhere = pl.BlockSpec(memory_space=pl.ANY)
+        names = flag_names(rows_n, cols_n)
         cut = pl.pallas_call(
-            functools.partial(prep_kernel, **last),
-            out_shape=[tall] * 4 + [flat] * 4 + [quad] * 2,
+            functools.partial(prep_kernel, rows_n=rows_n, cols_n=cols_n),
+            out_shape=[jax.ShapeDtypeStruct((len(names), width), jnp.int32)] + [tall] * 4 + [flat] * 4 + [quad] * 2,
             in_specs=[SCALARS, SCALARS, anywhere, anywhere],
-            out_specs=[WHOLE] * 10,
+            out_specs=[WHOLE] * 11,
             scratch_shapes=[pltpu.VMEM(tile_v.shape, BF16), pltpu.SemaphoreType.DMA(()), pltpu.SemaphoreType.DMA((8,))],
             compiler_params=params(),
         )(panel_order, tile_ranks, tile_u, tile_v)
-        rs_uk, rs_ug, rd_uk, rd_ug, rs_vk, rs_vg, rd_vk, rd_vg, c_k, c_g = cut
+        flags, rs_uk, rs_ug, rd_uk, rd_ug, rs_vk, rs_vg, rd_vk, rd_vg, c_k, c_g = cut
+
+        def flag(name, like):
+            k = names.index(name)
+            return flags[k:k + 1, :like.shape[-1]] != 0
+
+        def choose(name, one, two):
+            return jnp.where(flag(name, one), one, two)
+
+        def same(kind):
+            return lambda bit, like: flag((kind, bit), like)
 
         def lanes(fixed_keep, fixed_give, moving_keep, moving_give):
-            return (Lane(fixed_keep, fixed_give, "row", rows_n, rows_n - 1),
-                    Lane(moving_keep, moving_give, "row", rows_n, row_root))
-
-        def by_col(keep, give, roots):
-            lane = Lane(keep, give, "col", cols_n, roots)
+            return (Lane(moving_keep, moving_give, "row", rows_n, same("rd")),
+                    Lane(fixed_keep, fixed_give, "row", rows_n, same("rs"), rows_n - 1))
+
+        def joined(mine, axis, n, side):
+            other = swap(mine, axis, n, 1)
+            return choose(side, mine, other), choose(side, other, mine)
+
+        def both_q(bit, like):
+            return jnp.stack([flag(("q1", bit), like), flag(("q2", bit), like)])
+
+        def cross(one, two):
+            shape = one.shape[1:]
+            cand = jnp.stack([choose("q1_low", two[0], two[1]), choose("q2_low", one[0], one[1])])
+            cand = cand.reshape(2, 2, shape[0] // 2, shape[1])
+            lane = Lane(choose("side_c", cand[:, 0], cand[:, 1]), choose("side_c", cand[:, 1], cand[:, 0]), "col", cols_n, both_q)
             for k in range(len(lane.bits)):
                 lane.step(k)
-            other = swap(lane.mine, "col", cols_n, 1)
-            return jnp.where(side_c == 0, lane.mine, other), jnp.where(side_c == 0, other, lane.mine)
-
-        def cross(one, two):
-            shape = one.shape[1:]
-            cand = jnp.stack([jnp.where(q1 % cols == 0, two[0], two[1]), jnp.where(q2 % cols == 0, one[0], one[1])])
-            cand = cand.reshape(2, 2, shape[0] // 2, shape[1])
-            keep = jnp.where(side_c == 0, cand[:, 0], cand[:, 1])
-            give = jnp.where(side_c == 0, cand[:, 1], cand[:, 0])
-            both = jnp.concatenate(by_col(keep, give, jnp.stack([q1 // cols, q2 // cols])[:, None, None]), axis=1)
+            both = jnp.concatenate(joined(lane.mine, "col", cols_n, "side_c"), axis=1)
             return both[0], both[1]
 
         v_lanes = lanes(rs_vk, rs_vg, rd_vk, rd_vg)
+        c_got = swap(c_g, "col", cols_n, 1)
+        c_lanes = [Lane(c_k[k], None, "col", cols_n, same(kind), got=c_got[k]) for k, kind in enumerate(("cs", "cd"))]
         arrived = [lane.mine for lane in v_lanes]
         u_lanes = lanes(rs_uk, after(rs_ug, *arrived), rd_uk, after(rd_ug, *arrived))
-        first, second = by_col(c_k, after(c_g, arrived[1]), jnp.stack([cols_n - 1, col_root])[:, None, None, None])
+
+        mark = []
+        ties = [lane.mine for lane in c_lanes]
         for k in range(len(upper_bits(rows_n))):
             for lane in v_lanes:
-                lane.step(k)
+                lane.step(k, *ties)
+            if k == 0:
+                for lane, before in zip(c_lanes, ((), (c_lanes[0],))):
+                    for m in range(len(lane.bits)):
+                        lane.step(m, *(other.mine for other in before))
+                ties = [lane.mine for lane in u_lanes] + [c_lanes[0].mine]
             arrived = [lane.mine for lane in v_lanes]
+            if k > 0:
+                ties = [lane.mine for lane in u_lanes]
+                mark = ties
             for lane in u_lanes:
                 lane.step(k, *arrived)
-        fixed, moving = arrived
-        mine = jnp.stack([jnp.where(row_first, fixed, moving), jnp.where(row_first, moving, fixed)])
-        other = swap(mine, "row", rows_n, 1)
-        vp1, vp2 = (jnp.stack([jnp.where(side_r == 0, mine[s], other[s]), jnp.where(side_r == 0, other[s], mine[s])]) for s in range(2))
-        v21, v12 = cross(vp1, vp2)
+            if k == 0:
+                mark = [lane.mine for lane in u_lanes]
+        moving, fixed = (after(x, *mark, c_lanes[1].mine) for x in arrived)
+        mine = jnp.stack([choose("row_first", fixed, moving), choose("row_first", moving, fixed)])
+        vj0, vj1 = joined(mine, "row", rows_n, "side_r")
+        vp1, vp2 = (jnp.stack([vj0[s], vj1[s]]) for s in range(2))
+        first, second = joined(jnp.stack([lane.mine for lane in c_lanes]), "col", cols_n, "side_c")
+        waits = [lane.mine for lane in u_lanes]
+        v21, v12 = cross(after(vp1, *waits), after(vp2, *waits))
 
         solved = pl.pallas_call(
             functools.partial(solve_kernel, last_row=last["last_row"]),
@@ -227,7 +270,7 @@
             in_specs=[SCALARS] + [WHOLE] * 3,
             out_specs=WHOLE,
             compiler_params=params(),
-        )(panel_order, inverses, u_lanes[0].mine, u_lanes[1].mine)
+        )(panel_order, inverses, u_lanes[1].mine, u_lanes[0].mine)
         swapped = swap(solved, "row", rows_n, 1)
         cores, edge = pl.pallas_call(
             functools.partial(core_kernel, last_col=last["last_col"]),
@@ -236,10 +279,11 @@
             out_specs=[WHOLE] * 2,
             compiler_params=params(),
         )(panel_order, solved, swapped, first, second, v21, v12)
-        edge_root = jnp.where(jnp.arange(5 * rank)[:, None] < 2 * rank, q2 // cols, q1 // cols)
-        for bit in [1] + upper_bits(cols_n):
+        for bit in all_bits(cols_n):
             got = swap(edge, "col", cols_n, bit)
-            edge = jnp.where(((edge_root ^ me_col) & bit) == 0, edge, got)
+            early = jnp.arange(5 * rank)[:, None] < 2 * rank
+            stays = jnp.where(early, flag(("q2", bit), edge), flag(("q1", bit), edge))
+            edge = jnp.where(stays, edge, got)
 
         return pl.pallas_call(
             functools.partial(final_kernel, last_col=last["last_col"]),

time: 120 us -> 115 us (0.958)
  starting transfers between devices: 32.2 us -> 45 us
  between operations: 9.41 us -> 0.42 us
  waiting for transfers between devices: 54.2 us -> 50.5 us
  other arithmetic: 5.33 us -> 2.03 us
  local copies, waits for them, and re-layouts: 3.96 us -> 2.68 us
    ppermute x22 -> x23, starting transfers between devices: 32.2 us -> 45 us  [swap(): return lax.ppermute(block, axis, [(s, s ^ bit) for s in senders])]
    ppermute x22 -> x23, waiting for transfers between devices: 54.2 us -> 50.5 us  [swap(): return lax.ppermute(block, axis, [(s, s ^ bit) for s in senders])]
    select_n x22 -> x24, other arithmetic: 4.96 us -> 1.46 us  [the longest x17 0.72 us: move(): self.mine = jnp.where(self.same(bit, self.mine), self.mine, got)]
    unnamed x18 -> x14, local copies, waits for them, and re-layouts: 3.31 us -> 2.6 us
  transfers between devices with their start and end apart: 22 -> 23, of which waited for: 9 -> 12; matrix products, arithmetic and copies ran while one was open for 5% -> 2% of each run, Pallas kernels for 2% -> 2%
where the time goes in v1:
time: 115 us; the launch traced here: 114 us
  waiting for transfers between devices  50.5 us (44%)
  starting transfers between devices  45 us (39%)
  Pallas kernels  13.8 us (12%)
  local copies, waits for them, and re-layouts  2.68 us (2%)
  other arithmetic  2.03 us (2%)
    ppermute x23, waiting for transfers between devices, swap(): return lax.ppermute(block, axis, [(s, s ^ bit) for s in senders])  50.5 us
    ppermute x23, starting transfers between devices, swap(): return lax.ppermute(block, axis, [(s, s ^ bit) for s in senders])  45 us
    pallas_call x1, Pallas kernels, on_device(): pl.pallas_call(functools.partial(final_kernel, last_col=last['last_col'])...  8.7 us
    unnamed x14, local copies, waits for them, and re-layouts  2.6 us
  transfers between devices with their start and end apart: 23, of which 12 were waited for; matrix products, arithmetic and copies ran while one was open for 2% of the time, Pallas kernels for 2%

profile of v1, /device:TPU:0, one launch (start us, length us, event | category | flops | bytes accessed | tf_op | source)
XLA Modules:
  0.0 114.4 jit_solution(6755556422627879387)
XLA Ops:
  2.6 2.1 %shard_map.55 = (s32[19,1024]{1,0:T(8,128)S(1)}, bf16[1024,128]{1,0:T(8,128)(2,1)S(1)}, bf16[1024,128]{1,0:T(8,128)(2,1)S(1)}, bf16[1024,128]{1,0:T(8,128)(2,1)S...) custom-call(s32[2,2]{1,0:T(2,128)S(1)} %copy-done.4, ...), custom_call_target="tpu_custom_call" | custom-call | tf_op jit(solution)/shard_map/pallas_call | solution.py:194
  5.9 2.6 %collective-permute-start.6 = (bf16[128,1024]{1,0:T(8,128)(2,1)S(1)}, bf16[128,1024]{1,0:T(8,128)(2,1)S(1)}, u32[]{:S(2)}, u32[]{:S(2)}) collective-permute-start(bf16[128,1024]{1,0:T(8,128)(2,1)S(1)} %get-tuple-element.43), channel_id=1, source_target_pairs={{0,4},{4,0},{8,12},{12,8},{16,20},{20,16},{24,28},{28,24},{1,5},{5... | collective-permute-start | bytes 786440 | tf_op jit(solution)/shard_map/ppermute | solution.py:27
  8.8 6.7 %collective-permute-done.6 = bf16[128,1024]{1,0:T(8,128)(2,1)S(1)} collective-permute-done((bf16[128,1024]{1,0:T(8,128)(2,1)S(1)}, bf16[128,1024]{1,0:T(8,128)(2,1)S(1)}, u32[]{:S(2)}, u32[]{:S(2)}) %collective-permute-start.6) | collective-permute-done | bytes 262176 | tf_op jit(solution)/shard_map/ppermute | solution.py:27
  15.5 1.8 %collective-permute-start.7 = (bf16[1024,128]{1,0:T(8,128)(2,1)S(1)}, bf16[1024,128]{1,0:T(8,128)(2,1)S(1)}, u32[]{:S(2)}, u32[]{:S(2)}) collective-permute-start(bf16[1024,128]{1,0:T(8,128)(2,1)S(1)} %get-tuple-element.44), channel_id=1, source_target_pairs={{0,4},{4,0},{8,12},{12,8},{16,20},{20,16},{24,28},{28,24},{1,5},{5... | collective-permute-start | bytes 786440 | tf_op jit(solution)/shard_map/ppermute | solution.py:27
  18.8 4.9 %collective-permute-done.7 = bf16[1024,128]{1,0:T(8,128)(2,1)S(1)} collective-permute-done((bf16[1024,128]{1,0:T(8,128)(2,1)S(1)}, bf16[1024,128]{1,0:T(8,128)(2,1)S(1)}, u32[]{:S(2)}, u32[]{:S(2)}) %collective-permute-start.7) | collective-permute-done | bytes 262176 | tf_op jit(solution)/shard_map/ppermute | solution.py:27
  23.7 1.6 %collective-permute-start.1 = (bf16[2,1024,128]{2,1,0:T(8,128)(2,1)S(1)}, bf16[2,1024,128]{2,1,0:T(8,128)(2,1)S(1)}, u32[]{:S(2)}, u32[]{:S(2)}) collective-permute-start(bf16[2,1024,128]{2,1,0:T(8,128)(2,1)S(1)} %get-tuple-element.74), channel_id=1, source_target_pairs={{0,2},{1,3},{2,0},{3,1},{4,6},{5,7},{6,4},{7,5},{8,10},{9,11},{10,... | collective-permute-start | bytes 1572872 | tf_op jit(solution)/shard_map/ppermute | solution.py:27
  25.3 1.6 %collective-permute-start.10 = (bf16[128,1024]{1,0:T(8,128)(2,1)S(1)}, bf16[128,1024]{1,0:T(8,128)(2,1)S(1)}, u32[]{:S(2)}, u32[]{:S(2)}) collective-permute-start(bf16[128,1024]{1,0:T(8,128)(2,1)S(1)} %broadcast_select_fusion.17), channel_id=1, source_target_pairs={{0,8},{4,12},{8,0},{12,4},{16,24},{20,28},{24,16},{28,20},{1,9},{5... | collective-permute-start | bytes 786440 | tf_op jit(solution)/shard_map/ppermute | solution.py:27
  27.0 5.1 %collective-permute-done.10 = bf16[128,1024]{1,0:T(8,128)(2,1)S(1)} collective-permute-done((bf16[128,1024]{1,0:T(8,128)(2,1)S(1)}, bf16[128,1024]{1,0:T(8,128)(2,1)S(1)}, u32[]{:S(2)}, u32[]{:S(2)}) %collective-permute-start.10) | collective-permute-done | bytes 262176 | tf_op jit(solution)/shard_map/ppermute | solution.py:27
  32.1 3.7 %collective-permute-start.11 = (bf16[1024,128]{1,0:T(8,128)(2,1)S(1)}, bf16[1024,128]{1,0:T(8,128)(2,1)S(1)}, u32[]{:S(2)}, u32[]{:S(2)}) collective-permute-start(bf16[1024,128]{1,0:T(8,128)(2,1)S(1)} %broadcast_select_fusion.18), channel_id=1, source_target_pairs={{0,8},{4,12},{8,0},{12,4},{16,24},{20,28},{24,16},{28,20},{1,9},{5... | collective-permute-start | bytes 786440 | tf_op jit(solution)/shard_map/ppermute | solution.py:27
  36.7 1.3 %collective-permute-start.9 = (bf16[128,1024]{1,0:T(8,128)(2,1)S(1)}, bf16[128,1024]{1,0:T(8,128)(2,1)S(1)}, u32[]{:S(2)}, u32[]{:S(2)}) collective-permute-start(bf16[128,1024]{1,0:T(8,128)(2,1)S(1)} %broadcast_select_fusion.20), channel_id=1, source_target_pairs={{8,0},{12,4},{24,16},{28,20},{9,1},{13,5},{25,17},{29,21},{10,2},{... | collective-permute-start | bytes 786440 | tf_op jit(solution)/shard_map/ppermute | solution.py:27
  38.0 9.0 %collective-permute-start.13 = (bf16[128,1024]{1,0:T(8,128)(2,1)S(1)}, bf16[128,1024]{1,0:T(8,128)(2,1)S(1)}, u32[]{:S(2)}, u32[]{:S(2)}) collective-permute-start(bf16[128,1024]{1,0:T(8,128)(2,1)S(1)} %broadcast_select_fusion.14), channel_id=1, source_target_pairs={{0,16},{4,20},{8,24},{12,28},{16,0},{20,4},{24,8},{28,12},{1,17},{... | collective-permute-start | bytes 786440 | tf_op jit(solution)/shard_map/ppermute | solution.py:27
  47.6 5.0 %collective-permute-done.9 = bf16[128,1024]{1,0:T(8,128)(2,1)S(1)} collective-permute-done((bf16[128,1024]{1,0:T(8,128)(2,1)S(1)}, bf16[128,1024]{1,0:T(8,128)(2,1)S(1)}, u32[]{:S(2)}, u32[]{:S(2)}) %collective-permute-start.9) | collective-permute-done | bytes 262176 | tf_op jit(solution)/shard_map/ppermute | solution.py:27
  52.7 1.3 %collective-permute-start.15 = (bf16[1024,128]{1,0:T(8,128)(2,1)S(1)}, bf16[1024,128]{1,0:T(8,128)(2,1)S(1)}, u32[]{:S(2)}, u32[]{:S(2)}) collective-permute-start(bf16[1024,128]{1,0:T(8,128)(2,1)S(1)} %broadcast_select_fusion.13), channel_id=1, source_target_pairs={{8,0},{12,4},{24,16},{28,20},{9,1},{13,5},{25,17},{29,21},{10,2},{... | collective-permute-start | bytes 786440 | tf_op jit(solution)/shard_map/ppermute | solution.py:27
  54.0 9.1 %collective-permute-start.16 = (bf16[1024,128]{1,0:T(8,128)(2,1)S(1)}, bf16[1024,128]{1,0:T(8,128)(2,1)S(1)}, u32[]{:S(2)}, u32[]{:S(2)}) collective-permute-start(bf16[1024,128]{1,0:T(8,128)(2,1)S(1)} %broadcast_select_fusion.15), channel_id=1, source_target_pairs={{0,16},{4,20},{8,24},{12,28},{16,0},{20,4},{24,8},{28,12},{1,17},{... | collective-permute-start | bytes 786440 | tf_op jit(solution)/shard_map/ppermute | solution.py:27
  63.2 2.7 %collective-permute-start.14 = (bf16[2,128,1024]{2,1,0:T(8,128)(2,1)S(1)}, bf16[2,128,1024]{2,1,0:T(8,128)(2,1)S(1)}, u32[]{:S(2)}, u32[]{:S(2)}) collective-permute-start(bf16[2,128,1024]{2,1,0:T(8,128)(2,1)S(1)} %pad_maximum_fusion.1), channel_id=1, source_target_pairs={{0,4},{4,0},{8,12},{12,8},{16,20},{20,16},{24,28},{28,24},{1,5},{5... | collective-permute-start | bytes 1572872 | tf_op jit(solution)/shard_map/ppermute | solution.py:27
  66.0 8.0 %collective-permute-done.15 = bf16[1024,128]{1,0:T(8,128)(2,1)S(1)} collective-permute-done((bf16[1024,128]{1,0:T(8,128)(2,1)S(1)}, bf16[1024,128]{1,0:T(8,128)(2,1)S(1)}, u32[]{:S(2)}, u32[]{:S(2)}) %collective-permute-start.15) | collective-permute-done | bytes 262176 | tf_op jit(solution)/shard_map/ppermute | solution.py:27
  75.2 2.0 %collective-permute-done.18 = bf16[2,64,1024]{2,1,0:T(8,128)(2,1)S(1)} collective-permute-done((bf16[2,64,1024]{2,1,0:T(8,128)(2,1)S(1)}, bf16[2,64,1024]{2,1,0:T(8,128)(2,1)S(1)}, u32[]{:S(2)}, u32[]{:S(2)}) %collective-permute-start.18) | collective-permute-done | bytes 262176 | tf_op jit(solution)/shard_map/ppermute | solution.py:27
  77.6 1.8 %shard_map.56.solved = bf16[2,1024,128]{2,1,0:T(8,128)(2,1)S(1)} custom-call(s32[2,2]{1,0:T(2,128)S(1)} %copy-done.4, bf16[2,1024,1024]{2,1,0:T(8,128)(2,1)S(1)} %copy-done, bf16[1024,128]{1,0:T(8,128)(2,1)S(1)} %broadcast_select_fusion.11.fixed, bf16[1024,128]{1,0:T(8,128)(2,1)S(1)} %broadcast_select_fusion.10.moving), custom_call_target="tpu_custom_call" | custom-call | tf_op jit(solution)/shard_map/pallas_call | solution.py:267
  79.4 5.1 %collective-permute-start.17 = (bf16[2,1024,128]{2,1,0:T(8,128)(2,1)S(1)}, bf16[2,1024,128]{2,1,0:T(8,128)(2,1)S(1)}, u32[]{:S(2)}, u32[]{:S(2)}) collective-permute-start(bf16[2,1024,128]{2,1,0:T(8,128)(2,1)S(1)} %shard_map.56.solved), channel_id=1, source_target_pairs={{0,4},{4,0},{8,12},{12,8},{16,20},{20,16},{24,28},{28,24},{1,5},{5... | collective-permute-start | bytes 1572872 | tf_op jit(solution)/shard_map/ppermute | solution.py:27
  86.0 1.4 %collective-permute-done.20 = bf16[2,64,1024]{2,1,0:T(8,128)(2,1)S(1)} collective-permute-done((bf16[2,64,1024]{2,1,0:T(8,128)(2,1)S(1)}, bf16[2,64,1024]{2,1,0:T(8,128)(2,1)S(1)}, u32[]{:S(2)}, u32[]{:S(2)}) %collective-permute-start.20) | collective-permute-done | bytes 262176 | tf_op jit(solution)/shard_map/ppermute | solution.py:27
  87.4 9.0 %collective-permute-done.17.swapped = bf16[2,1024,128]{2,1,0:T(8,128)(2,1)S(1)} collective-permute-done((bf16[2,1024,128]{2,1,0:T(8,128)(2,1)S(1)}, bf16[2,1024,128]{2,1,0:T(8,128)(2,1)S(1)}, u32[]{:S(2)}, u32[]{:S(2)}) %collective-permute-start.17) | collective-permute-done | bytes 524320 | tf_op jit(solution)/shard_map/ppermute | solution.py:27
  97.7 1.4 %collective-permute-done.21 = bf16[640,128]{1,0:T(8,128)(2,1)S(1)} collective-permute-done((bf16[640,128]{1,0:T(8,128)(2,1)S(1)}, bf16[640,128]{1,0:T(8,128)(2,1)S(1)}, u32[]{:S(2)}, u32[]{:S(2)}) %collective-permute-start.21) | collective-permute-done | bytes 163872 | tf_op jit(solution)/shard_map/ppermute | solution.py:27
  99.8 5.7 %collective-permute-done.22 = bf16[640,128]{1,0:T(8,128)(2,1)S(1)} collective-permute-done((bf16[640,128]{1,0:T(8,128)(2,1)S(1)}, bf16[640,128]{1,0:T(8,128)(2,1)S(1)}, u32[]{:S(2)}, u32[]{:S(2)}) %collective-permute-start.22) | collective-permute-done | bytes 163872 | tf_op jit(solution)/shard_map/ppermute | solution.py:27
  105.7 8.7 %shard_map.58 = bf16[2,2,1024,1024]{3,2,1,0:T(8,128)(2,1)} custom-call(s32[2,2]{1,0:T(2,128)S(1)} %copy-done.4, s32[2,2]{1,0:T(2,128)S(1)} %copy-done.6, bf16[2,2,1024,128]{3,2,1,0:T(8,128)(2,1)S(1)} %copy-done.2, bf16[2,2,128,1024]{3,2,1,0:T(8,128)(2,1)S(1)} %copy-done.3, bf16[2,2,1024,128]{3,2,1,0:T(8,128)(2,1)S(1)} %get-tuple-element.73.first, ...), custom_call_target="tpu_custom_call" | custom-call | tf_op jit(solution)/shard_map/pallas_call | solution.py:288
  (77 shorter events, 12.6 us)
Async XLA Ops:
  4.7 13.2 %collective-permute-start = (bf16[2,2,1024,128]{3,2,1,0:T(8,128)(2,1)S(1)}, bf16[2,2,1024,128]{3,2,1,0:T(8,128)(2,1)S(1)}, u32[]{:S(2)}, u32[]{:S(2)}) collective-permute-start(bf16[2,2,1024,128]{3,2,1,0:T(8,128)(2,1)S(1)} %get-tuple-element.35), channel_id=1, source_target_pairs={{0,1},{1,0},{2,3},{3,2},{4,5},{5,4},{6,7},{7,6},{8,9},{9,8},{10,11... | collective-permute-start | bytes 3145736 | tf_op jit(solution)/shard_map/ppermute | solution.py:27
  5.3 3.5 %collective-permute-start.4 = (bf16[128,1024]{1,0:T(8,128)(2,1)S(1)}, bf16[128,1024]{1,0:T(8,128)(2,1)S(1)}, u32[]{:S(2)}, u32[]{:S(2)}) collective-permute-start(bf16[128,1024]{1,0:T(8,128)(2,1)S(1)} %get-tuple-element.38), channel_id=1, source_target_pairs={{28,24},{29,25},{30,26},{31,27}} | collective-permute-start | bytes 786440 | tf_op jit(solution)/shard_map/ppermute | solution.py:27
  5.9 9.5 %collective-permute-start.6 = (bf16[128,1024]{1,0:T(8,128)(2,1)S(1)}, bf16[128,1024]{1,0:T(8,128)(2,1)S(1)}, u32[]{:S(2)}, u32[]{:S(2)}) collective-permute-start(bf16[128,1024]{1,0:T(8,128)(2,1)S(1)} %get-tuple-element.43), channel_id=1, source_target_pairs={{0,4},{4,0},{8,12},{12,8},{16,20},{20,16},{24,28},{28,24},{1,5},{5... | collective-permute-start | bytes 786440 | tf_op jit(solution)/shard_map/ppermute | solution.py:27
  15.5 8.2 %collective-permute-start.7 = (bf16[1024,128]{1,0:T(8,128)(2,1)S(1)}, bf16[1024,128]{1,0:T(8,128)(2,1)S(1)}, u32[]{:S(2)}, u32[]{:S(2)}) collective-permute-start(bf16[1024,128]{1,0:T(8,128)(2,1)S(1)} %get-tuple-element.44), channel_id=1, source_target_pairs={{0,4},{4,0},{8,12},{12,8},{16,20},{20,16},{24,28},{28,24},{1,5},{5... | collective-permute-start | bytes 786440 | tf_op jit(solution)/shard_map/ppermute | solution.py:27
  17.3 9.6 %collective-permute-start.8 = (bf16[1024,128]{1,0:T(8,128)(2,1)S(1)}, bf16[1024,128]{1,0:T(8,128)(2,1)S(1)}, u32[]{:S(2)}, u32[]{:S(2)}) collective-permute-start(bf16[1024,128]{1,0:T(8,128)(2,1)S(1)} %get-tuple-element.47), channel_id=1, source_target_pairs={{28,24},{29,25},{30,26},{31,27}} | collective-permute-start | bytes 786440 | tf_op jit(solution)/shard_map/ppermute | solution.py:27
  18.1 8.8 %collective-permute-start.5 = (bf16[128,1024]{1,0:T(8,128)(2,1)S(1)}, bf16[128,1024]{1,0:T(8,128)(2,1)S(1)}, u32[]{:S(2)}, u32[]{:S(2)}) collective-permute-start(bf16[128,1024]{1,0:T(8,128)(2,1)S(1)} %broadcast_select_fusion.19), channel_id=1, source_target_pairs={{24,8},{28,12},{25,9},{29,13},{26,10},{30,14},{27,11},{31,15}} | collective-permute-start | bytes 786440 | tf_op jit(solution)/shard_map/ppermute | solution.py:27
  23.7 12.9 %collective-permute-start.1 = (bf16[2,1024,128]{2,1,0:T(8,128)(2,1)S(1)}, bf16[2,1024,128]{2,1,0:T(8,128)(2,1)S(1)}, u32[]{:S(2)}, u32[]{:S(2)}) collective-permute-start(bf16[2,1024,128]{2,1,0:T(8,128)(2,1)S(1)} %get-tuple-element.74), channel_id=1, source_target_pairs={{0,2},{1,3},{2,0},{3,1},{4,6},{5,7},{6,4},{7,5},{8,10},{9,11},{10,... | collective-permute-start | bytes 1572872 | tf_op jit(solution)/shard_map/ppermute | solution.py:27
  25.3 6.7 %collective-permute-start.10 = (bf16[128,1024]{1,0:T(8,128)(2,1)S(1)}, bf16[128,1024]{1,0:T(8,128)(2,1)S(1)}, u32[]{:S(2)}, u32[]{:S(2)}) collective-permute-start(bf16[128,1024]{1,0:T(8,128)(2,1)S(1)} %broadcast_select_fusion.17), channel_id=1, source_target_pairs={{0,8},{4,12},{8,0},{12,4},{16,24},{20,28},{24,16},{28,20},{1,9},{5... | collective-permute-start | bytes 786440 | tf_op jit(solution)/shard_map/ppermute | solution.py:27
  32.1 15.4 %collective-permute-start.11 = (bf16[1024,128]{1,0:T(8,128)(2,1)S(1)}, bf16[1024,128]{1,0:T(8,128)(2,1)S(1)}, u32[]{:S(2)}, u32[]{:S(2)}) collective-permute-start(bf16[1024,128]{1,0:T(8,128)(2,1)S(1)} %broadcast_select_fusion.18), channel_id=1, source_target_pairs={{0,8},{4,12},{8,0},{12,4},{16,24},{20,28},{24,16},{28,20},{1,9},{5... | collective-permute-start | bytes 786440 | tf_op jit(solution)/shard_map/ppermute | solution.py:27
  35.8 11.8 %collective-permute-start.12 = (bf16[1024,128]{1,0:T(8,128)(2,1)S(1)}, bf16[1024,128]{1,0:T(8,128)(2,1)S(1)}, u32[]{:S(2)}, u32[]{:S(2)}) collective-permute-start(bf16[1024,128]{1,0:T(8,128)(2,1)S(1)} %broadcast_select_fusion.16), channel_id=1, source_target_pairs={{24,8},{28,12},{25,9},{29,13},{26,10},{30,14},{27,11},{31,15}} | collective-permute-start | bytes 786440 | tf_op jit(solution)/shard_map/ppermute | solution.py:27
  36.7 15.9 %collective-permute-start.9 = (bf16[128,1024]{1,0:T(8,128)(2,1)S(1)}, bf16[128,1024]{1,0:T(8,128)(2,1)S(1)}, u32[]{:S(2)}, u32[]{:S(2)}) collective-permute-start(bf16[128,1024]{1,0:T(8,128)(2,1)S(1)} %broadcast_select_fusion.20), channel_id=1, source_target_pairs={{8,0},{12,4},{24,16},{28,20},{9,1},{13,5},{25,17},{29,21},{10,2},{... | collective-permute-start | bytes 786440 | tf_op jit(solution)/shard_map/ppermute | solution.py:27
  38.0 14.7 %collective-permute-start.13 = (bf16[128,1024]{1,0:T(8,128)(2,1)S(1)}, bf16[128,1024]{1,0:T(8,128)(2,1)S(1)}, u32[]{:S(2)}, u32[]{:S(2)}) collective-permute-start(bf16[128,1024]{1,0:T(8,128)(2,1)S(1)} %broadcast_select_fusion.14), channel_id=1, source_target_pairs={{0,16},{4,20},{8,24},{12,28},{16,0},{20,4},{24,8},{28,12},{1,17},{... | collective-permute-start | bytes 786440 | tf_op jit(solution)/shard_map/ppermute | solution.py:27
  47.0 16.1 %collective-permute-start.2 = (bf16[2,1024,128]{2,1,0:T(8,128)(2,1)S(1)}, bf16[2,1024,128]{2,1,0:T(8,128)(2,1)S(1)}, u32[]{:S(2)}, u32[]{:S(2)}) collective-permute-start(bf16[2,1024,128]{2,1,0:T(8,128)(2,1)S(1)} %get-tuple-element.36), channel_id=1, source_target_pairs={{0,2},{1,3},{2,0},{3,1},{4,6},{5,7},{6,4},{7,5},{8,10},{9,11},{10,... | collective-permute-start | bytes 1572872 | tf_op jit(solution)/shard_map/ppermute | solution.py:27
  52.7 21.2 %collective-permute-start.15 = (bf16[1024,128]{1,0:T(8,128)(2,1)S(1)}, bf16[1024,128]{1,0:T(8,128)(2,1)S(1)}, u32[]{:S(2)}, u32[]{:S(2)}) collective-permute-start(bf16[1024,128]{1,0:T(8,128)(2,1)S(1)} %broadcast_select_fusion.13), channel_id=1, source_target_pairs={{8,0},{12,4},{24,16},{28,20},{9,1},{13,5},{25,17},{29,21},{10,2},{... | collective-permute-start | bytes 786440 | tf_op jit(solution)/shard_map/ppermute | solution.py:27
  54.0 19.9 %collective-permute-start.16 = (bf16[1024,128]{1,0:T(8,128)(2,1)S(1)}, bf16[1024,128]{1,0:T(8,128)(2,1)S(1)}, u32[]{:S(2)}, u32[]{:S(2)}) collective-permute-start(bf16[1024,128]{1,0:T(8,128)(2,1)S(1)} %broadcast_select_fusion.15), channel_id=1, source_target_pairs={{0,16},{4,20},{8,24},{12,28},{16,0},{20,4},{24,8},{28,12},{1,17},{... | collective-permute-start | bytes 786440 | tf_op jit(solution)/shard_map/ppermute | solution.py:27
  63.2 11.0 %collective-permute-start.14 = (bf16[2,128,1024]{2,1,0:T(8,128)(2,1)S(1)}, bf16[2,128,1024]{2,1,0:T(8,128)(2,1)S(1)}, u32[]{:S(2)}, u32[]{:S(2)}) collective-permute-start(bf16[2,128,1024]{2,1,0:T(8,128)(2,1)S(1)} %pad_maximum_fusion.1), channel_id=1, source_target_pairs={{0,4},{4,0},{8,12},{12,8},{16,20},{20,16},{24,28},{28,24},{1,5},{5... | collective-permute-start | bytes 1572872 | tf_op jit(solution)/shard_map/ppermute | solution.py:27
  74.1 11.7 %collective-permute-start.3 = (bf16[2,2,1024,128]{3,2,1,0:T(8,128)(2,1)S(1)}, bf16[2,2,1024,128]{3,2,1,0:T(8,128)(2,1)S(1)}, u32[]{:S(2)}, u32[]{:S(2)}) collective-permute-start(bf16[2,2,1024,128]{3,2,1,0:T(8,128)(2,1)S(1)} %pad_maximum_fusion), channel_id=1, source_target_pairs={{0,1},{1,0},{2,3},{3,2},{4,5},{5,4},{6,7},{7,6},{8,9},{9,8},{10,11... | collective-permute-start | bytes 3145736 | tf_op jit(solution)/shard_map/ppermute | solution.py:27
  74.7 2.5 %collective-permute-start.18 = (bf16[2,64,1024]{2,1,0:T(8,128)(2,1)S(1)}, bf16[2,64,1024]{2,1,0:T(8,128)(2,1)S(1)}, u32[]{:S(2)}, u32[]{:S(2)}) collective-permute-start(bf16[2,64,1024]{2,1,0:T(8,128)(2,1)S(1)} %broadcast_select_fusion.9), channel_id=1, source_target_pairs={{0,1},{1,0},{2,3},{3,2},{4,5},{5,4},{6,7},{7,6},{8,9},{9,8},{10,11... | collective-permute-start | bytes 786440 | tf_op jit(solution)/shard_map/ppermute | solution.py:27
  77.3 8.4 %collective-permute-start.19 = (bf16[2,64,1024]{2,1,0:T(8,128)(2,1)S(1)}, bf16[2,64,1024]{2,1,0:T(8,128)(2,1)S(1)}, u32[]{:S(2)}, u32[]{:S(2)}) collective-permute-start(bf16[2,64,1024]{2,1,0:T(8,128)(2,1)S(1)} %select_select_fusion.2), channel_id=1, source_target_pairs={{0,2},{1,3},{2,0},{3,1},{4,6},{5,7},{6,4},{7,5},{8,10},{9,11},{10,... | collective-permute-start | bytes 786440 | tf_op jit(solution)/shard_map/ppermute | solution.py:27
  77.6 28.1 %copy-start.2 = (bf16[2,2,1024,128]{3,2,1,0:T(8,128)(2,1)S(1)}, bf16[2,2,1024,128]{3,2,1,0:T(8,128)(2,1)}, u32[]{:S(2)}) copy-start(bf16[2,2,1024,128]{3,2,1,0:T(8,128)(2,1)} %u.3) | copy-start | bytes 3145732
  79.4 17.0 %collective-permute-start.17 = (bf16[2,1024,128]{2,1,0:T(8,128)(2,1)S(1)}, bf16[2,1024,128]{2,1,0:T(8,128)(2,1)S(1)}, u32[]{:S(2)}, u32[]{:S(2)}) collective-permute-start(bf16[2,1024,128]{2,1,0:T(8,128)(2,1)S(1)} %shard_map.56.solved), channel_id=1, source_target_pairs={{0,4},{4,0},{8,12},{12,8},{16,20},{20,16},{24,28},{28,24},{1,5},{5... | collective-permute-start | bytes 1572872 | tf_op jit(solution)/shard_map/ppermute | solution.py:27
  85.7 1.6 %collective-permute-start.20 = (bf16[2,64,1024]{2,1,0:T(8,128)(2,1)S(1)}, bf16[2,64,1024]{2,1,0:T(8,128)(2,1)S(1)}, u32[]{:S(2)}, u32[]{:S(2)}) collective-permute-start(bf16[2,64,1024]{2,1,0:T(8,128)(2,1)S(1)} %broadcast_select_fusion.6), channel_id=1, source_target_pairs={{0,1},{1,0},{2,3},{3,2},{4,5},{5,4},{6,7},{7,6},{8,9},{9,8},{10,11... | collective-permute-start | bytes 786440 | tf_op jit(solution)/shard_map/ppermute | solution.py:27
  97.6 1.5 %collective-permute-start.21 = (bf16[640,128]{1,0:T(8,128)(2,1)S(1)}, bf16[640,128]{1,0:T(8,128)(2,1)S(1)}, u32[]{:S(2)}, u32[]{:S(2)}) collective-permute-start(bf16[640,128]{1,0:T(8,128)(2,1)S(1)} %get-tuple-element.60), channel_id=1, source_target_pairs={{0,1},{1,0},{2,3},{3,2},{4,5},{5,4},{6,7},{7,6},{8,9},{9,8},{10,11... | collective-permute-start | bytes 491528 | tf_op jit(solution)/shard_map/ppermute | solution.py:27
  99.2 6.3 %collective-permute-start.22 = (bf16[640,128]{1,0:T(8,128)(2,1)S(1)}, bf16[640,128]{1,0:T(8,128)(2,1)S(1)}, u32[]{:S(2)}, u32[]{:S(2)}) collective-permute-start(bf16[640,128]{1,0:T(8,128)(2,1)S(1)} %select_select_fusion), channel_id=1, source_target_pairs={{0,2},{1,3},{2,0},{3,1},{4,6},{5,7},{6,4},{7,5},{8,10},{9,11},{10,... | collective-permute-start | bytes 491528 | tf_op jit(solution)/shard_map/ppermute | solution.py:27
  (6 other events, 73.3 us)

commit v2 on v1

--- a/solution.py
+++ b/solution.py
@@ -59,14 +59,15 @@
 
 
 def flag_names(rows_n, cols_n):
-    names = ["row_first", "side_r", "side_c", "q1_low", "q2_low"]
+    names = ["row_first", "side_r", "side_c", "q1_side", "q2_side"]
+    names += [(kind, bit) for kind in ("p1", "p2") for bit in upper_bits(rows_n)]
     names += [(kind, bit) for kind in ("rs", "rd") for bit in all_bits(rows_n)]
     names += [(kind, bit) for kind in ("cs", "cd", "q1", "q2") for bit in all_bits(cols_n)]
     return names
 
 
 def prep_kernel(order, ranks, u, v, *refs, rows_n, cols_n):
-    flags, rs_uk, rs_ug, rd_uk, rd_ug, rs_vk, rs_vg, rd_vk, rd_vg, c_k, c_g, held, v_sem, u_sems = refs
+    flags, rs_uk, rs_ug, rd_uk, rd_ug, rs_vk, rs_vg, rd_vk, rd_vg, cu_k, cu_g, cv_k, cv_g, held, v_sem, u_sems = refs
     rows, cols = u.shape[:2]
     rank, width = v.shape[2:]
     me_row, me_col = lax.axis_index("row"), lax.axis_index("col")
@@ -84,7 +85,7 @@
             copies.append((u.at[i, j], outs[slot]))
     for which, j in enumerate((cols - 1, col_dyn)):
         for slot, i in enumerate((col_side, 1 - col_side)):
-            copies.append((u.at[i, j], (c_k, c_g)[slot].at[which, 0]))
+            copies.append((u.at[i, j], (cu_k, cu_g)[slot].at[which]))
     copies = [pltpu.make_async_copy(a, b, u_sems.at[k]) for k, (a, b) in enumerate(copies)]
     for copy in copies:
         copy.start()
@@ -92,9 +93,11 @@
     q1, q2 = order[0, 1], order[1, 1]
     truth = {
         "row_first": row_first, "side_r": row_side == 0, "side_c": col_side == 0,
-        "q1_low": lax.rem(q1, cols) == 0, "q2_low": lax.rem(q2, cols) == 0}
+        "q1_side": lax.rem(q1, cols) == row_side, "q2_side": lax.rem(q2, cols) == row_side}
     for bit in all_bits(rows_n):
         truth["rs", bit] = (me_row & bit) == (rows_n - 1) & bit
+        truth["p1", bit] = (me_row & bit) == (lax.div(order[0, 0], rows) & bit)
+        truth["p2", bit] = (me_row & bit) == (lax.div(order[1, 0], rows) & bit)
         truth["rd", bit] = (me_row & bit) == (lax.div(row_other, rows) & bit)
     truth["rs", 1] = me_row != (rows_n - 1) ^ 1
     for bit in all_bits(cols_n):
@@ -116,7 +119,7 @@
         for slot, i in enumerate((col_side, 1 - col_side)):
             value = kept(i, j)
             for k in range(width // rank):
-                (c_k, c_g)[slot][which, 1, k * rank:(k + 1) * rank, :] = value[:, k * rank:(k + 1) * rank]
+                (cv_k, cv_g)[slot][which, k * rank:(k + 1) * rank, :] = value[:, k * rank:(k + 1) * rank]
     for copy in copies:
         copy.wait()
 
@@ -127,28 +130,23 @@
     out[1] = dot(inverses[1], jnp.where(fixed_first, moving[...], fixed[...])).astype(BF16)
 
 
-def core_kernel(order, solved, swapped, first, second, v21, v12, out, edge, *, last_col):
-    rank, width = v21.shape
-    count = width // rank
-    swap_first = lax.rem(lax.axis_index("row"), 2) == 1
+def core_kernel(order, solved, first, second, out, foot, *, last_col):
+    rank = out.shape[2]
+    count = solved.shape[1] // rank
+    me = lax.axis_index("row")
     step_of = jnp.where(order[0, 1] == last_col, 0, 1)
-    for s, more in enumerate((v21, v12)):
+    for s in range(2):
         which = step_of if s == 0 else 1 - step_of
-        lines = [jnp.concatenate([tiles[which, 1, k * rank:(k + 1) * rank, :] for k in range(count)], axis=1) for tiles in (first, second)]
-        tall = jnp.concatenate(lines + [more[...]], axis=0)
-        mine, other = solved[s], swapped[s]
-        wide = jnp.concatenate([jnp.where(swap_first, other, mine), jnp.where(swap_first, mine, other)], axis=1)
-        got = dot(tall, wide).astype(BF16)
-        out[s] = got
-        late = lax.rem(order[1 - s, 1], 2) == 1
-        pivot = jnp.where(late, got[:, rank:], got[:, :rank])
-        if s == 0:
-            edge[:2 * rank] = pivot[:2 * rank]
-        else:
-            edge[2 * rank:] = pivot
-
-
-def final_kernel(order, ranks, u, v, first, second, vp1, vp2, cores, edge, out, *, last_col):
+        lines = [
+            jnp.concatenate([tiles[which + far, k * rank:(k + 1) * rank, :] for k in range(count)], axis=1)
+            for far in (0, 2) for tiles in (first, second)]
+        out[s] = dot(jnp.concatenate(lines, axis=0), solved[s]).astype(BF16)
+        row = order[1 - s, 0]
+        far = lax.rem(lax.div(row, 2) + me, 2)
+        foot[s] = out[s, pl.ds(pl.multiple_of((2 * far + lax.rem(row, 2)) * rank, rank), rank), :]
+
+
+def final_kernel(order, ranks, u, v, first, second, vp1, vp2, cores, swapped, edge, out, *, last_col):
     i, j = pl.program_id(0), pl.program_id(1)
     rank, width = v.shape[2:]
     row = lax.axis_index("row") * pl.num_programs(0) + i
@@ -161,8 +159,10 @@
     top = pl.ds(pl.multiple_of(i * rank, rank), rank)
     below = pl.ds(pl.multiple_of(2 * rank + i * rank, rank), rank)
 
+    here = j == lax.rem(lax.axis_index("row"), 2)
+
     def left(s, lines):
-        return jnp.where(j == 0, cores[s, lines, :rank], cores[s, lines, rank:])
+        return jnp.where(here, cores[s, lines, :], swapped[s, lines, :])
 
     c1_ij, c1_iq2, c1_p2j = left(0, top), edge[top], left(0, pl.ds(foot, rank))
     high_a, high_b = left(1, top), edge[below]
@@ -178,7 +178,7 @@
     own = jnp.where(line < ranks[i, j], v[0, 0], jnp.zeros((), BF16))
     right = jnp.concatenate([own, change], axis=0)
     w1 = jnp.where(order[0, 1] == last_col, 0, 1)
-    uq1, uq2 = (jnp.where(i == 0, first[w, 0], second[w, 0]) for w in (w1, 1 - w1))
+    uq1, uq2 = (jnp.where(i == 0, first[w], second[w]) for w in (w1, 1 - w1))
     out[0, 0] = dot(jnp.concatenate([u[0, 0], uq1, uq2], axis=1), right).astype(BF16)
 
 
@@ -188,18 +188,18 @@
         last = dict(last_row=rows_n * rows - 1, last_col=cols_n * cols - 1)
         tall = jax.ShapeDtypeStruct((width, rank), BF16)
         flat = jax.ShapeDtypeStruct((rank, width), BF16)
-        quad = jax.ShapeDtypeStruct((2, 2, width, rank), BF16)
+        pair = jax.ShapeDtypeStruct((2, width, rank), BF16)
         anywhere = pl.BlockSpec(memory_space=pl.ANY)
         names = flag_names(rows_n, cols_n)
         cut = pl.pallas_call(
             functools.partial(prep_kernel, rows_n=rows_n, cols_n=cols_n),
-            out_shape=[jax.ShapeDtypeStruct((len(names), width), jnp.int32)] + [tall] * 4 + [flat] * 4 + [quad] * 2,
+            out_shape=[jax.ShapeDtypeStruct((len(names), width), jnp.int32)] + [tall] * 4 + [flat] * 4 + [pair] * 4,
             in_specs=[SCALARS, SCALARS, anywhere, anywhere],
-            out_specs=[WHOLE] * 11,
+            out_specs=[WHOLE] * 13,
             scratch_shapes=[pltpu.VMEM(tile_v.shape, BF16), pltpu.SemaphoreType.DMA(()), pltpu.SemaphoreType.DMA((8,))],
             compiler_params=params(),
         )(panel_order, tile_ranks, tile_u, tile_v)
-        flags, rs_uk, rs_ug, rd_uk, rd_ug, rs_vk, rs_vg, rd_vk, rd_vg, c_k, c_g = cut
+        flags, rs_uk, rs_ug, rd_uk, rd_ug, rs_vk, rs_vg, rd_vk, rd_vg, cu_k, cu_g, cv_k, cv_g = cut
 
         def flag(name, like):
             k = names.index(name)
@@ -219,71 +219,72 @@
             other = swap(mine, axis, n, 1)
             return choose(side, mine, other), choose(side, other, mine)
 
-        def both_q(bit, like):
-            return jnp.stack([flag(("q1", bit), like), flag(("q2", bit), like)])
-
-        def cross(one, two):
-            shape = one.shape[1:]
-            cand = jnp.stack([choose("q1_low", two[0], two[1]), choose("q2_low", one[0], one[1])])
-            cand = cand.reshape(2, 2, shape[0] // 2, shape[1])
-            lane = Lane(choose("side_c", cand[:, 0], cand[:, 1]), choose("side_c", cand[:, 1], cand[:, 0]), "col", cols_n, both_q)
-            for k in range(len(lane.bits)):
-                lane.step(k)
-            both = jnp.concatenate(joined(lane.mine, "col", cols_n, "side_c"), axis=1)
-            return both[0], both[1]
-
-        v_lanes = lanes(rs_vk, rs_vg, rd_vk, rd_vg)
-        c_got = swap(c_g, "col", cols_n, 1)
-        c_lanes = [Lane(c_k[k], None, "col", cols_n, same(kind), got=c_got[k]) for k, kind in enumerate(("cs", "cd"))]
-        arrived = [lane.mine for lane in v_lanes]
-        u_lanes = lanes(rs_uk, after(rs_ug, *arrived), rd_uk, after(rd_ug, *arrived))
-
-        mark = []
-        ties = [lane.mine for lane in c_lanes]
+        def same_both(bit, like):
+            return jnp.stack([flag(("cs", bit), like), flag(("cd", bit), like)])
+
+        def mines(pair):
+            return [lane.mine for lane in pair]
+
+        u_lanes = lanes(rs_uk, rs_ug, rd_uk, rd_ug)
+        cv = Lane(cv_k, cv_g, "col", cols_n, same_both)
+        ties = mines(u_lanes)
+        v_lanes = lanes(rs_vk, after(rs_vg, *ties), rd_vk, after(rd_vg, *ties))
+        ties = [cv.mine]
         for k in range(len(upper_bits(rows_n))):
-            for lane in v_lanes:
+            for lane in u_lanes:
                 lane.step(k, *ties)
+            ties = mines(v_lanes)
+            follow = mines(u_lanes)
             if k == 0:
-                for lane, before in zip(c_lanes, ((), (c_lanes[0],))):
-                    for m in range(len(lane.bits)):
-                        lane.step(m, *(other.mine for other in before))
-                ties = [lane.mine for lane in u_lanes] + [c_lanes[0].mine]
-            arrived = [lane.mine for lane in v_lanes]
-            if k > 0:
-                ties = [lane.mine for lane in u_lanes]
-                mark = ties
-            for lane in u_lanes:
-                lane.step(k, *arrived)
-            if k == 0:
-                mark = [lane.mine for lane in u_lanes]
-        moving, fixed = (after(x, *mark, c_lanes[1].mine) for x in arrived)
-        mine = jnp.stack([choose("row_first", fixed, moving), choose("row_first", moving, fixed)])
-        vj0, vj1 = joined(mine, "row", rows_n, "side_r")
-        vp1, vp2 = (jnp.stack([vj0[s], vj1[s]]) for s in range(2))
-        first, second = joined(jnp.stack([lane.mine for lane in c_lanes]), "col", cols_n, "side_c")
-        waits = [lane.mine for lane in u_lanes]
-        v21, v12 = cross(after(vp1, *waits), after(vp2, *waits))
-
+                for m in range(len(cv.bits)):
+                    cv.step(m)
+                ties.append(cv.mine)
+                near = swap(cv.mine, "row", rows_n, 1)
+                cu = Lane(cu_k, after(cu_g, cv.mine), "col", cols_n, same_both)
+            else:
+                follow.append(near)
+            if k < len(upper_bits(rows_n)) - 1:
+                for lane in v_lanes:
+                    lane.step(k, *follow)
+        v_lanes[1].step(k, *follow)
+        for m in range(len(cu.bits)):
+            cu.step(m)
+        cv_first, cv_second = joined(jnp.concatenate([cv.mine, near]), "col", cols_n, "side_c")
+        cu_first, cu_second = joined(cu.mine, "col", cols_n, "side_c")
+
+        moving, fixed = mines(u_lanes)
         solved = pl.pallas_call(
             functools.partial(solve_kernel, last_row=last["last_row"]),
             out_shape=jax.ShapeDtypeStruct((2, width, rank), BF16),
             in_specs=[SCALARS] + [WHOLE] * 3,
             out_specs=WHOLE,
             compiler_params=params(),
-        )(panel_order, inverses, u_lanes[1].mine, u_lanes[0].mine)
-        swapped = swap(solved, "row", rows_n, 1)
-        cores, edge = pl.pallas_call(
+        )(panel_order, inverses, fixed, moving)
+        cores, foot = pl.pallas_call(
             functools.partial(core_kernel, last_col=last["last_col"]),
-            out_shape=[jax.ShapeDtypeStruct((2, 3 * rank, 2 * rank), BF16), jax.ShapeDtypeStruct((5 * rank, rank), BF16)],
-            in_specs=[SCALARS] + [WHOLE] * 6,
+            out_shape=[jax.ShapeDtypeStruct((2, 4 * rank, rank), BF16), jax.ShapeDtypeStruct((2, rank, rank), BF16)],
+            in_specs=[SCALARS] + [WHOLE] * 3,
             out_specs=[WHOLE] * 2,
             compiler_params=params(),
-        )(panel_order, solved, swapped, first, second, v21, v12)
+        )(panel_order, solved, cv_first, cv_second)
+        for m, bit in enumerate(upper_bits(rows_n)):
+            got = swap(foot, "row", rows_n, bit)
+            foot = jnp.where(jnp.stack([flag(("p2", bit), foot), flag(("p1", bit), foot)]), foot, got)
+            if m == 0:
+                v_lanes[0].step(k, foot, *follow)
+        swapped = swap(jnp.concatenate([cores[:, 2 * rank:], foot], axis=1), "row", rows_n, 1)
+        cores = jnp.concatenate([cores[:, :2 * rank], foot], axis=1)
+        edge = jnp.concatenate([choose("q2_side", cores[0, :2 * rank], swapped[0, :2 * rank]), choose("q1_side", cores[1], swapped[1])])
         for bit in all_bits(cols_n):
             got = swap(edge, "col", cols_n, bit)
             early = jnp.arange(5 * rank)[:, None] < 2 * rank
             stays = jnp.where(early, flag(("q2", bit), edge), flag(("q1", bit), edge))
             edge = jnp.where(stays, edge, got)
+
+        moving, fixed = mines(v_lanes)
+        mine = jnp.stack([choose("row_first", fixed, moving), choose("row_first", moving, fixed)])
+        vj0, vj1 = joined(mine, "row", rows_n, "side_r")
+        vp1, vp2 = (jnp.stack([vj0[s], vj1[s]]) for s in range(2))
 
         return pl.pallas_call(
             functools.partial(final_kernel, last_col=last["last_col"]),
@@ -296,10 +297,10 @@
                 WHOLE, WHOLE,
                 pl.BlockSpec((1, rank, width), lambda i, j: (j, 0, 0)),
                 pl.BlockSpec((1, rank, width), lambda i, j: (j, 0, 0)),
-                WHOLE, WHOLE],
+                WHOLE, WHOLE, WHOLE],
             out_specs=pl.BlockSpec((1, 1, width, width), lambda i, j: (i, j, 0, 0)),
             compiler_params=params(),
-        )(panel_order, tile_ranks, tile_u, tile_v, first, second, vp1, vp2, cores, edge)
+        )(panel_order, tile_ranks, tile_u, tile_v, cu_first, cu_second, vp1, vp2, cores, swapped, edge)
 
     return on_device
 

time: 115 us -> 117 us (1.017)
  waiting for transfers between devices: 50.5 us -> 55.8 us
  starting transfers between devices: 45 us -> 42.1 us
    ppermute x23 -> x25, waiting for transfers between devices: 50.5 us -> 55.8 us  [swap(): return lax.ppermute(block, axis, [(s, s ^ bit) for s in senders])]
    ppermute x23 -> x25, starting transfers between devices: 45 us -> 42.1 us  [swap(): return lax.ppermute(block, axis, [(s, s ^ bit) for s in senders])]
    unnamed x14 -> x18, local copies, waits for them, and re-layouts: 2.6 us -> 2.63 us
  transfers between devices with their start and end apart: 23 -> 25, of which waited for: 12 -> 11; matrix products, arithmetic and copies ran while one was open for 2% -> 1% of each run, Pallas kernels for 2% -> 3%
where the time goes in v2:
time: 117 us
  waiting for transfers between devices  55.8 us (48%)
  starting transfers between devices  42.1 us (36%)
  Pallas kernels  14.1 us (12%)
  local copies, waits for them, and re-layouts  2.72 us (2%)
  other arithmetic  1.8 us (2%)
    ppermute x25, waiting for transfers between devices, swap(): return lax.ppermute(block, axis, [(s, s ^ bit) for s in senders])  55.8 us
    ppermute x25, starting transfers between devices, swap(): return lax.ppermute(block, axis, [(s, s ^ bit) for s in senders])  42.1 us
    pallas_call x1, Pallas kernels, on_device(): pl.pallas_call(functools.partial(final_kernel, last_col=last['last_col'])...  8.56 us
    unnamed x18, local copies, waits for them, and re-layouts  2.63 us
    pallas_call x1, Pallas kernels, on_device(): pl.pallas_call(functools.partial(prep_kernel, rows_n=rows_n, cols_n=cols_...  2.42 us
  transfers between devices with their start and end apart: 25, of which 11 were waited for; matrix products, arithmetic and copies ran while one was open for 1% of the time, Pallas kernels for 3%

profile of v2, /device:TPU:0, one launch (start us, length us, event | category | flops | bytes accessed | tf_op | source)
XLA Modules:
  0.0 116.9 jit_solution(15289693125014467604)
XLA Ops:
  2.6 2.4 %shard_map.55 = (s32[23,1024]{1,0:T(8,128)S(1)}, bf16[1024,128]{1,0:T(8,128)(2,1)S(1)}, bf16[1024,128]{1,0:T(8,128)(2,1)S(1)}, bf16[1024,128]{1,0:T(8,128)(2,1)S...) custom-call(s32[2,2]{1,0:T(2,128)S(1)} %copy-done.4, ...), custom_call_target="tpu_custom_call" | custom-call | tf_op jit(solution)/shard_map/pallas_call | solution.py:194
  5.0 3.0 %collective-permute-start.5 = (bf16[1024,128]{1,0:T(8,128)(2,1)S(1)}, bf16[1024,128]{1,0:T(8,128)(2,1)S(1)}, u32[]{:S(2)}, u32[]{:S(2)}) collective-permute-start(bf16[1024,128]{1,0:T(8,128)(2,1)S(1)} %get-tuple-element.40), channel_id=1, source_target_pairs={{0,4},{4,0},{8,12},{12,8},{16,20},{20,16},{24,28},{28,24},{1,5},{5... | collective-permute-start | bytes 786440 | tf_op jit(solution)/shard_map/ppermute | solution.py:27
  8.9 5.5 %collective-permute-done.5 = bf16[1024,128]{1,0:T(8,128)(2,1)S(1)} collective-permute-done((bf16[1024,128]{1,0:T(8,128)(2,1)S(1)}, bf16[1024,128]{1,0:T(8,128)(2,1)S(1)}, u32[]{:S(2)}, u32[]{:S(2)}) %collective-permute-start.5) | collective-permute-done | bytes 262176 | tf_op jit(solution)/shard_map/ppermute | solution.py:27
  15.2 1.8 %collective-permute-start.1 = (bf16[2,1024,128]{2,1,0:T(8,128)(2,1)S(1)}, bf16[2,1024,128]{2,1,0:T(8,128)(2,1)S(1)}, u32[]{:S(2)}, u32[]{:S(2)}) collective-permute-start(bf16[2,1024,128]{2,1,0:T(8,128)(2,1)S(1)} %broadcast_select_fusion.5), channel_id=1, source_target_pairs={{0,2},{1,3},{2,0},{3,1},{4,6},{5,7},{6,4},{7,5},{8,10},{9,11},{10,... | collective-permute-start | bytes 1572872 | tf_op jit(solution)/shard_map/ppermute | solution.py:27
  17.2 1.6 %collective-permute-start.11 = (bf16[128,1024]{1,0:T(8,128)(2,1)S(1)}, bf16[128,1024]{1,0:T(8,128)(2,1)S(1)}, u32[]{:S(2)}, u32[]{:S(2)}) collective-permute-start(bf16[128,1024]{1,0:T(8,128)(2,1)S(1)} %get-tuple-element.49), channel_id=1, source_target_pairs={{0,4},{4,0},{8,12},{12,8},{16,20},{20,16},{24,28},{28,24},{1,5},{5... | collective-permute-start | bytes 786440 | tf_op jit(solution)/shard_map/ppermute | solution.py:27
  18.7 1.6 %collective-permute-start.8 = (bf16[1024,128]{1,0:T(8,128)(2,1)S(1)}, bf16[1024,128]{1,0:T(8,128)(2,1)S(1)}, u32[]{:S(2)}, u32[]{:S(2)}) collective-permute-start(bf16[1024,128]{1,0:T(8,128)(2,1)S(1)} %broadcast_select_fusion.18), channel_id=1, source_target_pairs={{0,8},{4,12},{8,0},{12,4},{16,24},{20,28},{24,16},{28,20},{1,9},{5... | collective-permute-start | bytes 786440 | tf_op jit(solution)/shard_map/ppermute | solution.py:27
  21.0 7.3 %collective-permute-done.1 = bf16[2,1024,128]{2,1,0:T(8,128)(2,1)S(1)} collective-permute-done((bf16[2,1024,128]{2,1,0:T(8,128)(2,1)S(1)}, bf16[2,1024,128]{2,1,0:T(8,128)(2,1)S(1)}, u32[]{:S(2)}, u32[]{:S(2)}) %collective-permute-start.1) | collective-permute-done | bytes 524320 | tf_op jit(solution)/shard_map/ppermute | solution.py:27
  28.4 1.5 %collective-permute-start.14 = (bf16[2,1024,128]{2,1,0:T(8,128)(2,1)S(1)}, bf16[2,1024,128]{2,1,0:T(8,128)(2,1)S(1)}, u32[]{:S(2)}, u32[]{:S(2)}) collective-permute-start(bf16[2,1024,128]{2,1,0:T(8,128)(2,1)S(1)} %broadcast_select_fusion.7), channel_id=1, source_target_pairs={{0,4},{4,0},{8,12},{12,8},{16,20},{20,16},{24,28},{28,24},{1,5},{5... | collective-permute-start | bytes 1572872 | tf_op jit(solution)/shard_map/ppermute | solution.py:27
  30.7 11.2 %collective-permute-start.16 = (bf16[128,1024]{1,0:T(8,128)(2,1)S(1)}, bf16[128,1024]{1,0:T(8,128)(2,1)S(1)}, u32[]{:S(2)}, u32[]{:S(2)}) collective-permute-start(bf16[128,1024]{1,0:T(8,128)(2,1)S(1)} %broadcast_select_fusion.13), channel_id=1, source_target_pairs={{0,8},{4,12},{8,0},{12,4},{16,24},{20,28},{24,16},{28,20},{1,9},{5... | collective-permute-start | bytes 786440 | tf_op jit(solution)/shard_map/ppermute | solution.py:27
  42.1 3.6 %collective-permute-start.12 = (bf16[1024,128]{1,0:T(8,128)(2,1)S(1)}, bf16[1024,128]{1,0:T(8,128)(2,1)S(1)}, u32[]{:S(2)}, u32[]{:S(2)}) collective-permute-start(bf16[1024,128]{1,0:T(8,128)(2,1)S(1)} %broadcast_select_fusion.16), channel_id=1, source_target_pairs={{0,16},{4,20},{8,24},{12,28},{16,0},{20,4},{24,8},{28,12},{1,17},{... | collective-permute-start | bytes 786440 | tf_op jit(solution)/shard_map/ppermute | solution.py:27
  47.4 12.5 %collective-permute-done.12 = bf16[1024,128]{1,0:T(8,128)(2,1)S(1)} collective-permute-done((bf16[1024,128]{1,0:T(8,128)(2,1)S(1)}, bf16[1024,128]{1,0:T(8,128)(2,1)S(1)}, u32[]{:S(2)}, u32[]{:S(2)}) %collective-permute-start.12) | collective-permute-done | bytes 262176 | tf_op jit(solution)/shard_map/ppermute | solution.py:27
  59.9 1.5 %collective-permute-done.13 = bf16[1024,128]{1,0:T(8,128)(2,1)S(1)} collective-permute-done((bf16[1024,128]{1,0:T(8,128)(2,1)S(1)}, bf16[1024,128]{1,0:T(8,128)(2,1)S(1)}, u32[]{:S(2)}, u32[]{:S(2)}) %collective-permute-start.13) | collective-permute-done | bytes 262176 | tf_op jit(solution)/shard_map/ppermute | solution.py:27
  61.5 1.8 %shard_map.56.solved = bf16[2,1024,128]{2,1,0:T(8,128)(2,1)S(1)} custom-call(s32[2,2]{1,0:T(2,128)S(1)} %copy-done.4, bf16[2,1024,1024]{2,1,0:T(8,128)(2,1)S(1)} %copy-done, bf16[1024,128]{1,0:T(8,128)(2,1)S(1)} %broadcast_select_fusion.12.fixed, bf16[1024,128]{1,0:T(8,128)(2,1)S(1)} %broadcast_select_fusion.14.moving), custom_call_target="tpu_custom_call" | custom-call | tf_op jit(solution)/shard_map/pallas_call | solution.py:256
  65.7 1.4 %collective-permute-start.15 = (bf16[128,1024]{1,0:T(8,128)(2,1)S(1)}, bf16[128,1024]{1,0:T(8,128)(2,1)S(1)}, u32[]{:S(2)}, u32[]{:S(2)}) collective-permute-start(bf16[128,1024]{1,0:T(8,128)(2,1)S(1)} %broadcast_select_fusion.20), channel_id=1, source_target_pairs={{8,0},{12,4},{24,16},{28,20},{9,1},{13,5},{25,17},{29,21},{10,2},{... | collective-permute-start | bytes 786440 | tf_op jit(solution)/shard_map/ppermute | solution.py:27
  67.1 1.9 %collective-permute-done.18 = bf16[2,128,128]{2,1,0:T(8,128)(2,1)S(1)} collective-permute-done((bf16[2,128,128]{2,1,0:T(8,128)(2,1)S(1)}, bf16[2,128,128]{2,1,0:T(8,128)(2,1)S(1)}, u32[]{:S(2)}, u32[]{:S(2)}) %collective-permute-start.18) | collective-permute-done | bytes 65568 | tf_op jit(solution)/shard_map/ppermute | solution.py:27
  69.1 4.7 %collective-permute-start.21 = (bf16[2,128,128]{2,1,0:T(8,128)(2,1)S(1)}, bf16[2,128,128]{2,1,0:T(8,128)(2,1)S(1)}, u32[]{:S(2)}, u32[]{:S(2)}) collective-permute-start(bf16[2,128,128]{2,1,0:T(8,128)(2,1)S(1)} %broadcast_select_fusion.23), channel_id=1, source_target_pairs={{0,16},{4,20},{8,24},{12,28},{16,0},{20,4},{24,8},{28,12},{1,17},{... | collective-permute-start | bytes 196616 | tf_op jit(solution)/shard_map/ppermute | solution.py:27
  73.8 2.3 %collective-permute-done.21 = bf16[2,128,128]{2,1,0:T(8,128)(2,1)S(1)} collective-permute-done((bf16[2,128,128]{2,1,0:T(8,128)(2,1)S(1)}, bf16[2,128,128]{2,1,0:T(8,128)(2,1)S(1)}, u32[]{:S(2)}, u32[]{:S(2)}) %collective-permute-start.21) | collective-permute-done | bytes 65568 | tf_op jit(solution)/shard_map/ppermute | solution.py:27
  76.7 2.1 %collective-permute-done.3 = bf16[2,1024,128]{2,1,0:T(8,128)(2,1)S(1)} collective-permute-done((bf16[2,1024,128]{2,1,0:T(8,128)(2,1)S(1)}, bf16[2,1024,128]{2,1,0:T(8,128)(2,1)S(1)}, u32[]{:S(2)}, u32[]{:S(2)}) %collective-permute-start.3) | collective-permute-done | bytes 524320 | tf_op jit(solution)/shard_map/ppermute | solution.py:27
  78.9 2.8 %collective-permute-start.19 = (bf16[128,1024]{1,0:T(8,128)(2,1)S(1)}, bf16[128,1024]{1,0:T(8,128)(2,1)S(1)}, u32[]{:S(2)}, u32[]{:S(2)}) collective-permute-start(bf16[128,1024]{1,0:T(8,128)(2,1)S(1)} %broadcast_select_fusion.10), channel_id=1, source_target_pairs={{0,16},{4,20},{8,24},{12,28},{16,0},{20,4},{24,8},{28,12},{1,17},{... | collective-permute-start | bytes 786440 | tf_op jit(solution)/shard_map/ppermute | solution.py:27
  82.1 12.1 %collective-permute-done.19 = bf16[128,1024]{1,0:T(8,128)(2,1)S(1)} collective-permute-done((bf16[128,1024]{1,0:T(8,128)(2,1)S(1)}, bf16[128,1024]{1,0:T(8,128)(2,1)S(1)}, u32[]{:S(2)}, u32[]{:S(2)}) %collective-permute-start.19) | collective-permute-done | bytes 262176 | tf_op jit(solution)/shard_map/ppermute | solution.py:27
  94.3 1.8 %collective-permute-start.20 = (bf16[2,128,1024]{2,1,0:T(8,128)(2,1)S(1)}, bf16[2,128,1024]{2,1,0:T(8,128)(2,1)S(1)}, u32[]{:S(2)}, u32[]{:S(2)}) collective-permute-start(bf16[2,128,1024]{2,1,0:T(8,128)(2,1)S(1)} %pad_maximum_fusion.1), channel_id=1, source_target_pairs={{0,4},{4,0},{8,12},{12,8},{16,20},{20,16},{24,28},{28,24},{1,5},{5... | collective-permute-start | bytes 1572872 | tf_op jit(solution)/shard_map/ppermute | solution.py:27
  97.7 4.3 %collective-permute-done.24 = bf16[640,128]{1,0:T(8,128)(2,1)S(1)} collective-permute-done((bf16[640,128]{1,0:T(8,128)(2,1)S(1)}, bf16[640,128]{1,0:T(8,128)(2,1)S(1)}, u32[]{:S(2)}, u32[]{:S(2)}) %collective-permute-start.24) | collective-permute-done | bytes 163872 | tf_op jit(solution)/shard_map/ppermute | solution.py:27
  102.2 5.9 %collective-permute-done.20 = bf16[2,128,1024]{2,1,0:T(8,128)(2,1)S(1)} collective-permute-done((bf16[2,128,1024]{2,1,0:T(8,128)(2,1)S(1)}, bf16[2,128,1024]{2,1,0:T(8,128)(2,1)S(1)}, u32[]{:S(2)}, u32[]{:S(2)}) %collective-permute-start.20) | collective-permute-done | bytes 524320 | tf_op jit(solution)/shard_map/ppermute | solution.py:27
  108.4 8.6 %shard_map.58 = bf16[2,2,1024,1024]{3,2,1,0:T(8,128)(2,1)} custom-call(s32[2,2]{1,0:T(2,128)S(1)} %copy-done.4, s32[2,2]{1,0:T(2,128)S(1)} %copy-done.6, bf16[2,2,1024,128]{3,2,1,0:T(8,128)(2,1)S(1)} %copy-done.2, bf16[2,2,128,1024]{3,2,1,0:T(8,128)(2,1)S(1)} %copy-done.3, bf16[2,1024,128]{2,1,0:T(8,128)(2,1)S(1)} %get-tuple-element.72.first, ...), custom_call_target="tpu_custom_call" | custom-call | tf_op jit(solution)/shard_map/pallas_call | solution.py:289
  (88 shorter events, 13.3 us)
Async XLA Ops:
  5.0 9.3 %collective-permute-start.5 = (bf16[1024,128]{1,0:T(8,128)(2,1)S(1)}, bf16[1024,128]{1,0:T(8,128)(2,1)S(1)}, u32[]{:S(2)}, u32[]{:S(2)}) collective-permute-start(bf16[1024,128]{1,0:T(8,128)(2,1)S(1)} %get-tuple-element.40), channel_id=1, source_target_pairs={{0,4},{4,0},{8,12},{12,8},{16,20},{20,16},{24,28},{28,24},{1,5},{5... | collective-permute-start | bytes 786440 | tf_op jit(solution)/shard_map/ppermute | solution.py:27
  8.0 6.3 %collective-permute-start.6 = (bf16[1024,128]{1,0:T(8,128)(2,1)S(1)}, bf16[1024,128]{1,0:T(8,128)(2,1)S(1)}, u32[]{:S(2)}, u32[]{:S(2)}) collective-permute-start(bf16[1024,128]{1,0:T(8,128)(2,1)S(1)} %get-tuple-element.42), channel_id=1, source_target_pairs={{28,24},{29,25},{30,26},{31,27}} | collective-permute-start | bytes 786440 | tf_op jit(solution)/shard_map/ppermute | solution.py:27
  8.7 6.4 %collective-permute-start = (bf16[2,1024,128]{2,1,0:T(8,128)(2,1)S(1)}, bf16[2,1024,128]{2,1,0:T(8,128)(2,1)S(1)}, u32[]{:S(2)}, u32[]{:S(2)}) collective-permute-start(bf16[2,1024,128]{2,1,0:T(8,128)(2,1)S(1)} %get-tuple-element.35), channel_id=1, source_target_pairs={{0,1},{1,0},{2,3},{3,2},{4,5},{5,4},{6,7},{7,6},{8,9},{9,8},{10,11... | collective-permute-start | bytes 1572872 | tf_op jit(solution)/shard_map/ppermute | solution.py:27
  14.4 6.6 %collective-permute-start.7 = (bf16[128,1024]{1,0:T(8,128)(2,1)S(1)}, bf16[128,1024]{1,0:T(8,128)(2,1)S(1)}, u32[]{:S(2)}, u32[]{:S(2)}) collective-permute-start(bf16[128,1024]{1,0:T(8,128)(2,1)S(1)} %get-tuple-element.43), channel_id=1, source_target_pairs={{28,24},{29,25},{30,26},{31,27}} | collective-permute-start | bytes 786440 | tf_op jit(solution)/shard_map/ppermute | solution.py:27
  15.2 13.2 %collective-permute-start.1 = (bf16[2,1024,128]{2,1,0:T(8,128)(2,1)S(1)}, bf16[2,1024,128]{2,1,0:T(8,128)(2,1)S(1)}, u32[]{:S(2)}, u32[]{:S(2)}) collective-permute-start(bf16[2,1024,128]{2,1,0:T(8,128)(2,1)S(1)} %broadcast_select_fusion.5), channel_id=1, source_target_pairs={{0,2},{1,3},{2,0},{3,1},{4,6},{5,7},{6,4},{7,5},{8,10},{9,11},{10,... | collective-permute-start | bytes 1572872 | tf_op jit(solution)/shard_map/ppermute | solution.py:27
  17.2 13.5 %collective-permute-start.11 = (bf16[128,1024]{1,0:T(8,128)(2,1)S(1)}, bf16[128,1024]{1,0:T(8,128)(2,1)S(1)}, u32[]{:S(2)}, u32[]{:S(2)}) collective-permute-start(bf16[128,1024]{1,0:T(8,128)(2,1)S(1)} %get-tuple-element.49), channel_id=1, source_target_pairs={{0,4},{4,0},{8,12},{12,8},{16,20},{20,16},{24,28},{28,24},{1,5},{5... | collective-permute-start | bytes 786440 | tf_op jit(solution)/shard_map/ppermute | solution.py:27
  18.7 11.2 %collective-permute-start.8 = (bf16[1024,128]{1,0:T(8,128)(2,1)S(1)}, bf16[1024,128]{1,0:T(8,128)(2,1)S(1)}, u32[]{:S(2)}, u32[]{:S(2)}) collective-permute-start(bf16[1024,128]{1,0:T(8,128)(2,1)S(1)} %broadcast_select_fusion.18), channel_id=1, source_target_pairs={{0,8},{4,12},{8,0},{12,4},{16,24},{20,28},{24,16},{28,20},{1,9},{5... | collective-permute-start | bytes 786440 | tf_op jit(solution)/shard_map/ppermute | solution.py:27
  20.3 9.7 %collective-permute-start.9 = (bf16[1024,128]{1,0:T(8,128)(2,1)S(1)}, bf16[1024,128]{1,0:T(8,128)(2,1)S(1)}, u32[]{:S(2)}, u32[]{:S(2)}) collective-permute-start(bf16[1024,128]{1,0:T(8,128)(2,1)S(1)} %broadcast_select_fusion.17), channel_id=1, source_target_pairs={{24,8},{28,12},{25,9},{29,13},{26,10},{30,14},{27,11},{31,15}} | collective-permute-start | bytes 786440 | tf_op jit(solution)/shard_map/ppermute | solution.py:27
  28.4 13.5 %collective-permute-start.14 = (bf16[2,1024,128]{2,1,0:T(8,128)(2,1)S(1)}, bf16[2,1024,128]{2,1,0:T(8,128)(2,1)S(1)}, u32[]{:S(2)}, u32[]{:S(2)}) collective-permute-start(bf16[2,1024,128]{2,1,0:T(8,128)(2,1)S(1)} %broadcast_select_fusion.7), channel_id=1, source_target_pairs={{0,4},{4,0},{8,12},{12,8},{16,20},{20,16},{24,28},{28,24},{1,5},{5... | collective-permute-start | bytes 1572872 | tf_op jit(solution)/shard_map/ppermute | solution.py:27
  30.0 17.0 %collective-permute-start.10 = (bf16[128,1024]{1,0:T(8,128)(2,1)S(1)}, bf16[128,1024]{1,0:T(8,128)(2,1)S(1)}, u32[]{:S(2)}, u32[]{:S(2)}) collective-permute-start(bf16[128,1024]{1,0:T(8,128)(2,1)S(1)} %broadcast_select_fusion.19), channel_id=1, source_target_pairs={{24,8},{28,12},{25,9},{29,13},{26,10},{30,14},{27,11},{31,15}} | collective-permute-start | bytes 786440 | tf_op jit(solution)/shard_map/ppermute | solution.py:27
  30.7 16.6 %collective-permute-start.16 = (bf16[128,1024]{1,0:T(8,128)(2,1)S(1)}, bf16[128,1024]{1,0:T(8,128)(2,1)S(1)}, u32[]{:S(2)}, u32[]{:S(2)}) collective-permute-start(bf16[128,1024]{1,0:T(8,128)(2,1)S(1)} %broadcast_select_fusion.13), channel_id=1, source_target_pairs={{0,8},{4,12},{8,0},{12,4},{16,24},{20,28},{24,16},{28,20},{1,9},{5... | collective-permute-start | bytes 786440 | tf_op jit(solution)/shard_map/ppermute | solution.py:27
  42.0 21.4 %collective-permute-start.17 = (bf16[4,1024,128]{2,1,0:T(8,128)(2,1)S(1)}, bf16[4,1024,128]{2,1,0:T(8,128)(2,1)S(1)}, u32[]{:S(2)}, u32[]{:S(2)}) collective-permute-start(bf16[4,1024,128]{2,1,0:T(8,128)(2,1)S(1)} %pad_maximum_fusion), channel_id=1, source_target_pairs={{0,1},{1,0},{2,3},{3,2},{4,5},{5,4},{6,7},{7,6},{8,9},{9,8},{10,11... | collective-permute-start | bytes 3145736 | tf_op jit(solution)/shard_map/ppermute | solution.py:27
  42.1 17.8 %collective-permute-start.12 = (bf16[1024,128]{1,0:T(8,128)(2,1)S(1)}, bf16[1024,128]{1,0:T(8,128)(2,1)S(1)}, u32[]{:S(2)}, u32[]{:S(2)}) collective-permute-start(bf16[1024,128]{1,0:T(8,128)(2,1)S(1)} %broadcast_select_fusion.16), channel_id=1, source_target_pairs={{0,16},{4,20},{8,24},{12,28},{16,0},{20,4},{24,8},{28,12},{1,17},{... | collective-permute-start | bytes 786440 | tf_op jit(solution)/shard_map/ppermute | solution.py:27
  45.7 15.8 %collective-permute-start.13 = (bf16[1024,128]{1,0:T(8,128)(2,1)S(1)}, bf16[1024,128]{1,0:T(8,128)(2,1)S(1)}, u32[]{:S(2)}, u32[]{:S(2)}) collective-permute-start(bf16[1024,128]{1,0:T(8,128)(2,1)S(1)} %broadcast_select_fusion.15), channel_id=1, source_target_pairs={{8,0},{12,4},{24,16},{28,20},{9,1},{13,5},{25,17},{29,21},{10,2},{... | collective-permute-start | bytes 786440 | tf_op jit(solution)/shard_map/ppermute | solution.py:27
  47.0 18.5 %collective-permute-start.2 = (bf16[2,1024,128]{2,1,0:T(8,128)(2,1)S(1)}, bf16[2,1024,128]{2,1,0:T(8,128)(2,1)S(1)}, u32[]{:S(2)}, u32[]{:S(2)}) collective-permute-start(bf16[2,1024,128]{2,1,0:T(8,128)(2,1)S(1)} %get-tuple-element.36), channel_id=1, source_target_pairs={{0,1},{1,0},{2,3},{3,2},{4,5},{5,4},{6,7},{7,6},{8,9},{9,8},{10,11... | collective-permute-start | bytes 1572872 | tf_op jit(solution)/shard_map/ppermute | solution.py:27
  65.6 13.1 %collective-permute-start.3 = (bf16[2,1024,128]{2,1,0:T(8,128)(2,1)S(1)}, bf16[2,1024,128]{2,1,0:T(8,128)(2,1)S(1)}, u32[]{:S(2)}, u32[]{:S(2)}) collective-permute-start(bf16[2,1024,128]{2,1,0:T(8,128)(2,1)S(1)} %broadcast_select_fusion.4), channel_id=1, source_target_pairs={{0,2},{1,3},{2,0},{3,1},{4,6},{5,7},{6,4},{7,5},{8,10},{9,11},{10,... | collective-permute-start | bytes 1572872 | tf_op jit(solution)/shard_map/ppermute | solution.py:27
  65.7 16.4 %collective-permute-start.15 = (bf16[128,1024]{1,0:T(8,128)(2,1)S(1)}, bf16[128,1024]{1,0:T(8,128)(2,1)S(1)}, u32[]{:S(2)}, u32[]{:S(2)}) collective-permute-start(bf16[128,1024]{1,0:T(8,128)(2,1)S(1)} %broadcast_select_fusion.20), channel_id=1, source_target_pairs={{8,0},{12,4},{24,16},{28,20},{9,1},{13,5},{25,17},{29,21},{10,2},{... | collective-permute-start | bytes 786440 | tf_op jit(solution)/shard_map/ppermute | solution.py:27
  69.1 7.0 %collective-permute-start.21 = (bf16[2,128,128]{2,1,0:T(8,128)(2,1)S(1)}, bf16[2,128,128]{2,1,0:T(8,128)(2,1)S(1)}, u32[]{:S(2)}, u32[]{:S(2)}) collective-permute-start(bf16[2,128,128]{2,1,0:T(8,128)(2,1)S(1)} %broadcast_select_fusion.23), channel_id=1, source_target_pairs={{0,16},{4,20},{8,24},{12,28},{16,0},{20,4},{24,8},{28,12},{1,17},{... | collective-permute-start | bytes 196616 | tf_op jit(solution)/shard_map/ppermute | solution.py:27
  76.2 5.7 %collective-permute-start.22 = (bf16[2,384,128]{2,1,0:T(8,128)(2,1)S(1)}, bf16[2,384,128]{2,1,0:T(8,128)(2,1)S(1)}, u32[]{:S(2)}, u32[]{:S(2)}) collective-permute-start(bf16[2,384,128]{2,1,0:T(8,128)(2,1)S(1)} %get-tuple-element.100), channel_id=1, source_target_pairs={{0,4},{4,0},{8,12},{12,8},{16,20},{20,16},{24,28},{28,24},{1,5},{5... | collective-permute-start | bytes 589832 | tf_op jit(solution)/shard_map/ppermute | solution.py:27
  78.8 18.8 %collective-permute-start.4 = (bf16[2,1024,128]{2,1,0:T(8,128)(2,1)S(1)}, bf16[2,1024,128]{2,1,0:T(8,128)(2,1)S(1)}, u32[]{:S(2)}, u32[]{:S(2)}) collective-permute-start(bf16[2,1024,128]{2,1,0:T(8,128)(2,1)S(1)} %broadcast_select_fusion.6), channel_id=1, source_target_pairs={{0,1},{1,0},{2,3},{3,2},{4,5},{5,4},{6,7},{7,6},{8,9},{9,8},{10,11... | collective-permute-start | bytes 1572872 | tf_op jit(solution)/shard_map/ppermute | solution.py:27
  78.9 15.3 %collective-permute-start.19 = (bf16[128,1024]{1,0:T(8,128)(2,1)S(1)}, bf16[128,1024]{1,0:T(8,128)(2,1)S(1)}, u32[]{:S(2)}, u32[]{:S(2)}) collective-permute-start(bf16[128,1024]{1,0:T(8,128)(2,1)S(1)} %broadcast_select_fusion.10), channel_id=1, source_target_pairs={{0,16},{4,20},{8,24},{12,28},{16,0},{20,4},{24,8},{28,12},{1,17},{... | collective-permute-start | bytes 786440 | tf_op jit(solution)/shard_map/ppermute | solution.py:27
  82.0 14.1 %collective-permute-start.23 = (bf16[640,128]{1,0:T(8,128)(2,1)S(1)}, bf16[640,128]{1,0:T(8,128)(2,1)S(1)}, u32[]{:S(2)}, u32[]{:S(2)}) collective-permute-start(bf16[640,128]{1,0:T(8,128)(2,1)S(1)} %pad_maximum_fusion.6), channel_id=1, source_target_pairs={{0,1},{1,0},{2,3},{3,2},{4,5},{5,4},{6,7},{7,6},{8,9},{9,8},{10,11... | collective-permute-start | bytes 491528 | tf_op jit(solution)/shard_map/ppermute | solution.py:27
  94.3 13.7 %collective-permute-start.20 = (bf16[2,128,1024]{2,1,0:T(8,128)(2,1)S(1)}, bf16[2,128,1024]{2,1,0:T(8,128)(2,1)S(1)}, u32[]{:S(2)}, u32[]{:S(2)}) collective-permute-start(bf16[2,128,1024]{2,1,0:T(8,128)(2,1)S(1)} %pad_maximum_fusion.1), channel_id=1, source_target_pairs={{0,4},{4,0},{8,12},{12,8},{16,20},{20,16},{24,28},{28,24},{1,5},{5... | collective-permute-start | bytes 1572872 | tf_op jit(solution)/shard_map/ppermute | solution.py:27
  96.3 5.7 %collective-permute-start.24 = (bf16[640,128]{1,0:T(8,128)(2,1)S(1)}, bf16[640,128]{1,0:T(8,128)(2,1)S(1)}, u32[]{:S(2)}, u32[]{:S(2)}) collective-permute-start(bf16[640,128]{1,0:T(8,128)(2,1)S(1)} %select_select_fusion), channel_id=1, source_target_pairs={{0,2},{1,3},{2,0},{3,1},{4,6},{5,7},{6,4},{7,5},{8,10},{9,11},{10,... | collective-permute-start | bytes 491528 | tf_op jit(solution)/shard_map/ppermute | solution.py:27
  (8 other events, 194.0 us)

commit v3 on v2

--- a/solution.py
+++ b/solution.py
@@ -241,15 +241,13 @@
                 ties.append(cv.mine)
                 near = swap(cv.mine, "row", rows_n, 1)
                 cu = Lane(cu_k, after(cu_g, cv.mine), "col", cols_n, same_both)
+                cv_first, cv_second = joined(jnp.concatenate([cv.mine, near]), "col", cols_n, "side_c")
             else:
-                follow.append(near)
-            if k < len(upper_bits(rows_n)) - 1:
-                for lane in v_lanes:
-                    lane.step(k, *follow)
-        v_lanes[1].step(k, *follow)
+                follow.append(cv_first)
+            for lane in v_lanes:
+                lane.step(k, *follow)
         for m in range(len(cu.bits)):
             cu.step(m)
-        cv_first, cv_second = joined(jnp.concatenate([cv.mine, near]), "col", cols_n, "side_c")
         cu_first, cu_second = joined(cu.mine, "col", cols_n, "side_c")
 
         moving, fixed = mines(u_lanes)
@@ -267,11 +265,16 @@
             out_specs=[WHOLE] * 2,
             compiler_params=params(),
         )(panel_order, solved, cv_first, cv_second)
-        for m, bit in enumerate(upper_bits(rows_n)):
-            got = swap(foot, "row", rows_n, bit)
-            foot = jnp.where(jnp.stack([flag(("p2", bit), foot), flag(("p1", bit), foot)]), foot, got)
-            if m == 0:
-                v_lanes[0].step(k, foot, *follow)
+        def at_root(bit):
+            return jnp.stack([flag(("p2", bit), foot), flag(("p1", bit), foot)])
+
+        bits = upper_bits(rows_n)
+        if len(bits) == 2:
+            one, two, three = (swap(foot, "row", rows_n, bit) for bit in (*bits, sum(bits)))
+            foot = jnp.where(at_root(bits[1]), jnp.where(at_root(bits[0]), foot, one), jnp.where(at_root(bits[0]), two, three))
+        else:
+            for bit in bits:
+                foot = jnp.where(at_root(bit), foot, swap(foot, "row", rows_n, bit))
         swapped = swap(jnp.concatenate([cores[:, 2 * rank:], foot], axis=1), "row", rows_n, 1)
         cores = jnp.concatenate([cores[:, :2 * rank], foot], axis=1)
         edge = jnp.concatenate([choose("q2_side", cores[0, :2 * rank], swapped[0, :2 * rank]), choose("q1_side", cores[1], swapped[1])])
@@ -281,7 +284,7 @@
             stays = jnp.where(early, flag(("q2", bit), edge), flag(("q1", bit), edge))
             edge = jnp.where(stays, edge, got)
 
-        moving, fixed = mines(v_lanes)
+        moving, fixed = (after(x, foot) for x in mines(v_lanes))
         mine = jnp.stack([choose("row_first", fixed, moving), choose("row_first", moving, fixed)])
         vj0, vj1 = joined(mine, "row", rows_n, "side_r")
         vp1, vp2 = (jnp.stack([vj0[s], vj1[s]]) for s in range(2))

time: 117 us -> 113 us (0.966)
  waiting for transfers between devices: 55.8 us -> 48.5 us
  starting transfers between devices: 42.1 us -> 45.4 us
    ppermute x25 -> x26, waiting for transfers between devices: 55.8 us -> 48.5 us  [swap(): return lax.ppermute(block, axis, [(s, s ^ bit) for s in senders])]
    ppermute x25 -> x26, starting transfers between devices: 42.1 us -> 45.4 us  [swap(): return lax.ppermute(block, axis, [(s, s ^ bit) for s in senders])]
  transfers between devices with their start and end apart: 25 -> 26, of which waited for: 11 -> 11; matrix products, arithmetic and copies ran while one was open for 1% -> 2% of each run, Pallas kernels for 3% -> 3%
where the time goes in v3:
time: 113 us
  waiting for transfers between devices  48.5 us (43%)
  starting transfers between devices  45.4 us (40%)
  Pallas kernels  14.1 us (12%)
  local copies, waits for them, and re-layouts  2.72 us (2%)
  other arithmetic  1.84 us (2%)
    ppermute x26, waiting for transfers between devices, swap(): return lax.ppermute(block, axis, [(s, s ^ bit) for s in senders])  48.5 us
    ppermute x26, starting transfers between devices, swap(): return lax.ppermute(block, axis, [(s, s ^ bit) for s in senders])  45.4 us
    pallas_call x1, Pallas kernels, on_device(): pl.pallas_call(functools.partial(final_kernel, last_col=last['last_col'])...  8.58 us
    unnamed x18, local copies, waits for them, and re-layouts  2.63 us
    pallas_call x1, Pallas kernels, on_device(): pl.pallas_call(functools.partial(prep_kernel, rows_n=rows_n, cols_n=cols_...  2.42 us
  transfers between devices with their start and end apart: 26, of which 11 were waited for; matrix products, arithmetic and copies ran while one was open for 2% of the time, Pallas kernels for 3%

profile of v3, /device:TPU:0, one launch (start us, length us, event | category | flops | bytes accessed | tf_op | source)
XLA Modules:
  0.0 113.0 jit_solution(127213519543531644)
XLA Ops:
  2.6 2.4 %shard_map.55 = (s32[23,1024]{1,0:T(8,128)S(1)}, bf16[1024,128]{1,0:T(8,128)(2,1)S(1)}, bf16[1024,128]{1,0:T(8,128)(2,1)S(1)}, bf16[1024,128]{1,0:T(8,128)(2,1)S...) custom-call(s32[2,2]{1,0:T(2,128)S(1)} %copy-done.4, ...), custom_call_target="tpu_custom_call" | custom-call | tf_op jit(solution)/shard_map/pallas_call | solution.py:194
  5.0 3.0 %collective-permute-start.5 = (bf16[1024,128]{1,0:T(8,128)(2,1)S(1)}, bf16[1024,128]{1,0:T(8,128)(2,1)S(1)}, u32[]{:S(2)}, u32[]{:S(2)}) collective-permute-start(bf16[1024,128]{1,0:T(8,128)(2,1)S(1)} %get-tuple-element.42), channel_id=1, source_target_pairs={{0,4},{4,0},{8,12},{12,8},{16,20},{20,16},{24,28},{28,24},{1,5},{5... | collective-permute-start | bytes 786440 | tf_op jit(solution)/shard_map/ppermute | solution.py:27
  8.9 5.5 %collective-permute-done.5 = bf16[1024,128]{1,0:T(8,128)(2,1)S(1)} collective-permute-done((bf16[1024,128]{1,0:T(8,128)(2,1)S(1)}, bf16[1024,128]{1,0:T(8,128)(2,1)S(1)}, u32[]{:S(2)}, u32[]{:S(2)}) %collective-permute-start.5) | collective-permute-done | bytes 262176 | tf_op jit(solution)/shard_map/ppermute | solution.py:27
  15.2 1.8 %collective-permute-start.1 = (bf16[2,1024,128]{2,1,0:T(8,128)(2,1)S(1)}, bf16[2,1024,128]{2,1,0:T(8,128)(2,1)S(1)}, u32[]{:S(2)}, u32[]{:S(2)}) collective-permute-start(bf16[2,1024,128]{2,1,0:T(8,128)(2,1)S(1)} %broadcast_select_fusion.5), channel_id=1, source_target_pairs={{0,2},{1,3},{2,0},{3,1},{4,6},{5,7},{6,4},{7,5},{8,10},{9,11},{10,... | collective-permute-start | bytes 1572872 | tf_op jit(solution)/shard_map/ppermute | solution.py:27
  17.2 1.6 %collective-permute-start.11 = (bf16[128,1024]{1,0:T(8,128)(2,1)S(1)}, bf16[128,1024]{1,0:T(8,128)(2,1)S(1)}, u32[]{:S(2)}, u32[]{:S(2)}) collective-permute-start(bf16[128,1024]{1,0:T(8,128)(2,1)S(1)} %get-tuple-element.51), channel_id=1, source_target_pairs={{0,4},{4,0},{8,12},{12,8},{16,20},{20,16},{24,28},{28,24},{1,5},{5... | collective-permute-start | bytes 786440 | tf_op jit(solution)/shard_map/ppermute | solution.py:27
  18.7 1.6 %collective-permute-start.8 = (bf16[1024,128]{1,0:T(8,128)(2,1)S(1)}, bf16[1024,128]{1,0:T(8,128)(2,1)S(1)}, u32[]{:S(2)}, u32[]{:S(2)}) collective-permute-start(bf16[1024,128]{1,0:T(8,128)(2,1)S(1)} %broadcast_select_fusion.18), channel_id=1, source_target_pairs={{0,8},{4,12},{8,0},{12,4},{16,24},{20,28},{24,16},{28,20},{1,9},{5... | collective-permute-start | bytes 786440 | tf_op jit(solution)/shard_map/ppermute | solution.py:27
  21.0 7.3 %collective-permute-done.1 = bf16[2,1024,128]{2,1,0:T(8,128)(2,1)S(1)} collective-permute-done((bf16[2,1024,128]{2,1,0:T(8,128)(2,1)S(1)}, bf16[2,1024,128]{2,1,0:T(8,128)(2,1)S(1)}, u32[]{:S(2)}, u32[]{:S(2)}) %collective-permute-start.1) | collective-permute-done | bytes 524320 | tf_op jit(solution)/shard_map/ppermute | solution.py:27
  28.4 1.5 %collective-permute-start.14 = (bf16[2,1024,128]{2,1,0:T(8,128)(2,1)S(1)}, bf16[2,1024,128]{2,1,0:T(8,128)(2,1)S(1)}, u32[]{:S(2)}, u32[]{:S(2)}) collective-permute-start(bf16[2,1024,128]{2,1,0:T(8,128)(2,1)S(1)} %broadcast_select_fusion.7), channel_id=1, source_target_pairs={{0,4},{4,0},{8,12},{12,8},{16,20},{20,16},{24,28},{28,24},{1,5},{5... | collective-permute-start | bytes 1572872 | tf_op jit(solution)/shard_map/ppermute | solution.py:27
  30.8 11.1 %collective-permute-start.20 = (bf16[128,1024]{1,0:T(8,128)(2,1)S(1)}, bf16[128,1024]{1,0:T(8,128)(2,1)S(1)}, u32[]{:S(2)}, u32[]{:S(2)}) collective-permute-start(bf16[128,1024]{1,0:T(8,128)(2,1)S(1)} %broadcast_select_fusion.13), channel_id=1, source_target_pairs={{0,8},{4,12},{8,0},{12,4},{16,24},{20,28},{24,16},{28,20},{1,9},{5... | collective-permute-start | bytes 786440 | tf_op jit(solution)/shard_map/ppermute | solution.py:27
  41.9 3.6 %collective-permute-start.12 = (bf16[1024,128]{1,0:T(8,128)(2,1)S(1)}, bf16[1024,128]{1,0:T(8,128)(2,1)S(1)}, u32[]{:S(2)}, u32[]{:S(2)}) collective-permute-start(bf16[1024,128]{1,0:T(8,128)(2,1)S(1)} %broadcast_select_fusion.16), channel_id=1, source_target_pairs={{0,16},{4,20},{8,24},{12,28},{16,0},{20,4},{24,8},{28,12},{1,17},{... | collective-permute-start | bytes 786440 | tf_op jit(solution)/shard_map/ppermute | solution.py:27
  45.4 1.3 %collective-permute-start.13 = (bf16[1024,128]{1,0:T(8,128)(2,1)S(1)}, bf16[1024,128]{1,0:T(8,128)(2,1)S(1)}, u32[]{:S(2)}, u32[]{:S(2)}) collective-permute-start(bf16[1024,128]{1,0:T(8,128)(2,1)S(1)} %broadcast_select_fusion.15), channel_id=1, source_target_pairs={{8,0},{12,4},{24,16},{28,20},{9,1},{13,5},{25,17},{29,21},{10,2},{... | collective-permute-start | bytes 786440 | tf_op jit(solution)/shard_map/ppermute | solution.py:27
  48.5 9.0 %collective-permute-done.12 = bf16[1024,128]{1,0:T(8,128)(2,1)S(1)} collective-permute-done((bf16[1024,128]{1,0:T(8,128)(2,1)S(1)}, bf16[1024,128]{1,0:T(8,128)(2,1)S(1)}, u32[]{:S(2)}, u32[]{:S(2)}) %collective-permute-start.12) | collective-permute-done | bytes 262176 | tf_op jit(solution)/shard_map/ppermute | solution.py:27
  57.9 1.8 %shard_map.56.solved = bf16[2,1024,128]{2,1,0:T(8,128)(2,1)S(1)} custom-call(s32[2,2]{1,0:T(2,128)S(1)} %copy-done.4, bf16[2,1024,1024]{2,1,0:T(8,128)(2,1)S(1)} %copy-done, bf16[1024,128]{1,0:T(8,128)(2,1)S(1)} %broadcast_select_fusion.12.fixed, bf16[1024,128]{1,0:T(8,128)(2,1)S(1)} %broadcast_select_fusion.14.moving), custom_call_target="tpu_custom_call" | custom-call | tf_op jit(solution)/shard_map/pallas_call | solution.py:254
  59.7 1.7 %collective-permute-done.3 = bf16[2,1024,128]{2,1,0:T(8,128)(2,1)S(1)} collective-permute-done((bf16[2,1024,128]{2,1,0:T(8,128)(2,1)S(1)}, bf16[2,1024,128]{2,1,0:T(8,128)(2,1)S(1)}, u32[]{:S(2)}, u32[]{:S(2)}) %collective-permute-start.3) | collective-permute-done | bytes 524320 | tf_op jit(solution)/shard_map/ppermute | solution.py:27
  61.7 1.3 %shard_map.57 = (bf16[2,512,128]{2,1,0:T(8,128)(2,1)S(1)}, bf16[2,128,128]{2,1,0:T(8,128)(2,1)S(1)}) custom-call(s32[2,2]{1,0:T(2,128)S(1)} %copy-done.4, bf16[2,1024,128]{2,1,0:T(8,128)(2,1)S(1)} %shard_map.56.solved, bf16[4,1024,128]{2,1,0:T(8,128)(2,1)S(1)} %get-tuple-element.70.first, bf16[4,1024,128]{2,1,0:T(8,128)(2,1)S(1)} %get-tuple-element.69.second), custom_call_target="tpu_custom_call" | custom-call | tf_op jit(solution)/shard_map/pallas_call | solution.py:261
  63.0 6.0 %collective-permute-start.19 = (bf16[2,128,128]{2,1,0:T(8,128)(2,1)S(1)}, bf16[2,128,128]{2,1,0:T(8,128)(2,1)S(1)}, u32[]{:S(2)}, u32[]{:S(2)}) collective-permute-start(bf16[2,128,128]{2,1,0:T(8,128)(2,1)S(1)} %get-tuple-element.55), channel_id=1, source_target_pairs={{0,24},{4,28},{8,16},{12,20},{16,8},{20,12},{24,0},{28,4},{1,25},{... | collective-permute-start | bytes 196616 | tf_op jit(solution)/shard_map/ppermute | solution.py:27
  70.6 1.3 %collective-permute-start.16 = (bf16[128,1024]{1,0:T(8,128)(2,1)S(1)}, bf16[128,1024]{1,0:T(8,128)(2,1)S(1)}, u32[]{:S(2)}, u32[]{:S(2)}) collective-permute-start(bf16[128,1024]{1,0:T(8,128)(2,1)S(1)} %get-tuple-element.54), channel_id=1, source_target_pairs={{8,0},{12,4},{24,16},{28,20},{9,1},{13,5},{25,17},{29,21},{10,2},{... | collective-permute-start | bytes 786440 | tf_op jit(solution)/shard_map/ppermute | solution.py:27
  71.9 5.3 %collective-permute-start.21 = (bf16[128,1024]{1,0:T(8,128)(2,1)S(1)}, bf16[128,1024]{1,0:T(8,128)(2,1)S(1)}, u32[]{:S(2)}, u32[]{:S(2)}) collective-permute-start(bf16[128,1024]{1,0:T(8,128)(2,1)S(1)} %get-tuple-element.58), channel_id=1, source_target_pairs={{0,16},{4,20},{8,24},{12,28},{16,0},{20,4},{24,8},{28,12},{1,17},{... | collective-permute-start | bytes 786440 | tf_op jit(solution)/shard_map/ppermute | solution.py:27
  77.9 8.1 %collective-permute-done.16 = bf16[128,1024]{1,0:T(8,128)(2,1)S(1)} collective-permute-done((bf16[128,1024]{1,0:T(8,128)(2,1)S(1)}, bf16[128,1024]{1,0:T(8,128)(2,1)S(1)}, u32[]{:S(2)}, u32[]{:S(2)}) %collective-permute-start.16) | collective-permute-done | bytes 262176 | tf_op jit(solution)/shard_map/ppermute | solution.py:27
  86.0 3.4 %collective-permute-done.21 = bf16[128,1024]{1,0:T(8,128)(2,1)S(1)} collective-permute-done((bf16[128,1024]{1,0:T(8,128)(2,1)S(1)}, bf16[128,1024]{1,0:T(8,128)(2,1)S(1)}, u32[]{:S(2)}, u32[]{:S(2)}) %collective-permute-start.21) | collective-permute-done | bytes 262176 | tf_op jit(solution)/shard_map/ppermute | solution.py:27
  91.1 1.6 %collective-permute-start.25 = (bf16[640,128]{1,0:T(8,128)(2,1)S(1)}, bf16[640,128]{1,0:T(8,128)(2,1)S(1)}, u32[]{:S(2)}, u32[]{:S(2)}) collective-permute-start(bf16[640,128]{1,0:T(8,128)(2,1)S(1)} %select_select_fusion), channel_id=1, source_target_pairs={{0,2},{1,3},{2,0},{3,1},{4,6},{5,7},{6,4},{7,5},{8,10},{9,11},{10,... | collective-permute-start | bytes 491528 | tf_op jit(solution)/shard_map/ppermute | solution.py:27
  92.8 4.6 %collective-permute-done.25 = bf16[640,128]{1,0:T(8,128)(2,1)S(1)} collective-permute-done((bf16[640,128]{1,0:T(8,128)(2,1)S(1)}, bf16[640,128]{1,0:T(8,128)(2,1)S(1)}, u32[]{:S(2)}, u32[]{:S(2)}) %collective-permute-start.25) | collective-permute-done | bytes 163872 | tf_op jit(solution)/shard_map/ppermute | solution.py:27
  97.6 6.5 %collective-permute-done.22 = bf16[2,128,1024]{2,1,0:T(8,128)(2,1)S(1)} collective-permute-done((bf16[2,128,1024]{2,1,0:T(8,128)(2,1)S(1)}, bf16[2,128,1024]{2,1,0:T(8,128)(2,1)S(1)}, u32[]{:S(2)}, u32[]{:S(2)}) %collective-permute-start.22) | collective-permute-done | bytes 524320 | tf_op jit(solution)/shard_map/ppermute | solution.py:27
  104.4 8.6 %shard_map.58 = bf16[2,2,1024,1024]{3,2,1,0:T(8,128)(2,1)} custom-call(s32[2,2]{1,0:T(2,128)S(1)} %copy-done.4, s32[2,2]{1,0:T(2,128)S(1)} %copy-done.6, bf16[2,2,1024,128]{3,2,1,0:T(8,128)(2,1)S(1)} %copy-done.2, bf16[2,2,128,1024]{3,2,1,0:T(8,128)(2,1)S(1)} %copy-done.3, bf16[2,1024,128]{2,1,0:T(8,128)(2,1)S(1)} %get-tuple-element.74.first, ...), custom_call_target="tpu_custom_call" | custom-call | tf_op jit(solution)/shard_map/pallas_call | solution.py:292
  (90 shorter events, 12.8 us)
Async XLA Ops:
  5.0 9.3 %collective-permute-start.5 = (bf16[1024,128]{1,0:T(8,128)(2,1)S(1)}, bf16[1024,128]{1,0:T(8,128)(2,1)S(1)}, u32[]{:S(2)}, u32[]{:S(2)}) collective-permute-start(bf16[1024,128]{1,0:T(8,128)(2,1)S(1)} %get-tuple-element.42), channel_id=1, source_target_pairs={{0,4},{4,0},{8,12},{12,8},{16,20},{20,16},{24,28},{28,24},{1,5},{5... | collective-permute-start | bytes 786440 | tf_op jit(solution)/shard_map/ppermute | solution.py:27
  8.0 6.3 %collective-permute-start.6 = (bf16[1024,128]{1,0:T(8,128)(2,1)S(1)}, bf16[1024,128]{1,0:T(8,128)(2,1)S(1)}, u32[]{:S(2)}, u32[]{:S(2)}) collective-permute-start(bf16[1024,128]{1,0:T(8,128)(2,1)S(1)} %get-tuple-element.44), channel_id=1, source_target_pairs={{28,24},{29,25},{30,26},{31,27}} | collective-permute-start | bytes 786440 | tf_op jit(solution)/shard_map/ppermute | solution.py:27
  8.7 6.4 %collective-permute-start = (bf16[2,1024,128]{2,1,0:T(8,128)(2,1)S(1)}, bf16[2,1024,128]{2,1,0:T(8,128)(2,1)S(1)}, u32[]{:S(2)}, u32[]{:S(2)}) collective-permute-start(bf16[2,1024,128]{2,1,0:T(8,128)(2,1)S(1)} %get-tuple-element.37), channel_id=1, source_target_pairs={{0,1},{1,0},{2,3},{3,2},{4,5},{5,4},{6,7},{7,6},{8,9},{9,8},{10,11... | collective-permute-start | bytes 1572872 | tf_op jit(solution)/shard_map/ppermute | solution.py:27
  14.4 6.6 %collective-permute-start.7 = (bf16[128,1024]{1,0:T(8,128)(2,1)S(1)}, bf16[128,1024]{1,0:T(8,128)(2,1)S(1)}, u32[]{:S(2)}, u32[]{:S(2)}) collective-permute-start(bf16[128,1024]{1,0:T(8,128)(2,1)S(1)} %get-tuple-element.45), channel_id=1, source_target_pairs={{28,24},{29,25},{30,26},{31,27}} | collective-permute-start | bytes 786440 | tf_op jit(solution)/shard_map/ppermute | solution.py:27
  15.2 13.2 %collective-permute-start.1 = (bf16[2,1024,128]{2,1,0:T(8,128)(2,1)S(1)}, bf16[2,1024,128]{2,1,0:T(8,128)(2,1)S(1)}, u32[]{:S(2)}, u32[]{:S(2)}) collective-permute-start(bf16[2,1024,128]{2,1,0:T(8,128)(2,1)S(1)} %broadcast_select_fusion.5), channel_id=1, source_target_pairs={{0,2},{1,3},{2,0},{3,1},{4,6},{5,7},{6,4},{7,5},{8,10},{9,11},{10,... | collective-permute-start | bytes 1572872 | tf_op jit(solution)/shard_map/ppermute | solution.py:27
  17.2 12.7 %collective-permute-start.11 = (bf16[128,1024]{1,0:T(8,128)(2,1)S(1)}, bf16[128,1024]{1,0:T(8,128)(2,1)S(1)}, u32[]{:S(2)}, u32[]{:S(2)}) collective-permute-start(bf16[128,1024]{1,0:T(8,128)(2,1)S(1)} %get-tuple-element.51), channel_id=1, source_target_pairs={{0,4},{4,0},{8,12},{12,8},{16,20},{20,16},{24,28},{28,24},{1,5},{5... | collective-permute-start | bytes 786440 | tf_op jit(solution)/shard_map/ppermute | solution.py:27
  18.7 11.3 %collective-permute-start.8 = (bf16[1024,128]{1,0:T(8,128)(2,1)S(1)}, bf16[1024,128]{1,0:T(8,128)(2,1)S(1)}, u32[]{:S(2)}, u32[]{:S(2)}) collective-permute-start(bf16[1024,128]{1,0:T(8,128)(2,1)S(1)} %broadcast_select_fusion.18), channel_id=1, source_target_pairs={{0,8},{4,12},{8,0},{12,4},{16,24},{20,28},{24,16},{28,20},{1,9},{5... | collective-permute-start | bytes 786440 | tf_op jit(solution)/shard_map/ppermute | solution.py:27
  20.3 9.8 %collective-permute-start.9 = (bf16[1024,128]{1,0:T(8,128)(2,1)S(1)}, bf16[1024,128]{1,0:T(8,128)(2,1)S(1)}, u32[]{:S(2)}, u32[]{:S(2)}) collective-permute-start(bf16[1024,128]{1,0:T(8,128)(2,1)S(1)} %broadcast_select_fusion.17), channel_id=1, source_target_pairs={{24,8},{28,12},{25,9},{29,13},{26,10},{30,14},{27,11},{31,15}} | collective-permute-start | bytes 786440 | tf_op jit(solution)/shard_map/ppermute | solution.py:27
  28.4 17.0 %collective-permute-start.14 = (bf16[2,1024,128]{2,1,0:T(8,128)(2,1)S(1)}, bf16[2,1024,128]{2,1,0:T(8,128)(2,1)S(1)}, u32[]{:S(2)}, u32[]{:S(2)}) collective-permute-start(bf16[2,1024,128]{2,1,0:T(8,128)(2,1)S(1)} %broadcast_select_fusion.7), channel_id=1, source_target_pairs={{0,4},{4,0},{8,12},{12,8},{16,20},{20,16},{24,28},{28,24},{1,5},{5... | collective-permute-start | bytes 1572872 | tf_op jit(solution)/shard_map/ppermute | solution.py:27
  29.9 16.9 %collective-permute-start.2 = (bf16[2,1024,128]{2,1,0:T(8,128)(2,1)S(1)}, bf16[2,1024,128]{2,1,0:T(8,128)(2,1)S(1)}, u32[]{:S(2)}, u32[]{:S(2)}) collective-permute-start(bf16[2,1024,128]{2,1,0:T(8,128)(2,1)S(1)} %get-tuple-element.38), channel_id=1, source_target_pairs={{0,1},{1,0},{2,3},{3,2},{4,5},{5,4},{6,7},{7,6},{8,9},{9,8},{10,11... | collective-permute-start | bytes 1572872 | tf_op jit(solution)/shard_map/ppermute | solution.py:27
  30.1 16.8 %collective-permute-start.10 = (bf16[128,1024]{1,0:T(8,128)(2,1)S(1)}, bf16[128,1024]{1,0:T(8,128)(2,1)S(1)}, u32[]{:S(2)}, u32[]{:S(2)}) collective-permute-start(bf16[128,1024]{1,0:T(8,128)(2,1)S(1)} %broadcast_select_fusion.19), channel_id=1, source_target_pairs={{24,8},{28,12},{25,9},{29,13},{26,10},{30,14},{27,11},{31,15}} | collective-permute-start | bytes 786440 | tf_op jit(solution)/shard_map/ppermute | solution.py:27
  30.8 17.6 %collective-permute-start.20 = (bf16[128,1024]{1,0:T(8,128)(2,1)S(1)}, bf16[128,1024]{1,0:T(8,128)(2,1)S(1)}, u32[]{:S(2)}, u32[]{:S(2)}) collective-permute-start(bf16[128,1024]{1,0:T(8,128)(2,1)S(1)} %broadcast_select_fusion.13), channel_id=1, source_target_pairs={{0,8},{4,12},{8,0},{12,4},{16,24},{20,28},{24,16},{28,20},{1,9},{5... | collective-permute-start | bytes 786440 | tf_op jit(solution)/shard_map/ppermute | solution.py:27
  41.9 15.7 %collective-permute-start.12 = (bf16[1024,128]{1,0:T(8,128)(2,1)S(1)}, bf16[1024,128]{1,0:T(8,128)(2,1)S(1)}, u32[]{:S(2)}, u32[]{:S(2)}) collective-permute-start(bf16[1024,128]{1,0:T(8,128)(2,1)S(1)} %broadcast_select_fusion.16), channel_id=1, source_target_pairs={{0,16},{4,20},{8,24},{12,28},{16,0},{20,4},{24,8},{28,12},{1,17},{... | collective-permute-start | bytes 786440 | tf_op jit(solution)/shard_map/ppermute | solution.py:27
  45.4 12.4 %collective-permute-start.13 = (bf16[1024,128]{1,0:T(8,128)(2,1)S(1)}, bf16[1024,128]{1,0:T(8,128)(2,1)S(1)}, u32[]{:S(2)}, u32[]{:S(2)}) collective-permute-start(bf16[1024,128]{1,0:T(8,128)(2,1)S(1)} %broadcast_select_fusion.15), channel_id=1, source_target_pairs={{8,0},{12,4},{24,16},{28,20},{9,1},{13,5},{25,17},{29,21},{10,2},{... | collective-permute-start | bytes 786440 | tf_op jit(solution)/shard_map/ppermute | solution.py:27
  46.8 14.7 %collective-permute-start.15 = (bf16[4,1024,128]{2,1,0:T(8,128)(2,1)S(1)}, bf16[4,1024,128]{2,1,0:T(8,128)(2,1)S(1)}, u32[]{:S(2)}, u32[]{:S(2)}) collective-permute-start(bf16[4,1024,128]{2,1,0:T(8,128)(2,1)S(1)} %pad_maximum_fusion), channel_id=1, source_target_pairs={{0,1},{1,0},{2,3},{3,2},{4,5},{5,4},{6,7},{7,6},{8,9},{9,8},{10,11... | collective-permute-start | bytes 3145736 | tf_op jit(solution)/shard_map/ppermute | solution.py:27
  47.0 14.4 %collective-permute-start.3 = (bf16[2,1024,128]{2,1,0:T(8,128)(2,1)S(1)}, bf16[2,1024,128]{2,1,0:T(8,128)(2,1)S(1)}, u32[]{:S(2)}, u32[]{:S(2)}) collective-permute-start(bf16[2,1024,128]{2,1,0:T(8,128)(2,1)S(1)} %broadcast_select_fusion.4), channel_id=1, source_target_pairs={{0,2},{1,3},{2,0},{3,1},{4,6},{5,7},{6,4},{7,5},{8,10},{9,11},{10,... | collective-permute-start | bytes 1572872 | tf_op jit(solution)/shard_map/ppermute | solution.py:27
  61.4 31.3 %collective-permute-start.4 = (bf16[2,1024,128]{2,1,0:T(8,128)(2,1)S(1)}, bf16[2,1024,128]{2,1,0:T(8,128)(2,1)S(1)}, u32[]{:S(2)}, u32[]{:S(2)}) collective-permute-start(bf16[2,1024,128]{2,1,0:T(8,128)(2,1)S(1)} %broadcast_select_fusion.6), channel_id=1, source_target_pairs={{0,1},{1,0},{2,3},{3,2},{4,5},{5,4},{6,7},{7,6},{8,9},{9,8},{10,11... | collective-permute-start | bytes 1572872 | tf_op jit(solution)/shard_map/ppermute | solution.py:27
  63.0 8.9 %collective-permute-start.19 = (bf16[2,128,128]{2,1,0:T(8,128)(2,1)S(1)}, bf16[2,128,128]{2,1,0:T(8,128)(2,1)S(1)}, u32[]{:S(2)}, u32[]{:S(2)}) collective-permute-start(bf16[2,128,128]{2,1,0:T(8,128)(2,1)S(1)} %get-tuple-element.55), channel_id=1, source_target_pairs={{0,24},{4,28},{8,16},{12,20},{16,8},{20,12},{24,0},{28,4},{1,25},{... | collective-permute-start | bytes 196616 | tf_op jit(solution)/shard_map/ppermute | solution.py:27
  69.0 8.2 %collective-permute-start.18 = (bf16[2,128,128]{2,1,0:T(8,128)(2,1)S(1)}, bf16[2,128,128]{2,1,0:T(8,128)(2,1)S(1)}, u32[]{:S(2)}, u32[]{:S(2)}) collective-permute-start(bf16[2,128,128]{2,1,0:T(8,128)(2,1)S(1)} %get-tuple-element.55), channel_id=1, source_target_pairs={{0,16},{4,20},{8,24},{12,28},{16,0},{20,4},{24,8},{28,12},{1,17},{... | collective-permute-start | bytes 196616 | tf_op jit(solution)/shard_map/ppermute | solution.py:27
  70.1 7.1 %collective-permute-start.17 = (bf16[2,128,128]{2,1,0:T(8,128)(2,1)S(1)}, bf16[2,128,128]{2,1,0:T(8,128)(2,1)S(1)}, u32[]{:S(2)}, u32[]{:S(2)}) collective-permute-start(bf16[2,128,128]{2,1,0:T(8,128)(2,1)S(1)} %get-tuple-element.55), channel_id=1, source_target_pairs={{0,8},{4,12},{8,0},{12,4},{16,24},{20,28},{24,16},{28,20},{1,9},{5... | collective-permute-start | bytes 196616 | tf_op jit(solution)/shard_map/ppermute | solution.py:27
  70.6 15.4 %collective-permute-start.16 = (bf16[128,1024]{1,0:T(8,128)(2,1)S(1)}, bf16[128,1024]{1,0:T(8,128)(2,1)S(1)}, u32[]{:S(2)}, u32[]{:S(2)}) collective-permute-start(bf16[128,1024]{1,0:T(8,128)(2,1)S(1)} %get-tuple-element.54), channel_id=1, source_target_pairs={{8,0},{12,4},{24,16},{28,20},{9,1},{13,5},{25,17},{29,21},{10,2},{... | collective-permute-start | bytes 786440 | tf_op jit(solution)/shard_map/ppermute | solution.py:27
  71.9 17.5 %collective-permute-start.21 = (bf16[128,1024]{1,0:T(8,128)(2,1)S(1)}, bf16[128,1024]{1,0:T(8,128)(2,1)S(1)}, u32[]{:S(2)}, u32[]{:S(2)}) collective-permute-start(bf16[128,1024]{1,0:T(8,128)(2,1)S(1)} %get-tuple-element.58), channel_id=1, source_target_pairs={{0,16},{4,20},{8,24},{12,28},{16,0},{20,4},{24,8},{28,12},{1,17},{... | collective-permute-start | bytes 786440 | tf_op jit(solution)/shard_map/ppermute | solution.py:27
  77.3 12.1 %collective-permute-start.23 = (bf16[2,384,128]{2,1,0:T(8,128)(2,1)S(1)}, bf16[2,384,128]{2,1,0:T(8,128)(2,1)S(1)}, u32[]{:S(2)}, u32[]{:S(2)}) collective-permute-start(bf16[2,384,128]{2,1,0:T(8,128)(2,1)S(1)} %get-tuple-element.104), channel_id=1, source_target_pairs={{0,4},{4,0},{8,12},{12,8},{16,20},{20,16},{24,28},{28,24},{1,5},{5... | collective-permute-start | bytes 589832 | tf_op jit(solution)/shard_map/ppermute | solution.py:27
  89.7 14.4 %collective-permute-start.22 = (bf16[2,128,1024]{2,1,0:T(8,128)(2,1)S(1)}, bf16[2,128,1024]{2,1,0:T(8,128)(2,1)S(1)}, u32[]{:S(2)}, u32[]{:S(2)}) collective-permute-start(bf16[2,128,1024]{2,1,0:T(8,128)(2,1)S(1)} %pad_maximum_fusion.1), channel_id=1, source_target_pairs={{0,4},{4,0},{8,12},{12,8},{16,20},{20,16},{24,28},{28,24},{1,5},{5... | collective-permute-start | bytes 1572872 | tf_op jit(solution)/shard_map/ppermute | solution.py:27
  (9 other events, 190.0 us)

commit v4 on v3

--- a/solution.py
+++ b/solution.py
@@ -212,8 +212,8 @@
             return lambda bit, like: flag((kind, bit), like)
 
         def lanes(fixed_keep, fixed_give, moving_keep, moving_give):
-            return (Lane(moving_keep, moving_give, "row", rows_n, same("rd")),
-                    Lane(fixed_keep, fixed_give, "row", rows_n, same("rs"), rows_n - 1))
+            lane = Lane(moving_keep, moving_give, "row", rows_n, same("rd"))
+            return lane, Lane(fixed_keep, after(fixed_give, lane.mine), "row", rows_n, same("rs"), rows_n - 1)
 
         def joined(mine, axis, n, side):
             other = swap(mine, axis, n, 1)
@@ -233,7 +233,7 @@
         for k in range(len(upper_bits(rows_n))):
             for lane in u_lanes:
                 lane.step(k, *ties)
-            ties = mines(v_lanes)
+            ties = [v_lanes[0].mine]
             follow = mines(u_lanes)
             if k == 0:
                 for m in range(len(cv.bits)):
@@ -241,6 +241,7 @@
                 ties.append(cv.mine)
                 near = swap(cv.mine, "row", rows_n, 1)
                 cu = Lane(cu_k, after(cu_g, cv.mine), "col", cols_n, same_both)
+                follow.append(near)
                 cv_first, cv_second = joined(jnp.concatenate([cv.mine, near]), "col", cols_n, "side_c")
             else:
                 follow.append(cv_first)

time: 113 us -> 114 us (level)
  waiting for transfers between devices: 48.5 us -> 55.5 us
  starting transfers between devices: 45.4 us -> 39.4 us
    ppermute x26, waiting for transfers between devices: 48.5 us -> 55.5 us  [swap(): return lax.ppermute(block, axis, [(s, s ^ bit) for s in senders])]
    ppermute x26, starting transfers between devices: 45.4 us -> 39.4 us  [swap(): return lax.ppermute(block, axis, [(s, s ^ bit) for s in senders])]
  transfers between devices with their start and end apart: 26 -> 26, of which waited for: 11 -> 12; matrix products, arithmetic and copies ran while one was open for 2% -> 1% of each run, Pallas kernels for 3% -> 3%
where the time goes in v4:
time: 114 us
  waiting for transfers between devices  55.5 us (49%)
  starting transfers between devices  39.4 us (35%)
  Pallas kernels  14.1 us (12%)
  local copies, waits for them, and re-layouts  2.72 us (2%)
  other arithmetic  1.82 us (2%)
    ppermute x26, waiting for transfers between devices, swap(): return lax.ppermute(block, axis, [(s, s ^ bit) for s in senders])  55.5 us
    ppermute x26, starting transfers between devices, swap(): return lax.ppermute(block, axis, [(s, s ^ bit) for s in senders])  39.4 us
    pallas_call x1, Pallas kernels, on_device(): pl.pallas_call(functools.partial(final_kernel, last_col=last['last_col'])...  8.57 us
    unnamed x18, local copies, waits for them, and re-layouts  2.63 us
    pallas_call x1, Pallas kernels, on_device(): pl.pallas_call(functools.partial(prep_kernel, rows_n=rows_n, cols_n=cols_...  2.42 us
  transfers between devices with their start and end apart: 26, of which 12 were waited for; matrix products, arithmetic and copies ran while one was open for 1% of the time, Pallas kernels for 3%

profile of v4, /device:TPU:0, one launch (start us, length us, event | category | flops | bytes accessed | tf_op | source)
XLA Modules:
  0.0 114.0 jit_solution(11652770711605130726)
XLA Ops:
  2.6 2.4 %shard_map.55 = (s32[23,1024]{1,0:T(8,128)S(1)}, bf16[1024,128]{1,0:T(8,128)(2,1)S(1)}, bf16[1024,128]{1,0:T(8,128)(2,1)S(1)}, bf16[1024,128]{1,0:T(8,128)(2,1)S...) custom-call(s32[2,2]{1,0:T(2,128)S(1)} %copy-done.4, ...), custom_call_target="tpu_custom_call" | custom-call | tf_op jit(solution)/shard_map/pallas_call | solution.py:194
  5.0 3.0 %collective-permute-start.5 = (bf16[1024,128]{1,0:T(8,128)(2,1)S(1)}, bf16[1024,128]{1,0:T(8,128)(2,1)S(1)}, u32[]{:S(2)}, u32[]{:S(2)}) collective-permute-start(bf16[1024,128]{1,0:T(8,128)(2,1)S(1)} %get-tuple-element.44), channel_id=1, source_target_pairs={{0,4},{4,0},{8,12},{12,8},{16,20},{20,16},{24,28},{28,24},{1,5},{5... | collective-permute-start | bytes 786440 | tf_op jit(solution)/shard_map/ppermute | solution.py:27
  8.1 6.3 %collective-permute-done.5 = bf16[1024,128]{1,0:T(8,128)(2,1)S(1)} collective-permute-done((bf16[1024,128]{1,0:T(8,128)(2,1)S(1)}, bf16[1024,128]{1,0:T(8,128)(2,1)S(1)}, u32[]{:S(2)}, u32[]{:S(2)}) %collective-permute-start.5) | collective-permute-done | bytes 262176 | tf_op jit(solution)/shard_map/ppermute | solution.py:27
  15.1 1.8 %collective-permute-start.7 = (bf16[128,1024]{1,0:T(8,128)(2,1)S(1)}, bf16[128,1024]{1,0:T(8,128)(2,1)S(1)}, u32[]{:S(2)}, u32[]{:S(2)}) collective-permute-start(bf16[128,1024]{1,0:T(8,128)(2,1)S(1)} %get-tuple-element.51), channel_id=1, source_target_pairs={{0,4},{4,0},{8,12},{12,8},{16,20},{20,16},{24,28},{28,24},{1,5},{5... | collective-permute-start | bytes 786440 | tf_op jit(solution)/shard_map/ppermute | solution.py:27
  17.0 1.6 %collective-permute-start.1 = (bf16[2,1024,128]{2,1,0:T(8,128)(2,1)S(1)}, bf16[2,1024,128]{2,1,0:T(8,128)(2,1)S(1)}, u32[]{:S(2)}, u32[]{:S(2)}) collective-permute-start(bf16[2,1024,128]{2,1,0:T(8,128)(2,1)S(1)} %broadcast_select_fusion.5), channel_id=1, source_target_pairs={{0,2},{1,3},{2,0},{3,1},{4,6},{5,7},{6,4},{7,5},{8,10},{9,11},{10,... | collective-permute-start | bytes 1572872 | tf_op jit(solution)/shard_map/ppermute | solution.py:27
  18.8 1.6 %collective-permute-start.9 = (bf16[1024,128]{1,0:T(8,128)(2,1)S(1)}, bf16[1024,128]{1,0:T(8,128)(2,1)S(1)}, u32[]{:S(2)}, u32[]{:S(2)}) collective-permute-start(bf16[1024,128]{1,0:T(8,128)(2,1)S(1)} %broadcast_select_fusion.18), channel_id=1, source_target_pairs={{0,8},{4,12},{8,0},{12,4},{16,24},{20,28},{24,16},{28,20},{1,9},{5... | collective-permute-start | bytes 786440 | tf_op jit(solution)/shard_map/ppermute | solution.py:27
  21.1 1.6 %collective-permute-done.7 = bf16[128,1024]{1,0:T(8,128)(2,1)S(1)} collective-permute-done((bf16[128,1024]{1,0:T(8,128)(2,1)S(1)}, bf16[128,1024]{1,0:T(8,128)(2,1)S(1)}, u32[]{:S(2)}, u32[]{:S(2)}) %collective-permute-start.7) | collective-permute-done | bytes 262176 | tf_op jit(solution)/shard_map/ppermute | solution.py:27
  23.4 6.2 %collective-permute-done.1 = bf16[2,1024,128]{2,1,0:T(8,128)(2,1)S(1)} collective-permute-done((bf16[2,1024,128]{2,1,0:T(8,128)(2,1)S(1)}, bf16[2,1024,128]{2,1,0:T(8,128)(2,1)S(1)}, u32[]{:S(2)}, u32[]{:S(2)}) %collective-permute-start.1) | collective-permute-done | bytes 524320 | tf_op jit(solution)/shard_map/ppermute | solution.py:27
  30.5 6.6 %collective-permute-start.13 = (bf16[1024,128]{1,0:T(8,128)(2,1)S(1)}, bf16[1024,128]{1,0:T(8,128)(2,1)S(1)}, u32[]{:S(2)}, u32[]{:S(2)}) collective-permute-start(bf16[1024,128]{1,0:T(8,128)(2,1)S(1)} %broadcast_select_fusion.15), channel_id=1, source_target_pairs={{0,16},{4,20},{8,24},{12,28},{16,0},{20,4},{24,8},{28,12},{1,17},{... | collective-permute-start | bytes 786440 | tf_op jit(solution)/shard_map/ppermute | solution.py:27
  37.1 1.3 %collective-permute-start.14 = (bf16[1024,128]{1,0:T(8,128)(2,1)S(1)}, bf16[1024,128]{1,0:T(8,128)(2,1)S(1)}, u32[]{:S(2)}, u32[]{:S(2)}) collective-permute-start(bf16[1024,128]{1,0:T(8,128)(2,1)S(1)} %broadcast_select_fusion.14), channel_id=1, source_target_pairs={{8,0},{12,4},{24,16},{28,20},{9,1},{13,5},{25,17},{29,21},{10,2},{... | collective-permute-start | bytes 786440 | tf_op jit(solution)/shard_map/ppermute | solution.py:27
  38.5 2.8 %collective-permute-done.11 = bf16[2,1024,128]{2,1,0:T(8,128)(2,1)S(1)} collective-permute-done((bf16[2,1024,128]{2,1,0:T(8,128)(2,1)S(1)}, bf16[2,1024,128]{2,1,0:T(8,128)(2,1)S(1)}, u32[]{:S(2)}, u32[]{:S(2)}) %collective-permute-start.11) | collective-permute-done | bytes 524320 | tf_op jit(solution)/shard_map/ppermute | solution.py:27
  41.6 1.6 %collective-permute-start.3 = (bf16[2,1024,128]{2,1,0:T(8,128)(2,1)S(1)}, bf16[2,1024,128]{2,1,0:T(8,128)(2,1)S(1)}, u32[]{:S(2)}, u32[]{:S(2)}) collective-permute-start(bf16[2,1024,128]{2,1,0:T(8,128)(2,1)S(1)} %broadcast_select_fusion.4), channel_id=1, source_target_pairs={{0,2},{1,3},{2,0},{3,1},{4,6},{5,7},{6,4},{7,5},{8,10},{9,11},{10,... | collective-permute-start | bytes 1572872 | tf_op jit(solution)/shard_map/ppermute | solution.py:27
  43.8 6.7 %collective-permute-done.13 = bf16[1024,128]{1,0:T(8,128)(2,1)S(1)} collective-permute-done((bf16[1024,128]{1,0:T(8,128)(2,1)S(1)}, bf16[1024,128]{1,0:T(8,128)(2,1)S(1)}, u32[]{:S(2)}, u32[]{:S(2)}) %collective-permute-start.13) | collective-permute-done | bytes 262176 | tf_op jit(solution)/shard_map/ppermute | solution.py:27
  50.5 1.3 %collective-permute-done.14 = bf16[1024,128]{1,0:T(8,128)(2,1)S(1)} collective-permute-done((bf16[1024,128]{1,0:T(8,128)(2,1)S(1)}, bf16[1024,128]{1,0:T(8,128)(2,1)S(1)}, u32[]{:S(2)}, u32[]{:S(2)}) %collective-permute-start.14) | collective-permute-done | bytes 262176 | tf_op jit(solution)/shard_map/ppermute | solution.py:27
  51.9 1.8 %shard_map.56.solved = bf16[2,1024,128]{2,1,0:T(8,128)(2,1)S(1)} custom-call(s32[2,2]{1,0:T(2,128)S(1)} %copy-done.4, bf16[2,1024,1024]{2,1,0:T(8,128)(2,1)S(1)} %copy-done, bf16[1024,128]{1,0:T(8,128)(2,1)S(1)} %broadcast_select_fusion.12.fixed, bf16[1024,128]{1,0:T(8,128)(2,1)S(1)} %broadcast_select_fusion.13.moving), custom_call_target="tpu_custom_call" | custom-call | tf_op jit(solution)/shard_map/pallas_call | solution.py:255
  53.7 5.0 %collective-permute-done.20 = bf16[128,1024]{1,0:T(8,128)(2,1)S(1)} collective-permute-done((bf16[128,1024]{1,0:T(8,128)(2,1)S(1)}, bf16[128,1024]{1,0:T(8,128)(2,1)S(1)}, u32[]{:S(2)}, u32[]{:S(2)}) %collective-permute-start.20) | collective-permute-done | bytes 262176 | tf_op jit(solution)/shard_map/ppermute | solution.py:27
  60.4 9.6 %collective-permute-start.19 = (bf16[2,128,128]{2,1,0:T(8,128)(2,1)S(1)}, bf16[2,128,128]{2,1,0:T(8,128)(2,1)S(1)}, u32[]{:S(2)}, u32[]{:S(2)}) collective-permute-start(bf16[2,128,128]{2,1,0:T(8,128)(2,1)S(1)} %get-tuple-element.59), channel_id=1, source_target_pairs={{0,24},{4,28},{8,16},{12,20},{16,8},{20,12},{24,0},{28,4},{1,25},{... | collective-permute-start | bytes 196616 | tf_op jit(solution)/shard_map/ppermute | solution.py:27
  71.6 1.3 %collective-permute-start.16 = (bf16[128,1024]{1,0:T(8,128)(2,1)S(1)}, bf16[128,1024]{1,0:T(8,128)(2,1)S(1)}, u32[]{:S(2)}, u32[]{:S(2)}) collective-permute-start(bf16[128,1024]{1,0:T(8,128)(2,1)S(1)} %get-tuple-element.58), channel_id=1, source_target_pairs={{8,0},{12,4},{24,16},{28,20},{9,1},{13,5},{25,17},{29,21},{10,2},{... | collective-permute-start | bytes 786440 | tf_op jit(solution)/shard_map/ppermute | solution.py:27
  72.9 5.3 %collective-permute-start.21 = (bf16[128,1024]{1,0:T(8,128)(2,1)S(1)}, bf16[128,1024]{1,0:T(8,128)(2,1)S(1)}, u32[]{:S(2)}, u32[]{:S(2)}) collective-permute-start(bf16[128,1024]{1,0:T(8,128)(2,1)S(1)} %get-tuple-element.62), channel_id=1, source_target_pairs={{0,16},{4,20},{8,24},{12,28},{16,0},{20,4},{24,8},{28,12},{1,17},{... | collective-permute-start | bytes 786440 | tf_op jit(solution)/shard_map/ppermute | solution.py:27
  78.4 8.6 %collective-permute-done.16 = bf16[128,1024]{1,0:T(8,128)(2,1)S(1)} collective-permute-done((bf16[128,1024]{1,0:T(8,128)(2,1)S(1)}, bf16[128,1024]{1,0:T(8,128)(2,1)S(1)}, u32[]{:S(2)}, u32[]{:S(2)}) %collective-permute-start.16) | collective-permute-done | bytes 262176 | tf_op jit(solution)/shard_map/ppermute | solution.py:27
  87.0 3.4 %collective-permute-done.21 = bf16[128,1024]{1,0:T(8,128)(2,1)S(1)} collective-permute-done((bf16[128,1024]{1,0:T(8,128)(2,1)S(1)}, bf16[128,1024]{1,0:T(8,128)(2,1)S(1)}, u32[]{:S(2)}, u32[]{:S(2)}) %collective-permute-start.21) | collective-permute-done | bytes 262176 | tf_op jit(solution)/shard_map/ppermute | solution.py:27
  92.5 5.9 %collective-permute-done.25 = bf16[640,128]{1,0:T(8,128)(2,1)S(1)} collective-permute-done((bf16[640,128]{1,0:T(8,128)(2,1)S(1)}, bf16[640,128]{1,0:T(8,128)(2,1)S(1)}, u32[]{:S(2)}, u32[]{:S(2)}) %collective-permute-start.25) | collective-permute-done | bytes 163872 | tf_op jit(solution)/shard_map/ppermute | solution.py:27
  98.6 6.5 %collective-permute-done.22 = bf16[2,128,1024]{2,1,0:T(8,128)(2,1)S(1)} collective-permute-done((bf16[2,128,1024]{2,1,0:T(8,128)(2,1)S(1)}, bf16[2,128,1024]{2,1,0:T(8,128)(2,1)S(1)}, u32[]{:S(2)}, u32[]{:S(2)}) %collective-permute-start.22) | collective-permute-done | bytes 524320 | tf_op jit(solution)/shard_map/ppermute | solution.py:27
  105.4 8.6 %shard_map.58 = bf16[2,2,1024,1024]{3,2,1,0:T(8,128)(2,1)} custom-call(s32[2,2]{1,0:T(2,128)S(1)} %copy-done.4, s32[2,2]{1,0:T(2,128)S(1)} %copy-done.6, bf16[2,2,1024,128]{3,2,1,0:T(8,128)(2,1)S(1)} %copy-done.2, bf16[2,2,128,1024]{3,2,1,0:T(8,128)(2,1)S(1)} %copy-done.3, bf16[2,1024,128]{2,1,0:T(8,128)(2,1)S(1)} %get-tuple-element.78.first, ...), custom_call_target="tpu_custom_call" | custom-call | tf_op jit(solution)/shard_map/pallas_call | solution.py:293
  (90 shorter events, 12.7 us)
Async XLA Ops:
  5.0 9.3 %collective-permute-start.5 = (bf16[1024,128]{1,0:T(8,128)(2,1)S(1)}, bf16[1024,128]{1,0:T(8,128)(2,1)S(1)}, u32[]{:S(2)}, u32[]{:S(2)}) collective-permute-start(bf16[1024,128]{1,0:T(8,128)(2,1)S(1)} %get-tuple-element.44), channel_id=1, source_target_pairs={{0,4},{4,0},{8,12},{12,8},{16,20},{20,16},{24,28},{28,24},{1,5},{5... | collective-permute-start | bytes 786440 | tf_op jit(solution)/shard_map/ppermute | solution.py:27
  8.0 8.9 %collective-permute-start = (bf16[2,1024,128]{2,1,0:T(8,128)(2,1)S(1)}, bf16[2,1024,128]{2,1,0:T(8,128)(2,1)S(1)}, u32[]{:S(2)}, u32[]{:S(2)}) collective-permute-start(bf16[2,1024,128]{2,1,0:T(8,128)(2,1)S(1)} %get-tuple-element.39), channel_id=1, source_target_pairs={{0,1},{1,0},{2,3},{3,2},{4,5},{5,4},{6,7},{7,6},{8,9},{9,8},{10,11... | collective-permute-start | bytes 1572872 | tf_op jit(solution)/shard_map/ppermute | solution.py:27
  15.1 7.6 %collective-permute-start.7 = (bf16[128,1024]{1,0:T(8,128)(2,1)S(1)}, bf16[128,1024]{1,0:T(8,128)(2,1)S(1)}, u32[]{:S(2)}, u32[]{:S(2)}) collective-permute-start(bf16[128,1024]{1,0:T(8,128)(2,1)S(1)} %get-tuple-element.51), channel_id=1, source_target_pairs={{0,4},{4,0},{8,12},{12,8},{16,20},{20,16},{24,28},{28,24},{1,5},{5... | collective-permute-start | bytes 786440 | tf_op jit(solution)/shard_map/ppermute | solution.py:27
  17.0 12.6 %collective-permute-start.1 = (bf16[2,1024,128]{2,1,0:T(8,128)(2,1)S(1)}, bf16[2,1024,128]{2,1,0:T(8,128)(2,1)S(1)}, u32[]{:S(2)}, u32[]{:S(2)}) collective-permute-start(bf16[2,1024,128]{2,1,0:T(8,128)(2,1)S(1)} %broadcast_select_fusion.5), channel_id=1, source_target_pairs={{0,2},{1,3},{2,0},{3,1},{4,6},{5,7},{6,4},{7,5},{8,10},{9,11},{10,... | collective-permute-start | bytes 1572872 | tf_op jit(solution)/shard_map/ppermute | solution.py:27
  18.8 11.6 %collective-permute-start.9 = (bf16[1024,128]{1,0:T(8,128)(2,1)S(1)}, bf16[1024,128]{1,0:T(8,128)(2,1)S(1)}, u32[]{:S(2)}, u32[]{:S(2)}) collective-permute-start(bf16[1024,128]{1,0:T(8,128)(2,1)S(1)} %broadcast_select_fusion.18), channel_id=1, source_target_pairs={{0,8},{4,12},{8,0},{12,4},{16,24},{20,28},{24,16},{28,20},{1,9},{5... | collective-permute-start | bytes 786440 | tf_op jit(solution)/shard_map/ppermute | solution.py:27
  20.4 10.0 %collective-permute-start.10 = (bf16[1024,128]{1,0:T(8,128)(2,1)S(1)}, bf16[1024,128]{1,0:T(8,128)(2,1)S(1)}, u32[]{:S(2)}, u32[]{:S(2)}) collective-permute-start(bf16[1024,128]{1,0:T(8,128)(2,1)S(1)} %broadcast_select_fusion.17), channel_id=1, source_target_pairs={{24,8},{28,12},{25,9},{29,13},{26,10},{30,14},{27,11},{31,15}} | collective-permute-start | bytes 786440 | tf_op jit(solution)/shard_map/ppermute | solution.py:27
  22.7 15.7 %collective-permute-start.8 = (bf16[128,1024]{1,0:T(8,128)(2,1)S(1)}, bf16[128,1024]{1,0:T(8,128)(2,1)S(1)}, u32[]{:S(2)}, u32[]{:S(2)}) collective-permute-start(bf16[128,1024]{1,0:T(8,128)(2,1)S(1)} %get-tuple-element.52), channel_id=1, source_target_pairs={{28,24},{29,25},{30,26},{31,27}} | collective-permute-start | bytes 786440 | tf_op jit(solution)/shard_map/ppermute | solution.py:27
  29.6 11.7 %collective-permute-start.11 = (bf16[2,1024,128]{2,1,0:T(8,128)(2,1)S(1)}, bf16[2,1024,128]{2,1,0:T(8,128)(2,1)S(1)}, u32[]{:S(2)}, u32[]{:S(2)}) collective-permute-start(bf16[2,1024,128]{2,1,0:T(8,128)(2,1)S(1)} %broadcast_select_fusion.7), channel_id=1, source_target_pairs={{0,4},{4,0},{8,12},{12,8},{16,20},{20,16},{24,28},{28,24},{1,5},{5... | collective-permute-start | bytes 1572872 | tf_op jit(solution)/shard_map/ppermute | solution.py:27
  30.4 11.1 %collective-permute-start.2 = (bf16[2,1024,128]{2,1,0:T(8,128)(2,1)S(1)}, bf16[2,1024,128]{2,1,0:T(8,128)(2,1)S(1)}, u32[]{:S(2)}, u32[]{:S(2)}) collective-permute-start(bf16[2,1024,128]{2,1,0:T(8,128)(2,1)S(1)} %get-tuple-element.40), channel_id=1, source_target_pairs={{0,1},{1,0},{2,3},{3,2},{4,5},{5,4},{6,7},{7,6},{8,9},{9,8},{10,11... | collective-permute-start | bytes 1572872 | tf_op jit(solution)/shard_map/ppermute | solution.py:27
  30.5 20.0 %collective-permute-start.13 = (bf16[1024,128]{1,0:T(8,128)(2,1)S(1)}, bf16[1024,128]{1,0:T(8,128)(2,1)S(1)}, u32[]{:S(2)}, u32[]{:S(2)}) collective-permute-start(bf16[1024,128]{1,0:T(8,128)(2,1)S(1)} %broadcast_select_fusion.15), channel_id=1, source_target_pairs={{0,16},{4,20},{8,24},{12,28},{16,0},{20,4},{24,8},{28,12},{1,17},{... | collective-permute-start | bytes 786440 | tf_op jit(solution)/shard_map/ppermute | solution.py:27
  37.1 14.7 %collective-permute-start.14 = (bf16[1024,128]{1,0:T(8,128)(2,1)S(1)}, bf16[1024,128]{1,0:T(8,128)(2,1)S(1)}, u32[]{:S(2)}, u32[]{:S(2)}) collective-permute-start(bf16[1024,128]{1,0:T(8,128)(2,1)S(1)} %broadcast_select_fusion.14), channel_id=1, source_target_pairs={{8,0},{12,4},{24,16},{28,20},{9,1},{13,5},{25,17},{29,21},{10,2},{... | collective-permute-start | bytes 786440 | tf_op jit(solution)/shard_map/ppermute | solution.py:27
  41.4 17.5 %collective-permute-start.15 = (bf16[4,1024,128]{2,1,0:T(8,128)(2,1)S(1)}, bf16[4,1024,128]{2,1,0:T(8,128)(2,1)S(1)}, u32[]{:S(2)}, u32[]{:S(2)}) collective-permute-start(bf16[4,1024,128]{2,1,0:T(8,128)(2,1)S(1)} %pad_maximum_fusion), channel_id=1, source_target_pairs={{0,1},{1,0},{2,3},{3,2},{4,5},{5,4},{6,7},{7,6},{8,9},{9,8},{10,11... | collective-permute-start | bytes 3145736 | tf_op jit(solution)/shard_map/ppermute | solution.py:27
  41.6 17.2 %collective-permute-start.3 = (bf16[2,1024,128]{2,1,0:T(8,128)(2,1)S(1)}, bf16[2,1024,128]{2,1,0:T(8,128)(2,1)S(1)}, u32[]{:S(2)}, u32[]{:S(2)}) collective-permute-start(bf16[2,1024,128]{2,1,0:T(8,128)(2,1)S(1)} %broadcast_select_fusion.4), channel_id=1, source_target_pairs={{0,2},{1,3},{2,0},{3,1},{4,6},{5,7},{6,4},{7,5},{8,10},{9,11},{10,... | collective-permute-start | bytes 1572872 | tf_op jit(solution)/shard_map/ppermute | solution.py:27
  43.1 10.5 %collective-permute-start.12 = (bf16[128,1024]{1,0:T(8,128)(2,1)S(1)}, bf16[128,1024]{1,0:T(8,128)(2,1)S(1)}, u32[]{:S(2)}, u32[]{:S(2)}) collective-permute-start(bf16[128,1024]{1,0:T(8,128)(2,1)S(1)} %broadcast_select_fusion.19), channel_id=1, source_target_pairs={{24,8},{28,12},{25,9},{29,13},{26,10},{30,14},{27,11},{31,15}} | collective-permute-start | bytes 786440 | tf_op jit(solution)/shard_map/ppermute | solution.py:27
  50.5 8.2 %collective-permute-start.20 = (bf16[128,1024]{1,0:T(8,128)(2,1)S(1)}, bf16[128,1024]{1,0:T(8,128)(2,1)S(1)}, u32[]{:S(2)}, u32[]{:S(2)}) collective-permute-start(bf16[128,1024]{1,0:T(8,128)(2,1)S(1)} %broadcast_select_fusion.16), channel_id=1, source_target_pairs={{0,8},{4,12},{8,0},{12,4},{16,24},{20,28},{24,16},{28,20},{1,9},{5... | collective-permute-start | bytes 786440 | tf_op jit(solution)/shard_map/ppermute | solution.py:27
  58.8 33.6 %collective-permute-start.4 = (bf16[2,1024,128]{2,1,0:T(8,128)(2,1)S(1)}, bf16[2,1024,128]{2,1,0:T(8,128)(2,1)S(1)}, u32[]{:S(2)}, u32[]{:S(2)}) collective-permute-start(bf16[2,1024,128]{2,1,0:T(8,128)(2,1)S(1)} %broadcast_select_fusion.6), channel_id=1, source_target_pairs={{0,1},{1,0},{2,3},{3,2},{4,5},{5,4},{6,7},{7,6},{8,9},{9,8},{10,11... | collective-permute-start | bytes 1572872 | tf_op jit(solution)/shard_map/ppermute | solution.py:27
  60.4 12.5 %collective-permute-start.19 = (bf16[2,128,128]{2,1,0:T(8,128)(2,1)S(1)}, bf16[2,128,128]{2,1,0:T(8,128)(2,1)S(1)}, u32[]{:S(2)}, u32[]{:S(2)}) collective-permute-start(bf16[2,128,128]{2,1,0:T(8,128)(2,1)S(1)} %get-tuple-element.59), channel_id=1, source_target_pairs={{0,24},{4,28},{8,16},{12,20},{16,8},{20,12},{24,0},{28,4},{1,25},{... | collective-permute-start | bytes 196616 | tf_op jit(solution)/shard_map/ppermute | solution.py:27
  70.0 8.2 %collective-permute-start.18 = (bf16[2,128,128]{2,1,0:T(8,128)(2,1)S(1)}, bf16[2,128,128]{2,1,0:T(8,128)(2,1)S(1)}, u32[]{:S(2)}, u32[]{:S(2)}) collective-permute-start(bf16[2,128,128]{2,1,0:T(8,128)(2,1)S(1)} %get-tuple-element.59), channel_id=1, source_target_pairs={{0,16},{4,20},{8,24},{12,28},{16,0},{20,4},{24,8},{28,12},{1,17},{... | collective-permute-start | bytes 196616 | tf_op jit(solution)/shard_map/ppermute | solution.py:27
  71.1 7.1 %collective-permute-start.17 = (bf16[2,128,128]{2,1,0:T(8,128)(2,1)S(1)}, bf16[2,128,128]{2,1,0:T(8,128)(2,1)S(1)}, u32[]{:S(2)}, u32[]{:S(2)}) collective-permute-start(bf16[2,128,128]{2,1,0:T(8,128)(2,1)S(1)} %get-tuple-element.59), channel_id=1, source_target_pairs={{0,8},{4,12},{8,0},{12,4},{16,24},{20,28},{24,16},{28,20},{1,9},{5... | collective-permute-start | bytes 196616 | tf_op jit(solution)/shard_map/ppermute | solution.py:27
  71.6 15.4 %collective-permute-start.16 = (bf16[128,1024]{1,0:T(8,128)(2,1)S(1)}, bf16[128,1024]{1,0:T(8,128)(2,1)S(1)}, u32[]{:S(2)}, u32[]{:S(2)}) collective-permute-start(bf16[128,1024]{1,0:T(8,128)(2,1)S(1)} %get-tuple-element.58), channel_id=1, source_target_pairs={{8,0},{12,4},{24,16},{28,20},{9,1},{13,5},{25,17},{29,21},{10,2},{... | collective-permute-start | bytes 786440 | tf_op jit(solution)/shard_map/ppermute | solution.py:27
  72.9 17.5 %collective-permute-start.21 = (bf16[128,1024]{1,0:T(8,128)(2,1)S(1)}, bf16[128,1024]{1,0:T(8,128)(2,1)S(1)}, u32[]{:S(2)}, u32[]{:S(2)}) collective-permute-start(bf16[128,1024]{1,0:T(8,128)(2,1)S(1)} %get-tuple-element.62), channel_id=1, source_target_pairs={{0,16},{4,20},{8,24},{12,28},{16,0},{20,4},{24,8},{28,12},{1,17},{... | collective-permute-start | bytes 786440 | tf_op jit(solution)/shard_map/ppermute | solution.py:27
  78.3 12.1 %collective-permute-start.23 = (bf16[2,384,128]{2,1,0:T(8,128)(2,1)S(1)}, bf16[2,384,128]{2,1,0:T(8,128)(2,1)S(1)}, u32[]{:S(2)}, u32[]{:S(2)}) collective-permute-start(bf16[2,384,128]{2,1,0:T(8,128)(2,1)S(1)} %get-tuple-element.108), channel_id=1, source_target_pairs={{0,4},{4,0},{8,12},{12,8},{16,20},{20,16},{24,28},{28,24},{1,5},{5... | collective-permute-start | bytes 589832 | tf_op jit(solution)/shard_map/ppermute | solution.py:27
  90.7 14.4 %collective-permute-start.22 = (bf16[2,128,1024]{2,1,0:T(8,128)(2,1)S(1)}, bf16[2,128,1024]{2,1,0:T(8,128)(2,1)S(1)}, u32[]{:S(2)}, u32[]{:S(2)}) collective-permute-start(bf16[2,128,1024]{2,1,0:T(8,128)(2,1)S(1)} %pad_maximum_fusion.1), channel_id=1, source_target_pairs={{0,4},{4,0},{8,12},{12,8},{16,20},{20,16},{24,28},{28,24},{1,5},{5... | collective-permute-start | bytes 1572872 | tf_op jit(solution)/shard_map/ppermute | solution.py:27
  92.1 6.3 %collective-permute-start.25 = (bf16[640,128]{1,0:T(8,128)(2,1)S(1)}, bf16[640,128]{1,0:T(8,128)(2,1)S(1)}, u32[]{:S(2)}, u32[]{:S(2)}) collective-permute-start(bf16[640,128]{1,0:T(8,128)(2,1)S(1)} %select_select_fusion), channel_id=1, source_target_pairs={{0,2},{1,3},{2,0},{3,1},{4,6},{5,7},{6,4},{7,5},{8,10},{9,11},{10,... | collective-permute-start | bytes 491528 | tf_op jit(solution)/shard_map/ppermute | solution.py:27
  (9 other events, 189.2 us)

commit v5 on v4

--- a/solution.py
+++ b/solution.py
@@ -211,9 +211,9 @@
         def same(kind):
             return lambda bit, like: flag((kind, bit), like)
 
-        def lanes(fixed_keep, fixed_give, moving_keep, moving_give):
+        def lanes(fixed_keep, fixed_give, moving_keep, moving_give, first=None):
             lane = Lane(moving_keep, moving_give, "row", rows_n, same("rd"))
-            return lane, Lane(fixed_keep, after(fixed_give, lane.mine), "row", rows_n, same("rs"), rows_n - 1)
+            return lane, Lane(fixed_keep, after(fixed_give, lane.mine if first is None else first), "row", rows_n, same("rs"), rows_n - 1)
 
         def joined(mine, axis, n, side):
             other = swap(mine, axis, n, 1)
@@ -227,18 +227,16 @@
 
         u_lanes = lanes(rs_uk, rs_ug, rd_uk, rd_ug)
         cv = Lane(cv_k, cv_g, "col", cols_n, same_both)
-        ties = mines(u_lanes)
-        v_lanes = lanes(rs_vk, after(rs_vg, *ties), rd_vk, after(rd_vg, *ties))
         ties = [cv.mine]
         for k in range(len(upper_bits(rows_n))):
             for lane in u_lanes:
                 lane.step(k, *ties)
-            ties = [v_lanes[0].mine]
+            ties = []
             follow = mines(u_lanes)
             if k == 0:
+                v_lanes = lanes(rs_vk, rs_vg, rd_vk, after(rd_vg, u_lanes[0].mine), u_lanes[0].mine)
                 for m in range(len(cv.bits)):
                     cv.step(m)
-                ties.append(cv.mine)
                 near = swap(cv.mine, "row", rows_n, 1)
                 cu = Lane(cu_k, after(cu_g, cv.mine), "col", cols_n, same_both)
                 follow.append(near)

time: 114 us -> 112 us (0.982)
  starting transfers between devices: 39.4 us -> 36.2 us
  waiting for transfers between devices: 55.5 us -> 56.7 us
    ppermute x26, starting transfers between devices: 39.4 us -> 36.2 us  [swap(): return lax.ppermute(block, axis, [(s, s ^ bit) for s in senders])]
    ppermute x26, waiting for transfers between devices: 55.5 us -> 56.7 us  [swap(): return lax.ppermute(block, axis, [(s, s ^ bit) for s in senders])]
  transfers between devices with their start and end apart: 26 -> 26, of which waited for: 12 -> 12; matrix products, arithmetic and copies ran while one was open for 1% -> 2% of each run, Pallas kernels for 3% -> 3%
where the time goes in v5:
time: 112 us
  waiting for transfers between devices  56.7 us (51%)
  starting transfers between devices  36.2 us (32%)
  Pallas kernels  14.1 us (13%)
  local copies, waits for them, and re-layouts  2.72 us (2%)
  other arithmetic  1.87 us (2%)
    ppermute x26, waiting for transfers between devices, swap(): return lax.ppermute(block, axis, [(s, s ^ bit) for s in senders])  56.7 us
    ppermute x26, starting transfers between devices, swap(): return lax.ppermute(block, axis, [(s, s ^ bit) for s in senders])  36.2 us
    pallas_call x1, Pallas kernels, on_device(): pl.pallas_call(functools.partial(final_kernel, last_col=last['last_col'])...  8.58 us
    unnamed x18, local copies, waits for them, and re-layouts  2.63 us
    pallas_call x1, Pallas kernels, on_device(): pl.pallas_call(functools.partial(prep_kernel, rows_n=rows_n, cols_n=cols_...  2.42 us
  transfers between devices with their start and end apart: 26, of which 12 were waited for; matrix products, arithmetic and copies ran while one was open for 2% of the time, Pallas kernels for 3%

profile of v5, /device:TPU:0, one launch (start us, length us, event | category | flops | bytes accessed | tf_op | source)
XLA Modules:
  0.0 112.0 jit_solution(9180385566148808516)
XLA Ops:
  2.6 2.4 %shard_map.55 = (s32[23,1024]{1,0:T(8,128)S(1)}, bf16[1024,128]{1,0:T(8,128)(2,1)S(1)}, bf16[1024,128]{1,0:T(8,128)(2,1)S(1)}, bf16[1024,128]{1,0:T(8,128)(2,1)S...) custom-call(s32[2,2]{1,0:T(2,128)S(1)} %copy-done.4, ...), custom_call_target="tpu_custom_call" | custom-call | tf_op jit(solution)/shard_map/pallas_call | solution.py:194
  5.0 3.0 %collective-permute-start.5 = (bf16[1024,128]{1,0:T(8,128)(2,1)S(1)}, bf16[1024,128]{1,0:T(8,128)(2,1)S(1)}, u32[]{:S(2)}, u32[]{:S(2)}) collective-permute-start(bf16[1024,128]{1,0:T(8,128)(2,1)S(1)} %get-tuple-element.41), channel_id=1, source_target_pairs={{0,4},{4,0},{8,12},{12,8},{16,20},{20,16},{24,28},{28,24},{1,5},{5... | collective-permute-start | bytes 786440 | tf_op jit(solution)/shard_map/ppermute | solution.py:27
  8.2 6.1 %collective-permute-done.5 = bf16[1024,128]{1,0:T(8,128)(2,1)S(1)} collective-permute-done((bf16[1024,128]{1,0:T(8,128)(2,1)S(1)}, bf16[1024,128]{1,0:T(8,128)(2,1)S(1)}, u32[]{:S(2)}, u32[]{:S(2)}) %collective-permute-start.5) | collective-permute-done | bytes 262176 | tf_op jit(solution)/shard_map/ppermute | solution.py:27
  15.1 1.8 %collective-permute-start.1 = (bf16[2,1024,128]{2,1,0:T(8,128)(2,1)S(1)}, bf16[2,1024,128]{2,1,0:T(8,128)(2,1)S(1)}, u32[]{:S(2)}, u32[]{:S(2)}) collective-permute-start(bf16[2,1024,128]{2,1,0:T(8,128)(2,1)S(1)} %broadcast_select_fusion.5), channel_id=1, source_target_pairs={{0,2},{1,3},{2,0},{3,1},{4,6},{5,7},{6,4},{7,5},{8,10},{9,11},{10,... | collective-permute-start | bytes 1572872 | tf_op jit(solution)/shard_map/ppermute | solution.py:27
  17.0 1.6 %collective-permute-start.6 = (bf16[1024,128]{1,0:T(8,128)(2,1)S(1)}, bf16[1024,128]{1,0:T(8,128)(2,1)S(1)}, u32[]{:S(2)}, u32[]{:S(2)}) collective-permute-start(bf16[1024,128]{1,0:T(8,128)(2,1)S(1)} %broadcast_select_fusion.17), channel_id=1, source_target_pairs={{0,8},{4,12},{8,0},{12,4},{16,24},{20,28},{24,16},{28,20},{1,9},{5... | collective-permute-start | bytes 786440 | tf_op jit(solution)/shard_map/ppermute | solution.py:27
  19.3 4.5 %collective-permute-done.6 = bf16[1024,128]{1,0:T(8,128)(2,1)S(1)} collective-permute-done((bf16[1024,128]{1,0:T(8,128)(2,1)S(1)}, bf16[1024,128]{1,0:T(8,128)(2,1)S(1)}, u32[]{:S(2)}, u32[]{:S(2)}) %collective-permute-start.6) | collective-permute-done | bytes 262176 | tf_op jit(solution)/shard_map/ppermute | solution.py:27
  23.9 3.1 %collective-permute-start.12 = (bf16[1024,128]{1,0:T(8,128)(2,1)S(1)}, bf16[1024,128]{1,0:T(8,128)(2,1)S(1)}, u32[]{:S(2)}, u32[]{:S(2)}) collective-permute-start(bf16[1024,128]{1,0:T(8,128)(2,1)S(1)} %broadcast_select_fusion.18), channel_id=1, source_target_pairs={{0,16},{4,20},{8,24},{12,28},{16,0},{20,4},{24,8},{28,12},{1,17},{... | collective-permute-start | bytes 786440 | tf_op jit(solution)/shard_map/ppermute | solution.py:27
  27.7 4.0 %collective-permute-start.19 = (bf16[128,1024]{1,0:T(8,128)(2,1)S(1)}, bf16[128,1024]{1,0:T(8,128)(2,1)S(1)}, u32[]{:S(2)}, u32[]{:S(2)}) collective-permute-start(bf16[128,1024]{1,0:T(8,128)(2,1)S(1)} %get-tuple-element.54), channel_id=1, source_target_pairs={{0,4},{4,0},{8,12},{12,8},{16,20},{20,16},{24,28},{28,24},{1,5},{5... | collective-permute-start | bytes 786440 | tf_op jit(solution)/shard_map/ppermute | solution.py:27
  31.9 1.3 %collective-permute-start.13 = (bf16[1024,128]{1,0:T(8,128)(2,1)S(1)}, bf16[1024,128]{1,0:T(8,128)(2,1)S(1)}, u32[]{:S(2)}, u32[]{:S(2)}) collective-permute-start(bf16[1024,128]{1,0:T(8,128)(2,1)S(1)} %broadcast_select_fusion.16), channel_id=1, source_target_pairs={{8,0},{12,4},{24,16},{28,20},{9,1},{13,5},{25,17},{29,21},{10,2},{... | collective-permute-start | bytes 786440 | tf_op jit(solution)/shard_map/ppermute | solution.py:27
  33.2 9.6 %collective-permute-done.12 = bf16[1024,128]{1,0:T(8,128)(2,1)S(1)} collective-permute-done((bf16[1024,128]{1,0:T(8,128)(2,1)S(1)}, bf16[1024,128]{1,0:T(8,128)(2,1)S(1)}, u32[]{:S(2)}, u32[]{:S(2)}) %collective-permute-start.12) | collective-permute-done | bytes 262176 | tf_op jit(solution)/shard_map/ppermute | solution.py:27
  43.0 2.3 %collective-permute-done.10 = bf16[2,1024,128]{2,1,0:T(8,128)(2,1)S(1)} collective-permute-done((bf16[2,1024,128]{2,1,0:T(8,128)(2,1)S(1)}, bf16[2,1024,128]{2,1,0:T(8,128)(2,1)S(1)}, u32[]{:S(2)}, u32[]{:S(2)}) %collective-permute-start.10) | collective-permute-done | bytes 524320 | tf_op jit(solution)/shard_map/ppermute | solution.py:27
  46.8 3.6 %collective-permute-start.20 = (bf16[128,1024]{1,0:T(8,128)(2,1)S(1)}, bf16[128,1024]{1,0:T(8,128)(2,1)S(1)}, u32[]{:S(2)}, u32[]{:S(2)}) collective-permute-start(bf16[128,1024]{1,0:T(8,128)(2,1)S(1)} %get-tuple-element.55), channel_id=1, source_target_pairs={{0,8},{4,12},{8,0},{12,4},{16,24},{20,28},{24,16},{28,20},{1,9},{5... | collective-permute-start | bytes 786440 | tf_op jit(solution)/shard_map/ppermute | solution.py:27
  50.5 1.8 %shard_map.56.solved = bf16[2,1024,128]{2,1,0:T(8,128)(2,1)S(1)} custom-call(s32[2,2]{1,0:T(2,128)S(1)} %copy-done.4, bf16[2,1024,1024]{2,1,0:T(8,128)(2,1)S(1)} %copy-done, bf16[1024,128]{1,0:T(8,128)(2,1)S(1)} %broadcast_select_fusion.13.fixed, bf16[1024,128]{1,0:T(8,128)(2,1)S(1)} %broadcast_select_fusion.14.moving), custom_call_target="tpu_custom_call" | custom-call | tf_op jit(solution)/shard_map/pallas_call | solution.py:253
  52.3 4.8 %collective-permute-done.20 = bf16[128,1024]{1,0:T(8,128)(2,1)S(1)} collective-permute-done((bf16[128,1024]{1,0:T(8,128)(2,1)S(1)}, bf16[128,1024]{1,0:T(8,128)(2,1)S(1)}, u32[]{:S(2)}, u32[]{:S(2)}) %collective-permute-start.20) | collective-permute-done | bytes 262176 | tf_op jit(solution)/shard_map/ppermute | solution.py:27
  57.1 3.5 %collective-permute-done.3 = bf16[2,1024,128]{2,1,0:T(8,128)(2,1)S(1)} collective-permute-done((bf16[2,1024,128]{2,1,0:T(8,128)(2,1)S(1)}, bf16[2,1024,128]{2,1,0:T(8,128)(2,1)S(1)}, u32[]{:S(2)}, u32[]{:S(2)}) %collective-permute-start.3) | collective-permute-done | bytes 524320 | tf_op jit(solution)/shard_map/ppermute | solution.py:27
  62.2 9.2 %collective-permute-start.18 = (bf16[2,128,128]{2,1,0:T(8,128)(2,1)S(1)}, bf16[2,128,128]{2,1,0:T(8,128)(2,1)S(1)}, u32[]{:S(2)}, u32[]{:S(2)}) collective-permute-start(bf16[2,128,128]{2,1,0:T(8,128)(2,1)S(1)} %get-tuple-element.50), channel_id=1, source_target_pairs={{0,24},{4,28},{8,16},{12,20},{16,8},{20,12},{24,0},{28,4},{1,25},{... | collective-permute-start | bytes 196616 | tf_op jit(solution)/shard_map/ppermute | solution.py:27
  72.1 1.3 %collective-permute-start.15 = (bf16[128,1024]{1,0:T(8,128)(2,1)S(1)}, bf16[128,1024]{1,0:T(8,128)(2,1)S(1)}, u32[]{:S(2)}, u32[]{:S(2)}) collective-permute-start(bf16[128,1024]{1,0:T(8,128)(2,1)S(1)} %broadcast_select_fusion.20), channel_id=1, source_target_pairs={{8,0},{12,4},{24,16},{28,20},{9,1},{13,5},{25,17},{29,21},{10,2},{... | collective-permute-start | bytes 786440 | tf_op jit(solution)/shard_map/ppermute | solution.py:27
  74.4 1.4 %collective-permute-start.21 = (bf16[128,1024]{1,0:T(8,128)(2,1)S(1)}, bf16[128,1024]{1,0:T(8,128)(2,1)S(1)}, u32[]{:S(2)}, u32[]{:S(2)}) collective-permute-start(bf16[128,1024]{1,0:T(8,128)(2,1)S(1)} %broadcast_select_fusion.11), channel_id=1, source_target_pairs={{0,16},{4,20},{8,24},{12,28},{16,0},{20,4},{24,8},{28,12},{1,17},{... | collective-permute-start | bytes 786440 | tf_op jit(solution)/shard_map/ppermute | solution.py:27
  75.7 1.3 %collective-permute-done.17 = bf16[2,128,128]{2,1,0:T(8,128)(2,1)S(1)} collective-permute-done((bf16[2,128,128]{2,1,0:T(8,128)(2,1)S(1)}, bf16[2,128,128]{2,1,0:T(8,128)(2,1)S(1)}, u32[]{:S(2)}, u32[]{:S(2)}) %collective-permute-start.17) | collective-permute-done | bytes 65568 | tf_op jit(solution)/shard_map/ppermute | solution.py:27
  77.2 11.1 %collective-permute-done.15 = bf16[128,1024]{1,0:T(8,128)(2,1)S(1)} collective-permute-done((bf16[128,1024]{1,0:T(8,128)(2,1)S(1)}, bf16[128,1024]{1,0:T(8,128)(2,1)S(1)}, u32[]{:S(2)}, u32[]{:S(2)}) %collective-permute-start.15) | collective-permute-done | bytes 262176 | tf_op jit(solution)/shard_map/ppermute | solution.py:27
  90.1 1.6 %collective-permute-start.25 = (bf16[640,128]{1,0:T(8,128)(2,1)S(1)}, bf16[640,128]{1,0:T(8,128)(2,1)S(1)}, u32[]{:S(2)}, u32[]{:S(2)}) collective-permute-start(bf16[640,128]{1,0:T(8,128)(2,1)S(1)} %select_select_fusion), channel_id=1, source_target_pairs={{0,2},{1,3},{2,0},{3,1},{4,6},{5,7},{6,4},{7,5},{8,10},{9,11},{10,... | collective-permute-start | bytes 491528 | tf_op jit(solution)/shard_map/ppermute | solution.py:27
  91.8 4.6 %collective-permute-done.25 = bf16[640,128]{1,0:T(8,128)(2,1)S(1)} collective-permute-done((bf16[640,128]{1,0:T(8,128)(2,1)S(1)}, bf16[640,128]{1,0:T(8,128)(2,1)S(1)}, u32[]{:S(2)}, u32[]{:S(2)}) %collective-permute-start.25) | collective-permute-done | bytes 163872 | tf_op jit(solution)/shard_map/ppermute | solution.py:27
  96.6 6.5 %collective-permute-done.22 = bf16[2,128,1024]{2,1,0:T(8,128)(2,1)S(1)} collective-permute-done((bf16[2,128,1024]{2,1,0:T(8,128)(2,1)S(1)}, bf16[2,128,1024]{2,1,0:T(8,128)(2,1)S(1)}, u32[]{:S(2)}, u32[]{:S(2)}) %collective-permute-start.22) | collective-permute-done | bytes 524320 | tf_op jit(solution)/shard_map/ppermute | solution.py:27
  103.4 8.6 %shard_map.58 = bf16[2,2,1024,1024]{3,2,1,0:T(8,128)(2,1)} custom-call(s32[2,2]{1,0:T(2,128)S(1)} %copy-done.4, s32[2,2]{1,0:T(2,128)S(1)} %copy-done.6, bf16[2,2,1024,128]{3,2,1,0:T(8,128)(2,1)S(1)} %copy-done.2, bf16[2,2,128,1024]{3,2,1,0:T(8,128)(2,1)S(1)} %copy-done.3, bf16[2,1024,128]{2,1,0:T(8,128)(2,1)S(1)} %get-tuple-element.72.first, ...), custom_call_target="tpu_custom_call" | custom-call | tf_op jit(solution)/shard_map/pallas_call | solution.py:291
  (90 shorter events, 12.4 us)
Async XLA Ops:
  5.0 9.3 %collective-permute-start.5 = (bf16[1024,128]{1,0:T(8,128)(2,1)S(1)}, bf16[1024,128]{1,0:T(8,128)(2,1)S(1)}, u32[]{:S(2)}, u32[]{:S(2)}) collective-permute-start(bf16[1024,128]{1,0:T(8,128)(2,1)S(1)} %get-tuple-element.41), channel_id=1, source_target_pairs={{0,4},{4,0},{8,12},{12,8},{16,20},{20,16},{24,28},{28,24},{1,5},{5... | collective-permute-start | bytes 786440 | tf_op jit(solution)/shard_map/ppermute | solution.py:27
  8.0 7.0 %collective-permute-start = (bf16[2,1024,128]{2,1,0:T(8,128)(2,1)S(1)}, bf16[2,1024,128]{2,1,0:T(8,128)(2,1)S(1)}, u32[]{:S(2)}, u32[]{:S(2)}) collective-permute-start(bf16[2,1024,128]{2,1,0:T(8,128)(2,1)S(1)} %get-tuple-element.36), channel_id=1, source_target_pairs={{0,1},{1,0},{2,3},{3,2},{4,5},{5,4},{6,7},{7,6},{8,9},{9,8},{10,11... | collective-permute-start | bytes 1572872 | tf_op jit(solution)/shard_map/ppermute | solution.py:27
  14.4 4.2 %collective-permute-start.8 = (bf16[1024,128]{1,0:T(8,128)(2,1)S(1)}, bf16[1024,128]{1,0:T(8,128)(2,1)S(1)}, u32[]{:S(2)}, u32[]{:S(2)}) collective-permute-start(bf16[1024,128]{1,0:T(8,128)(2,1)S(1)} %get-tuple-element.46), channel_id=1, source_target_pairs={{28,24},{29,25},{30,26},{31,27}} | collective-permute-start | bytes 786440 | tf_op jit(solution)/shard_map/ppermute | solution.py:27
  15.1 16.6 %collective-permute-start.1 = (bf16[2,1024,128]{2,1,0:T(8,128)(2,1)S(1)}, bf16[2,1024,128]{2,1,0:T(8,128)(2,1)S(1)}, u32[]{:S(2)}, u32[]{:S(2)}) collective-permute-start(bf16[2,1024,128]{2,1,0:T(8,128)(2,1)S(1)} %broadcast_select_fusion.5), channel_id=1, source_target_pairs={{0,2},{1,3},{2,0},{3,1},{4,6},{5,7},{6,4},{7,5},{8,10},{9,11},{10,... | collective-permute-start | bytes 1572872 | tf_op jit(solution)/shard_map/ppermute | solution.py:27
  17.0 6.9 %collective-permute-start.6 = (bf16[1024,128]{1,0:T(8,128)(2,1)S(1)}, bf16[1024,128]{1,0:T(8,128)(2,1)S(1)}, u32[]{:S(2)}, u32[]{:S(2)}) collective-permute-start(bf16[1024,128]{1,0:T(8,128)(2,1)S(1)} %broadcast_select_fusion.17), channel_id=1, source_target_pairs={{0,8},{4,12},{8,0},{12,4},{16,24},{20,28},{24,16},{28,20},{1,9},{5... | collective-permute-start | bytes 786440 | tf_op jit(solution)/shard_map/ppermute | solution.py:27
  18.6 13.2 %collective-permute-start.9 = (bf16[1024,128]{1,0:T(8,128)(2,1)S(1)}, bf16[1024,128]{1,0:T(8,128)(2,1)S(1)}, u32[]{:S(2)}, u32[]{:S(2)}) collective-permute-start(bf16[1024,128]{1,0:T(8,128)(2,1)S(1)} %broadcast_select_fusion.15), channel_id=1, source_target_pairs={{24,8},{28,12},{25,9},{29,13},{26,10},{30,14},{27,11},{31,15}} | collective-permute-start | bytes 786440 | tf_op jit(solution)/shard_map/ppermute | solution.py:27
  23.9 19.0 %collective-permute-start.12 = (bf16[1024,128]{1,0:T(8,128)(2,1)S(1)}, bf16[1024,128]{1,0:T(8,128)(2,1)S(1)}, u32[]{:S(2)}, u32[]{:S(2)}) collective-permute-start(bf16[1024,128]{1,0:T(8,128)(2,1)S(1)} %broadcast_select_fusion.18), channel_id=1, source_target_pairs={{0,16},{4,20},{8,24},{12,28},{16,0},{20,4},{24,8},{28,12},{1,17},{... | collective-permute-start | bytes 786440 | tf_op jit(solution)/shard_map/ppermute | solution.py:27
  27.0 15.9 %collective-permute-start.7 = (bf16[128,1024]{1,0:T(8,128)(2,1)S(1)}, bf16[128,1024]{1,0:T(8,128)(2,1)S(1)}, u32[]{:S(2)}, u32[]{:S(2)}) collective-permute-start(bf16[128,1024]{1,0:T(8,128)(2,1)S(1)} %get-tuple-element.43), channel_id=1, source_target_pairs={{28,24},{29,25},{30,26},{31,27}} | collective-permute-start | bytes 786440 | tf_op jit(solution)/shard_map/ppermute | solution.py:27
  27.7 15.2 %collective-permute-start.19 = (bf16[128,1024]{1,0:T(8,128)(2,1)S(1)}, bf16[128,1024]{1,0:T(8,128)(2,1)S(1)}, u32[]{:S(2)}, u32[]{:S(2)}) collective-permute-start(bf16[128,1024]{1,0:T(8,128)(2,1)S(1)} %get-tuple-element.54), channel_id=1, source_target_pairs={{0,4},{4,0},{8,12},{12,8},{16,20},{20,16},{24,28},{28,24},{1,5},{5... | collective-permute-start | bytes 786440 | tf_op jit(solution)/shard_map/ppermute | solution.py:27
  31.8 13.5 %collective-permute-start.10 = (bf16[2,1024,128]{2,1,0:T(8,128)(2,1)S(1)}, bf16[2,1024,128]{2,1,0:T(8,128)(2,1)S(1)}, u32[]{:S(2)}, u32[]{:S(2)}) collective-permute-start(bf16[2,1024,128]{2,1,0:T(8,128)(2,1)S(1)} %broadcast_select_fusion.7), channel_id=1, source_target_pairs={{0,4},{4,0},{8,12},{12,8},{16,20},{20,16},{24,28},{28,24},{1,5},{5... | collective-permute-start | bytes 1572872 | tf_op jit(solution)/shard_map/ppermute | solution.py:27
  31.9 18.5 %collective-permute-start.13 = (bf16[1024,128]{1,0:T(8,128)(2,1)S(1)}, bf16[1024,128]{1,0:T(8,128)(2,1)S(1)}, u32[]{:S(2)}, u32[]{:S(2)}) collective-permute-start(bf16[1024,128]{1,0:T(8,128)(2,1)S(1)} %broadcast_select_fusion.16), channel_id=1, source_target_pairs={{8,0},{12,4},{24,16},{28,20},{9,1},{13,5},{25,17},{29,21},{10,2},{... | collective-permute-start | bytes 786440 | tf_op jit(solution)/shard_map/ppermute | solution.py:27
  45.3 7.0 %collective-permute-start.11 = (bf16[128,1024]{1,0:T(8,128)(2,1)S(1)}, bf16[128,1024]{1,0:T(8,128)(2,1)S(1)}, u32[]{:S(2)}, u32[]{:S(2)}) collective-permute-start(bf16[128,1024]{1,0:T(8,128)(2,1)S(1)} %get-tuple-element.48), channel_id=1, source_target_pairs={{24,8},{28,12},{25,9},{29,13},{26,10},{30,14},{27,11},{31,15}} | collective-permute-start | bytes 786440 | tf_op jit(solution)/shard_map/ppermute | solution.py:27
  46.1 14.7 %collective-permute-start.14 = (bf16[4,1024,128]{2,1,0:T(8,128)(2,1)S(1)}, bf16[4,1024,128]{2,1,0:T(8,128)(2,1)S(1)}, u32[]{:S(2)}, u32[]{:S(2)}) collective-permute-start(bf16[4,1024,128]{2,1,0:T(8,128)(2,1)S(1)} %pad_maximum_fusion), channel_id=1, source_target_pairs={{0,1},{1,0},{2,3},{3,2},{4,5},{5,4},{6,7},{7,6},{8,9},{9,8},{10,11... | collective-permute-start | bytes 3145736 | tf_op jit(solution)/shard_map/ppermute | solution.py:27
  46.2 14.4 %collective-permute-start.3 = (bf16[2,1024,128]{2,1,0:T(8,128)(2,1)S(1)}, bf16[2,1024,128]{2,1,0:T(8,128)(2,1)S(1)}, u32[]{:S(2)}, u32[]{:S(2)}) collective-permute-start(bf16[2,1024,128]{2,1,0:T(8,128)(2,1)S(1)} %broadcast_select_fusion.4), channel_id=1, source_target_pairs={{0,2},{1,3},{2,0},{3,1},{4,6},{5,7},{6,4},{7,5},{8,10},{9,11},{10,... | collective-permute-start | bytes 1572872 | tf_op jit(solution)/shard_map/ppermute | solution.py:27
  46.8 10.3 %collective-permute-start.20 = (bf16[128,1024]{1,0:T(8,128)(2,1)S(1)}, bf16[128,1024]{1,0:T(8,128)(2,1)S(1)}, u32[]{:S(2)}, u32[]{:S(2)}) collective-permute-start(bf16[128,1024]{1,0:T(8,128)(2,1)S(1)} %get-tuple-element.55), channel_id=1, source_target_pairs={{0,8},{4,12},{8,0},{12,4},{16,24},{20,28},{24,16},{28,20},{1,9},{5... | collective-permute-start | bytes 786440 | tf_op jit(solution)/shard_map/ppermute | solution.py:27
  60.7 31.0 %collective-permute-start.4 = (bf16[2,1024,128]{2,1,0:T(8,128)(2,1)S(1)}, bf16[2,1024,128]{2,1,0:T(8,128)(2,1)S(1)}, u32[]{:S(2)}, u32[]{:S(2)}) collective-permute-start(bf16[2,1024,128]{2,1,0:T(8,128)(2,1)S(1)} %broadcast_select_fusion.6), channel_id=1, source_target_pairs={{0,1},{1,0},{2,3},{3,2},{4,5},{5,4},{6,7},{7,6},{8,9},{9,8},{10,11... | collective-permute-start | bytes 1572872 | tf_op jit(solution)/shard_map/ppermute | solution.py:27
  62.2 12.1 %collective-permute-start.18 = (bf16[2,128,128]{2,1,0:T(8,128)(2,1)S(1)}, bf16[2,128,128]{2,1,0:T(8,128)(2,1)S(1)}, u32[]{:S(2)}, u32[]{:S(2)}) collective-permute-start(bf16[2,128,128]{2,1,0:T(8,128)(2,1)S(1)} %get-tuple-element.50), channel_id=1, source_target_pairs={{0,24},{4,28},{8,16},{12,20},{16,8},{20,12},{24,0},{28,4},{1,25},{... | collective-permute-start | bytes 196616 | tf_op jit(solution)/shard_map/ppermute | solution.py:27
  71.4 5.7 %collective-permute-start.17 = (bf16[2,128,128]{2,1,0:T(8,128)(2,1)S(1)}, bf16[2,128,128]{2,1,0:T(8,128)(2,1)S(1)}, u32[]{:S(2)}, u32[]{:S(2)}) collective-permute-start(bf16[2,128,128]{2,1,0:T(8,128)(2,1)S(1)} %get-tuple-element.50), channel_id=1, source_target_pairs={{0,16},{4,20},{8,24},{12,28},{16,0},{20,4},{24,8},{28,12},{1,17},{... | collective-permute-start | bytes 196616 | tf_op jit(solution)/shard_map/ppermute | solution.py:27
  71.4 5.7 %collective-permute-start.16 = (bf16[2,128,128]{2,1,0:T(8,128)(2,1)S(1)}, bf16[2,128,128]{2,1,0:T(8,128)(2,1)S(1)}, u32[]{:S(2)}, u32[]{:S(2)}) collective-permute-start(bf16[2,128,128]{2,1,0:T(8,128)(2,1)S(1)} %get-tuple-element.50), channel_id=1, source_target_pairs={{0,8},{4,12},{8,0},{12,4},{16,24},{20,28},{24,16},{28,20},{1,9},{5... | collective-permute-start | bytes 196616 | tf_op jit(solution)/shard_map/ppermute | solution.py:27
  72.1 16.3 %collective-permute-start.15 = (bf16[128,1024]{1,0:T(8,128)(2,1)S(1)}, bf16[128,1024]{1,0:T(8,128)(2,1)S(1)}, u32[]{:S(2)}, u32[]{:S(2)}) collective-permute-start(bf16[128,1024]{1,0:T(8,128)(2,1)S(1)} %broadcast_select_fusion.20), channel_id=1, source_target_pairs={{8,0},{12,4},{24,16},{28,20},{9,1},{13,5},{25,17},{29,21},{10,2},{... | collective-permute-start | bytes 786440 | tf_op jit(solution)/shard_map/ppermute | solution.py:27
  74.4 14.0 %collective-permute-start.21 = (bf16[128,1024]{1,0:T(8,128)(2,1)S(1)}, bf16[128,1024]{1,0:T(8,128)(2,1)S(1)}, u32[]{:S(2)}, u32[]{:S(2)}) collective-permute-start(bf16[128,1024]{1,0:T(8,128)(2,1)S(1)} %broadcast_select_fusion.11), channel_id=1, source_target_pairs={{0,16},{4,20},{8,24},{12,28},{16,0},{20,4},{24,8},{28,12},{1,17},{... | collective-permute-start | bytes 786440 | tf_op jit(solution)/shard_map/ppermute | solution.py:27
  77.2 11.3 %collective-permute-start.23 = (bf16[2,384,128]{2,1,0:T(8,128)(2,1)S(1)}, bf16[2,384,128]{2,1,0:T(8,128)(2,1)S(1)}, u32[]{:S(2)}, u32[]{:S(2)}) collective-permute-start(bf16[2,384,128]{2,1,0:T(8,128)(2,1)S(1)} %get-tuple-element.102), channel_id=1, source_target_pairs={{0,4},{4,0},{8,12},{12,8},{16,20},{20,16},{24,28},{28,24},{1,5},{5... | collective-permute-start | bytes 589832 | tf_op jit(solution)/shard_map/ppermute | solution.py:27
  88.7 14.4 %collective-permute-start.22 = (bf16[2,128,1024]{2,1,0:T(8,128)(2,1)S(1)}, bf16[2,128,1024]{2,1,0:T(8,128)(2,1)S(1)}, u32[]{:S(2)}, u32[]{:S(2)}) collective-permute-start(bf16[2,128,1024]{2,1,0:T(8,128)(2,1)S(1)} %pad_maximum_fusion.1), channel_id=1, source_target_pairs={{0,4},{4,0},{8,12},{12,8},{16,20},{20,16},{24,28},{28,24},{1,5},{5... | collective-permute-start | bytes 1572872 | tf_op jit(solution)/shard_map/ppermute | solution.py:27
  90.1 6.3 %collective-permute-start.25 = (bf16[640,128]{1,0:T(8,128)(2,1)S(1)}, bf16[640,128]{1,0:T(8,128)(2,1)S(1)}, u32[]{:S(2)}, u32[]{:S(2)}) collective-permute-start(bf16[640,128]{1,0:T(8,128)(2,1)S(1)} %select_select_fusion), channel_id=1, source_target_pairs={{0,2},{1,3},{2,0},{3,1},{4,6},{5,7},{6,4},{7,5},{8,10},{9,11},{10,... | collective-permute-start | bytes 491528 | tf_op jit(solution)/shard_map/ppermute | solution.py:27
  (9 other events, 178.8 us)

commit v6 on v5

--- a/solution.py
+++ b/solution.py
@@ -237,12 +237,9 @@
                 v_lanes = lanes(rs_vk, rs_vg, rd_vk, after(rd_vg, u_lanes[0].mine), u_lanes[0].mine)
                 for m in range(len(cv.bits)):
                     cv.step(m)
-                near = swap(cv.mine, "row", rows_n, 1)
                 cu = Lane(cu_k, after(cu_g, cv.mine), "col", cols_n, same_both)
-                follow.append(near)
+                near = swap(after(cv.mine, v_lanes[0].mine), "row", rows_n, 1)
                 cv_first, cv_second = joined(jnp.concatenate([cv.mine, near]), "col", cols_n, "side_c")
-            else:
-                follow.append(cv_first)
             for lane in v_lanes:
                 lane.step(k, *follow)
         for m in range(len(cu.bits)):

time: 112 us -> 112 us (level)
  waiting for transfers between devices: 56.7 us -> 51.7 us
  starting transfers between devices: 36.2 us -> 41.1 us
    ppermute x26, waiting for transfers between devices: 56.7 us -> 51.7 us  [swap(): return lax.ppermute(block, axis, [(s, s ^ bit) for s in senders])]
    ppermute x26, starting transfers between devices: 36.2 us -> 41.1 us  [swap(): return lax.ppermute(block, axis, [(s, s ^ bit) for s in senders])]
  transfers between devices with their start and end apart: 26 -> 26, of which waited for: 12 -> 13; matrix products, arithmetic and copies ran while one was open for 2% -> 2% of each run, Pallas kernels for 3% -> 3%
where the time goes in v6:
time: 112 us
  waiting for transfers between devices  51.7 us (46%)
  starting transfers between devices  41.1 us (37%)
  Pallas kernels  14.1 us (13%)
  local copies, waits for them, and re-layouts  2.72 us (2%)
  other arithmetic  1.88 us (2%)
    ppermute x26, waiting for transfers between devices, swap(): return lax.ppermute(block, axis, [(s, s ^ bit) for s in senders])  51.7 us
    ppermute x26, starting transfers between devices, swap(): return lax.ppermute(block, axis, [(s, s ^ bit) for s in senders])  41.1 us
    pallas_call x1, Pallas kernels, on_device(): pl.pallas_call(functools.partial(final_kernel, last_col=last['last_col'])...  8.57 us
    unnamed x18, local copies, waits for them, and re-layouts  2.63 us
    pallas_call x1, Pallas kernels, on_device(): pl.pallas_call(functools.partial(prep_kernel, rows_n=rows_n, cols_n=cols_...  2.42 us
  transfers between devices with their start and end apart: 26, of which 13 were waited for; matrix products, arithmetic and copies ran while one was open for 2% of the time, Pallas kernels for 3%

profile of v6, /device:TPU:0, one launch (start us, length us, event | category | flops | bytes accessed | tf_op | source)
XLA Modules:
  0.0 111.9 jit_solution(11739119169294326295)
XLA Ops:
  2.6 2.4 %shard_map.55 = (s32[23,1024]{1,0:T(8,128)S(1)}, bf16[1024,128]{1,0:T(8,128)(2,1)S(1)}, bf16[1024,128]{1,0:T(8,128)(2,1)S(1)}, bf16[1024,128]{1,0:T(8,128)(2,1)S...) custom-call(s32[2,2]{1,0:T(2,128)S(1)} %copy-done.4, ...), custom_call_target="tpu_custom_call" | custom-call | tf_op jit(solution)/shard_map/pallas_call | solution.py:194
  5.0 3.0 %collective-permute-start.5 = (bf16[1024,128]{1,0:T(8,128)(2,1)S(1)}, bf16[1024,128]{1,0:T(8,128)(2,1)S(1)}, u32[]{:S(2)}, u32[]{:S(2)}) collective-permute-start(bf16[1024,128]{1,0:T(8,128)(2,1)S(1)} %get-tuple-element.42), channel_id=1, source_target_pairs={{0,4},{4,0},{8,12},{12,8},{16,20},{20,16},{24,28},{28,24},{1,5},{5... | collective-permute-start | bytes 786440 | tf_op jit(solution)/shard_map/ppermute | solution.py:27
  8.2 6.1 %collective-permute-done.5 = bf16[1024,128]{1,0:T(8,128)(2,1)S(1)} collective-permute-done((bf16[1024,128]{1,0:T(8,128)(2,1)S(1)}, bf16[1024,128]{1,0:T(8,128)(2,1)S(1)}, u32[]{:S(2)}, u32[]{:S(2)}) %collective-permute-start.5) | collective-permute-done | bytes 262176 | tf_op jit(solution)/shard_map/ppermute | solution.py:27
  15.1 1.9 %collective-permute-start.6 = (bf16[1024,128]{1,0:T(8,128)(2,1)S(1)}, bf16[1024,128]{1,0:T(8,128)(2,1)S(1)}, u32[]{:S(2)}, u32[]{:S(2)}) collective-permute-start(bf16[1024,128]{1,0:T(8,128)(2,1)S(1)} %broadcast_select_fusion.17), channel_id=1, source_target_pairs={{0,8},{4,12},{8,0},{12,4},{16,24},{20,28},{24,16},{28,20},{1,9},{5... | collective-permute-start | bytes 786440 | tf_op jit(solution)/shard_map/ppermute | solution.py:27
  17.0 1.6 %collective-permute-start.1 = (bf16[2,1024,128]{2,1,0:T(8,128)(2,1)S(1)}, bf16[2,1024,128]{2,1,0:T(8,128)(2,1)S(1)}, u32[]{:S(2)}, u32[]{:S(2)}) collective-permute-start(bf16[2,1024,128]{2,1,0:T(8,128)(2,1)S(1)} %broadcast_select_fusion.5), channel_id=1, source_target_pairs={{0,2},{1,3},{2,0},{3,1},{4,6},{5,7},{6,4},{7,5},{8,10},{9,11},{10,... | collective-permute-start | bytes 1572872 | tf_op jit(solution)/shard_map/ppermute | solution.py:27
  19.3 3.4 %collective-permute-done.6 = bf16[1024,128]{1,0:T(8,128)(2,1)S(1)} collective-permute-done((bf16[1024,128]{1,0:T(8,128)(2,1)S(1)}, bf16[1024,128]{1,0:T(8,128)(2,1)S(1)}, u32[]{:S(2)}, u32[]{:S(2)}) %collective-permute-start.6) | collective-permute-done | bytes 262176 | tf_op jit(solution)/shard_map/ppermute | solution.py:27
  23.4 1.5 %collective-permute-start.14 = (bf16[128,1024]{1,0:T(8,128)(2,1)S(1)}, bf16[128,1024]{1,0:T(8,128)(2,1)S(1)}, u32[]{:S(2)}, u32[]{:S(2)}) collective-permute-start(bf16[128,1024]{1,0:T(8,128)(2,1)S(1)} %get-tuple-element.53), channel_id=1, source_target_pairs={{0,4},{4,0},{8,12},{12,8},{16,20},{20,16},{24,28},{28,24},{1,5},{5... | collective-permute-start | bytes 786440 | tf_op jit(solution)/shard_map/ppermute | solution.py:27
  24.9 4.3 %collective-permute-start.11 = (bf16[1024,128]{1,0:T(8,128)(2,1)S(1)}, bf16[1024,128]{1,0:T(8,128)(2,1)S(1)}, u32[]{:S(2)}, u32[]{:S(2)}) collective-permute-start(bf16[1024,128]{1,0:T(8,128)(2,1)S(1)} %broadcast_select_fusion.18), channel_id=1, source_target_pairs={{0,16},{4,20},{8,24},{12,28},{16,0},{20,4},{24,8},{28,12},{1,17},{... | collective-permute-start | bytes 786440 | tf_op jit(solution)/shard_map/ppermute | solution.py:27
  31.4 7.2 %collective-permute-start.20 = (bf16[128,1024]{1,0:T(8,128)(2,1)S(1)}, bf16[128,1024]{1,0:T(8,128)(2,1)S(1)}, u32[]{:S(2)}, u32[]{:S(2)}) collective-permute-start(bf16[128,1024]{1,0:T(8,128)(2,1)S(1)} %get-tuple-element.57), channel_id=1, source_target_pairs={{0,8},{4,12},{8,0},{12,4},{16,24},{20,28},{24,16},{28,20},{1,9},{5... | collective-permute-start | bytes 786440 | tf_op jit(solution)/shard_map/ppermute | solution.py:27
  38.8 7.7 %collective-permute-done.11 = bf16[1024,128]{1,0:T(8,128)(2,1)S(1)} collective-permute-done((bf16[1024,128]{1,0:T(8,128)(2,1)S(1)}, bf16[1024,128]{1,0:T(8,128)(2,1)S(1)}, u32[]{:S(2)}, u32[]{:S(2)}) %collective-permute-start.11) | collective-permute-done | bytes 262176 | tf_op jit(solution)/shard_map/ppermute | solution.py:27
  47.3 2.8 %collective-permute-done.20 = bf16[128,1024]{1,0:T(8,128)(2,1)S(1)} collective-permute-done((bf16[128,1024]{1,0:T(8,128)(2,1)S(1)}, bf16[128,1024]{1,0:T(8,128)(2,1)S(1)}, u32[]{:S(2)}, u32[]{:S(2)}) %collective-permute-start.20) | collective-permute-done | bytes 262176 | tf_op jit(solution)/shard_map/ppermute | solution.py:27
  51.5 6.2 %collective-permute-start.21 = (bf16[128,1024]{1,0:T(8,128)(2,1)S(1)}, bf16[128,1024]{1,0:T(8,128)(2,1)S(1)}, u32[]{:S(2)}, u32[]{:S(2)}) collective-permute-start(bf16[128,1024]{1,0:T(8,128)(2,1)S(1)} %broadcast_select_fusion.10), channel_id=1, source_target_pairs={{0,16},{4,20},{8,24},{12,28},{16,0},{20,4},{24,8},{28,12},{1,17},{... | collective-permute-start | bytes 786440 | tf_op jit(solution)/shard_map/ppermute | solution.py:27
  57.6 2.5 %collective-permute-done.15 = bf16[2,1024,128]{2,1,0:T(8,128)(2,1)S(1)} collective-permute-done((bf16[2,1024,128]{2,1,0:T(8,128)(2,1)S(1)}, bf16[2,1024,128]{2,1,0:T(8,128)(2,1)S(1)}, u32[]{:S(2)}, u32[]{:S(2)}) %collective-permute-start.15) | collective-permute-done | bytes 524320 | tf_op jit(solution)/shard_map/ppermute | solution.py:27
  60.4 1.6 %collective-permute-start.3 = (bf16[2,1024,128]{2,1,0:T(8,128)(2,1)S(1)}, bf16[2,1024,128]{2,1,0:T(8,128)(2,1)S(1)}, u32[]{:S(2)}, u32[]{:S(2)}) collective-permute-start(bf16[2,1024,128]{2,1,0:T(8,128)(2,1)S(1)} %broadcast_select_fusion.4), channel_id=1, source_target_pairs={{0,2},{1,3},{2,0},{3,1},{4,6},{5,7},{6,4},{7,5},{8,10},{9,11},{10,... | collective-permute-start | bytes 1572872 | tf_op jit(solution)/shard_map/ppermute | solution.py:27
  62.1 1.8 %shard_map.56.solved = bf16[2,1024,128]{2,1,0:T(8,128)(2,1)S(1)} custom-call(s32[2,2]{1,0:T(2,128)S(1)} %copy-done.4, bf16[2,1024,1024]{2,1,0:T(8,128)(2,1)S(1)} %copy-done, bf16[1024,128]{1,0:T(8,128)(2,1)S(1)} %broadcast_select_fusion.13.fixed, bf16[1024,128]{1,0:T(8,128)(2,1)S(1)} %broadcast_select_fusion.14.moving), custom_call_target="tpu_custom_call" | custom-call | tf_op jit(solution)/shard_map/pallas_call | solution.py:250
  64.1 10.7 %collective-permute-done.3 = bf16[2,1024,128]{2,1,0:T(8,128)(2,1)S(1)} collective-permute-done((bf16[2,1024,128]{2,1,0:T(8,128)(2,1)S(1)}, bf16[2,1024,128]{2,1,0:T(8,128)(2,1)S(1)}, u32[]{:S(2)}, u32[]{:S(2)}) %collective-permute-start.3) | collective-permute-done | bytes 524320 | tf_op jit(solution)/shard_map/ppermute | solution.py:27
  76.6 1.6 %collective-permute-start.18 = (bf16[2,128,128]{2,1,0:T(8,128)(2,1)S(1)}, bf16[2,128,128]{2,1,0:T(8,128)(2,1)S(1)}, u32[]{:S(2)}, u32[]{:S(2)}) collective-permute-start(bf16[2,128,128]{2,1,0:T(8,128)(2,1)S(1)} %get-tuple-element.55), channel_id=1, source_target_pairs={{0,16},{4,20},{8,24},{12,28},{16,0},{20,4},{24,8},{28,12},{1,17},{... | collective-permute-start | bytes 196616 | tf_op jit(solution)/shard_map/ppermute | solution.py:27
  78.1 2.8 %collective-permute-start.17 = (bf16[2,128,128]{2,1,0:T(8,128)(2,1)S(1)}, bf16[2,128,128]{2,1,0:T(8,128)(2,1)S(1)}, u32[]{:S(2)}, u32[]{:S(2)}) collective-permute-start(bf16[2,128,128]{2,1,0:T(8,128)(2,1)S(1)} %get-tuple-element.55), channel_id=1, source_target_pairs={{0,8},{4,12},{8,0},{12,4},{16,24},{20,28},{24,16},{28,20},{1,9},{5... | collective-permute-start | bytes 196616 | tf_op jit(solution)/shard_map/ppermute | solution.py:27
  81.0 2.4 %collective-permute-done.19 = bf16[2,128,128]{2,1,0:T(8,128)(2,1)S(1)} collective-permute-done((bf16[2,128,128]{2,1,0:T(8,128)(2,1)S(1)}, bf16[2,128,128]{2,1,0:T(8,128)(2,1)S(1)}, u32[]{:S(2)}, u32[]{:S(2)}) %collective-permute-start.19) | collective-permute-done | bytes 65568 | tf_op jit(solution)/shard_map/ppermute | solution.py:27
  85.3 1.8 %collective-permute-start.22 = (bf16[2,128,1024]{2,1,0:T(8,128)(2,1)S(1)}, bf16[2,128,1024]{2,1,0:T(8,128)(2,1)S(1)}, u32[]{:S(2)}, u32[]{:S(2)}) collective-permute-start(bf16[2,128,1024]{2,1,0:T(8,128)(2,1)S(1)} %pad_maximum_fusion.1), channel_id=1, source_target_pairs={{0,4},{4,0},{8,12},{12,8},{16,20},{20,16},{24,28},{28,24},{1,5},{5... | collective-permute-start | bytes 1572872 | tf_op jit(solution)/shard_map/ppermute | solution.py:27
  87.2 5.6 %collective-permute-done.23.swapped = bf16[2,384,128]{2,1,0:T(8,128)(2,1)S(1)} collective-permute-done((bf16[2,384,128]{2,1,0:T(8,128)(2,1)S(1)}, bf16[2,384,128]{2,1,0:T(8,128)(2,1)S(1)}, u32[]{:S(2)}, u32[]{:S(2)}) %collective-permute-start.23) | collective-permute-done | bytes 196640 | tf_op jit(solution)/shard_map/ppermute | solution.py:27
  94.4 1.6 %collective-permute-start.25 = (bf16[640,128]{1,0:T(8,128)(2,1)S(1)}, bf16[640,128]{1,0:T(8,128)(2,1)S(1)}, u32[]{:S(2)}, u32[]{:S(2)}) collective-permute-start(bf16[640,128]{1,0:T(8,128)(2,1)S(1)} %select_select_fusion), channel_id=1, source_target_pairs={{0,2},{1,3},{2,0},{3,1},{4,6},{5,7},{6,4},{7,5},{8,10},{9,11},{10,... | collective-permute-start | bytes 491528 | tf_op jit(solution)/shard_map/ppermute | solution.py:27
  96.0 6.8 %collective-permute-done.22 = bf16[2,128,1024]{2,1,0:T(8,128)(2,1)S(1)} collective-permute-done((bf16[2,128,1024]{2,1,0:T(8,128)(2,1)S(1)}, bf16[2,128,1024]{2,1,0:T(8,128)(2,1)S(1)}, u32[]{:S(2)}, u32[]{:S(2)}) %collective-permute-start.22) | collective-permute-done | bytes 524320 | tf_op jit(solution)/shard_map/ppermute | solution.py:27
  103.3 8.6 %shard_map.58 = bf16[2,2,1024,1024]{3,2,1,0:T(8,128)(2,1)} custom-call(s32[2,2]{1,0:T(2,128)S(1)} %copy-done.4, s32[2,2]{1,0:T(2,128)S(1)} %copy-done.6, bf16[2,2,1024,128]{3,2,1,0:T(8,128)(2,1)S(1)} %copy-done.2, bf16[2,2,128,1024]{3,2,1,0:T(8,128)(2,1)S(1)} %copy-done.3, bf16[2,1024,128]{2,1,0:T(8,128)(2,1)S(1)} %get-tuple-element.74.first, ...), custom_call_target="tpu_custom_call" | custom-call | tf_op jit(solution)/shard_map/pallas_call | solution.py:288
  (90 shorter events, 15.7 us)
Async XLA Ops:
  5.0 9.3 %collective-permute-start.5 = (bf16[1024,128]{1,0:T(8,128)(2,1)S(1)}, bf16[1024,128]{1,0:T(8,128)(2,1)S(1)}, u32[]{:S(2)}, u32[]{:S(2)}) collective-permute-start(bf16[1024,128]{1,0:T(8,128)(2,1)S(1)} %get-tuple-element.42), channel_id=1, source_target_pairs={{0,4},{4,0},{8,12},{12,8},{16,20},{20,16},{24,28},{28,24},{1,5},{5... | collective-permute-start | bytes 786440 | tf_op jit(solution)/shard_map/ppermute | solution.py:27
  8.0 7.0 %collective-permute-start = (bf16[2,1024,128]{2,1,0:T(8,128)(2,1)S(1)}, bf16[2,1024,128]{2,1,0:T(8,128)(2,1)S(1)}, u32[]{:S(2)}, u32[]{:S(2)}) collective-permute-start(bf16[2,1024,128]{2,1,0:T(8,128)(2,1)S(1)} %get-tuple-element.37), channel_id=1, source_target_pairs={{0,1},{1,0},{2,3},{3,2},{4,5},{5,4},{6,7},{7,6},{8,9},{9,8},{10,11... | collective-permute-start | bytes 1572872 | tf_op jit(solution)/shard_map/ppermute | solution.py:27
  15.1 7.6 %collective-permute-start.6 = (bf16[1024,128]{1,0:T(8,128)(2,1)S(1)}, bf16[1024,128]{1,0:T(8,128)(2,1)S(1)}, u32[]{:S(2)}, u32[]{:S(2)}) collective-permute-start(bf16[1024,128]{1,0:T(8,128)(2,1)S(1)} %broadcast_select_fusion.17), channel_id=1, source_target_pairs={{0,8},{4,12},{8,0},{12,4},{16,24},{20,28},{24,16},{28,20},{1,9},{5... | collective-permute-start | bytes 786440 | tf_op jit(solution)/shard_map/ppermute | solution.py:27
  17.0 21.6 %collective-permute-start.1 = (bf16[2,1024,128]{2,1,0:T(8,128)(2,1)S(1)}, bf16[2,1024,128]{2,1,0:T(8,128)(2,1)S(1)}, u32[]{:S(2)}, u32[]{:S(2)}) collective-permute-start(bf16[2,1024,128]{2,1,0:T(8,128)(2,1)S(1)} %broadcast_select_fusion.5), channel_id=1, source_target_pairs={{0,2},{1,3},{2,0},{3,1},{4,6},{5,7},{6,4},{7,5},{8,10},{9,11},{10,... | collective-permute-start | bytes 1572872 | tf_op jit(solution)/shard_map/ppermute | solution.py:27
  18.6 10.6 %collective-permute-start.9 = (bf16[1024,128]{1,0:T(8,128)(2,1)S(1)}, bf16[1024,128]{1,0:T(8,128)(2,1)S(1)}, u32[]{:S(2)}, u32[]{:S(2)}) collective-permute-start(bf16[1024,128]{1,0:T(8,128)(2,1)S(1)} %broadcast_select_fusion.15), channel_id=1, source_target_pairs={{24,8},{28,12},{25,9},{29,13},{26,10},{30,14},{27,11},{31,15}} | collective-permute-start | bytes 786440 | tf_op jit(solution)/shard_map/ppermute | solution.py:27
  22.7 7.9 %collective-permute-start.7 = (bf16[128,1024]{1,0:T(8,128)(2,1)S(1)}, bf16[128,1024]{1,0:T(8,128)(2,1)S(1)}, u32[]{:S(2)}, u32[]{:S(2)}) collective-permute-start(bf16[128,1024]{1,0:T(8,128)(2,1)S(1)} %get-tuple-element.44), channel_id=1, source_target_pairs={{28,24},{29,25},{30,26},{31,27}} | collective-permute-start | bytes 786440 | tf_op jit(solution)/shard_map/ppermute | solution.py:27
  23.4 7.2 %collective-permute-start.14 = (bf16[128,1024]{1,0:T(8,128)(2,1)S(1)}, bf16[128,1024]{1,0:T(8,128)(2,1)S(1)}, u32[]{:S(2)}, u32[]{:S(2)}) collective-permute-start(bf16[128,1024]{1,0:T(8,128)(2,1)S(1)} %get-tuple-element.53), channel_id=1, source_target_pairs={{0,4},{4,0},{8,12},{12,8},{16,20},{20,16},{24,28},{28,24},{1,5},{5... | collective-permute-start | bytes 786440 | tf_op jit(solution)/shard_map/ppermute | solution.py:27
  24.9 21.5 %collective-permute-start.11 = (bf16[1024,128]{1,0:T(8,128)(2,1)S(1)}, bf16[1024,128]{1,0:T(8,128)(2,1)S(1)}, u32[]{:S(2)}, u32[]{:S(2)}) collective-permute-start(bf16[1024,128]{1,0:T(8,128)(2,1)S(1)} %broadcast_select_fusion.18), channel_id=1, source_target_pairs={{0,16},{4,20},{8,24},{12,28},{16,0},{20,4},{24,8},{28,12},{1,17},{... | collective-permute-start | bytes 786440 | tf_op jit(solution)/shard_map/ppermute | solution.py:27
  29.3 18.0 %collective-permute-start.12 = (bf16[1024,128]{1,0:T(8,128)(2,1)S(1)}, bf16[1024,128]{1,0:T(8,128)(2,1)S(1)}, u32[]{:S(2)}, u32[]{:S(2)}) collective-permute-start(bf16[1024,128]{1,0:T(8,128)(2,1)S(1)} %broadcast_select_fusion.16), channel_id=1, source_target_pairs={{8,0},{12,4},{24,16},{28,20},{9,1},{13,5},{25,17},{29,21},{10,2},{... | collective-permute-start | bytes 786440 | tf_op jit(solution)/shard_map/ppermute | solution.py:27
  30.7 19.4 %collective-permute-start.10 = (bf16[128,1024]{1,0:T(8,128)(2,1)S(1)}, bf16[128,1024]{1,0:T(8,128)(2,1)S(1)}, u32[]{:S(2)}, u32[]{:S(2)}) collective-permute-start(bf16[128,1024]{1,0:T(8,128)(2,1)S(1)} %get-tuple-element.49), channel_id=1, source_target_pairs={{24,8},{28,12},{25,9},{29,13},{26,10},{30,14},{27,11},{31,15}} | collective-permute-start | bytes 786440 | tf_op jit(solution)/shard_map/ppermute | solution.py:27
  31.4 18.7 %collective-permute-start.20 = (bf16[128,1024]{1,0:T(8,128)(2,1)S(1)}, bf16[128,1024]{1,0:T(8,128)(2,1)S(1)}, u32[]{:S(2)}, u32[]{:S(2)}) collective-permute-start(bf16[128,1024]{1,0:T(8,128)(2,1)S(1)} %get-tuple-element.57), channel_id=1, source_target_pairs={{0,8},{4,12},{8,0},{12,4},{16,24},{20,28},{24,16},{28,20},{1,9},{5... | collective-permute-start | bytes 786440 | tf_op jit(solution)/shard_map/ppermute | solution.py:27
  38.7 21.7 %collective-permute-start.2 = (bf16[2,1024,128]{2,1,0:T(8,128)(2,1)S(1)}, bf16[2,1024,128]{2,1,0:T(8,128)(2,1)S(1)}, u32[]{:S(2)}, u32[]{:S(2)}) collective-permute-start(bf16[2,1024,128]{2,1,0:T(8,128)(2,1)S(1)} %get-tuple-element.38), channel_id=1, source_target_pairs={{0,1},{1,0},{2,3},{3,2},{4,5},{5,4},{6,7},{7,6},{8,9},{9,8},{10,11... | collective-permute-start | bytes 1572872 | tf_op jit(solution)/shard_map/ppermute | solution.py:27
  46.4 13.7 %collective-permute-start.15 = (bf16[2,1024,128]{2,1,0:T(8,128)(2,1)S(1)}, bf16[2,1024,128]{2,1,0:T(8,128)(2,1)S(1)}, u32[]{:S(2)}, u32[]{:S(2)}) collective-permute-start(bf16[2,1024,128]{2,1,0:T(8,128)(2,1)S(1)} %broadcast_select_fusion.7), channel_id=1, source_target_pairs={{0,4},{4,0},{8,12},{12,8},{16,20},{20,16},{24,28},{28,24},{1,5},{5... | collective-permute-start | bytes 1572872 | tf_op jit(solution)/shard_map/ppermute | solution.py:27
  50.2 13.9 %collective-permute-start.13 = (bf16[128,1024]{1,0:T(8,128)(2,1)S(1)}, bf16[128,1024]{1,0:T(8,128)(2,1)S(1)}, u32[]{:S(2)}, u32[]{:S(2)}) collective-permute-start(bf16[128,1024]{1,0:T(8,128)(2,1)S(1)} %broadcast_select_fusion.20), channel_id=1, source_target_pairs={{8,0},{12,4},{24,16},{28,20},{9,1},{13,5},{25,17},{29,21},{10,2},{... | collective-permute-start | bytes 786440 | tf_op jit(solution)/shard_map/ppermute | solution.py:27
  51.5 12.6 %collective-permute-start.21 = (bf16[128,1024]{1,0:T(8,128)(2,1)S(1)}, bf16[128,1024]{1,0:T(8,128)(2,1)S(1)}, u32[]{:S(2)}, u32[]{:S(2)}) collective-permute-start(bf16[128,1024]{1,0:T(8,128)(2,1)S(1)} %broadcast_select_fusion.10), channel_id=1, source_target_pairs={{0,16},{4,20},{8,24},{12,28},{16,0},{20,4},{24,8},{28,12},{1,17},{... | collective-permute-start | bytes 786440 | tf_op jit(solution)/shard_map/ppermute | solution.py:27
  60.3 14.7 %collective-permute-start.16 = (bf16[4,1024,128]{2,1,0:T(8,128)(2,1)S(1)}, bf16[4,1024,128]{2,1,0:T(8,128)(2,1)S(1)}, u32[]{:S(2)}, u32[]{:S(2)}) collective-permute-start(bf16[4,1024,128]{2,1,0:T(8,128)(2,1)S(1)} %pad_maximum_fusion), channel_id=1, source_target_pairs={{0,1},{1,0},{2,3},{3,2},{4,5},{5,4},{6,7},{7,6},{8,9},{9,8},{10,11... | collective-permute-start | bytes 3145736 | tf_op jit(solution)/shard_map/ppermute | solution.py:27
  60.4 14.4 %collective-permute-start.3 = (bf16[2,1024,128]{2,1,0:T(8,128)(2,1)S(1)}, bf16[2,1024,128]{2,1,0:T(8,128)(2,1)S(1)}, u32[]{:S(2)}, u32[]{:S(2)}) collective-permute-start(bf16[2,1024,128]{2,1,0:T(8,128)(2,1)S(1)} %broadcast_select_fusion.4), channel_id=1, source_target_pairs={{0,2},{1,3},{2,0},{3,1},{4,6},{5,7},{6,4},{7,5},{8,10},{9,11},{10,... | collective-permute-start | bytes 1572872 | tf_op jit(solution)/shard_map/ppermute | solution.py:27
  74.9 18.0 %collective-permute-start.4 = (bf16[2,1024,128]{2,1,0:T(8,128)(2,1)S(1)}, bf16[2,1024,128]{2,1,0:T(8,128)(2,1)S(1)}, u32[]{:S(2)}, u32[]{:S(2)}) collective-permute-start(bf16[2,1024,128]{2,1,0:T(8,128)(2,1)S(1)} %broadcast_select_fusion.6), channel_id=1, source_target_pairs={{0,1},{1,0},{2,3},{3,2},{4,5},{5,4},{6,7},{7,6},{8,9},{9,8},{10,11... | collective-permute-start | bytes 1572872 | tf_op jit(solution)/shard_map/ppermute | solution.py:27
  76.5 6.9 %collective-permute-start.19 = (bf16[2,128,128]{2,1,0:T(8,128)(2,1)S(1)}, bf16[2,128,128]{2,1,0:T(8,128)(2,1)S(1)}, u32[]{:S(2)}, u32[]{:S(2)}) collective-permute-start(bf16[2,128,128]{2,1,0:T(8,128)(2,1)S(1)} %get-tuple-element.55), channel_id=1, source_target_pairs={{0,24},{4,28},{8,16},{12,20},{16,8},{20,12},{24,0},{28,4},{1,25},{... | collective-permute-start | bytes 196616 | tf_op jit(solution)/shard_map/ppermute | solution.py:27
  76.6 8.3 %collective-permute-start.18 = (bf16[2,128,128]{2,1,0:T(8,128)(2,1)S(1)}, bf16[2,128,128]{2,1,0:T(8,128)(2,1)S(1)}, u32[]{:S(2)}, u32[]{:S(2)}) collective-permute-start(bf16[2,128,128]{2,1,0:T(8,128)(2,1)S(1)} %get-tuple-element.55), channel_id=1, source_target_pairs={{0,16},{4,20},{8,24},{12,28},{16,0},{20,4},{24,8},{28,12},{1,17},{... | collective-permute-start | bytes 196616 | tf_op jit(solution)/shard_map/ppermute | solution.py:27
  78.1 6.7 %collective-permute-start.17 = (bf16[2,128,128]{2,1,0:T(8,128)(2,1)S(1)}, bf16[2,128,128]{2,1,0:T(8,128)(2,1)S(1)}, u32[]{:S(2)}, u32[]{:S(2)}) collective-permute-start(bf16[2,128,128]{2,1,0:T(8,128)(2,1)S(1)} %get-tuple-element.55), channel_id=1, source_target_pairs={{0,8},{4,12},{8,0},{12,4},{16,24},{20,28},{24,16},{28,20},{1,9},{5... | collective-permute-start | bytes 196616 | tf_op jit(solution)/shard_map/ppermute | solution.py:27
  84.9 7.9 %collective-permute-start.23 = (bf16[2,384,128]{2,1,0:T(8,128)(2,1)S(1)}, bf16[2,384,128]{2,1,0:T(8,128)(2,1)S(1)}, u32[]{:S(2)}, u32[]{:S(2)}) collective-permute-start(bf16[2,384,128]{2,1,0:T(8,128)(2,1)S(1)} %get-tuple-element.104), channel_id=1, source_target_pairs={{0,4},{4,0},{8,12},{12,8},{16,20},{20,16},{24,28},{28,24},{1,5},{5... | collective-permute-start | bytes 589832 | tf_op jit(solution)/shard_map/ppermute | solution.py:27
  85.3 17.5 %collective-permute-start.22 = (bf16[2,128,1024]{2,1,0:T(8,128)(2,1)S(1)}, bf16[2,128,1024]{2,1,0:T(8,128)(2,1)S(1)}, u32[]{:S(2)}, u32[]{:S(2)}) collective-permute-start(bf16[2,128,1024]{2,1,0:T(8,128)(2,1)S(1)} %pad_maximum_fusion.1), channel_id=1, source_target_pairs={{0,4},{4,0},{8,12},{12,8},{16,20},{20,16},{24,28},{28,24},{1,5},{5... | collective-permute-start | bytes 1572872 | tf_op jit(solution)/shard_map/ppermute | solution.py:27
  94.4 8.7 %collective-permute-start.25 = (bf16[640,128]{1,0:T(8,128)(2,1)S(1)}, bf16[640,128]{1,0:T(8,128)(2,1)S(1)}, u32[]{:S(2)}, u32[]{:S(2)}) collective-permute-start(bf16[640,128]{1,0:T(8,128)(2,1)S(1)} %select_select_fusion), channel_id=1, source_target_pairs={{0,2},{1,3},{2,0},{3,1},{4,6},{5,7},{6,4},{7,5},{8,10},{9,11},{10,... | collective-permute-start | bytes 491528 | tf_op jit(solution)/shard_map/ppermute | solution.py:27
  (9 other events, 152.1 us)

commit v7 on v6

--- a/solution.py
+++ b/solution.py
@@ -244,8 +244,6 @@
                 lane.step(k, *follow)
         for m in range(len(cu.bits)):
             cu.step(m)
-        cu_first, cu_second = joined(cu.mine, "col", cols_n, "side_c")
-
         moving, fixed = mines(u_lanes)
         solved = pl.pallas_call(
             functools.partial(solve_kernel, last_row=last["last_row"]),
@@ -271,6 +269,7 @@
         else:
             for bit in bits:
                 foot = jnp.where(at_root(bit), foot, swap(foot, "row", rows_n, bit))
+        cu_first, cu_second = joined(after(cu.mine, foot), "col", cols_n, "side_c")
         swapped = swap(jnp.concatenate([cores[:, 2 * rank:], foot], axis=1), "row", rows_n, 1)
         cores = jnp.concatenate([cores[:, :2 * rank], foot], axis=1)
         edge = jnp.concatenate([choose("q2_side", cores[0, :2 * rank], swapped[0, :2 * rank]), choose("q1_side", cores[1], swapped[1])])

time: 112 us -> 103 us (0.920)
  waiting for transfers between devices: 51.7 us -> 44.1 us
  starting transfers between devices: 41.1 us -> 39.1 us
    ppermute x26, waiting for transfers between devices: 51.7 us -> 44.1 us  [swap(): return lax.ppermute(block, axis, [(s, s ^ bit) for s in senders])]
    ppermute x26, starting transfers between devices: 41.1 us -> 39.1 us  [swap(): return lax.ppermute(block, axis, [(s, s ^ bit) for s in senders])]
  transfers between devices with their start and end apart: 26 -> 26, of which waited for: 13 -> 11; matrix products, arithmetic and copies ran while one was open for 2% -> 2% of each run, Pallas kernels for 3% -> 3%
where the time goes in v7:
time: 103 us; the launch traced here: 102 us
  waiting for transfers between devices  44.1 us (43%)
  starting transfers between devices  39.1 us (38%)
  Pallas kernels  14.1 us (14%)
  local copies, waits for them, and re-layouts  2.72 us (3%)
  other arithmetic  1.88 us (2%)
    ppermute x26, waiting for transfers between devices, swap(): return lax.ppermute(block, axis, [(s, s ^ bit) for s in senders])  44.1 us
    ppermute x26, starting transfers between devices, swap(): return lax.ppermute(block, axis, [(s, s ^ bit) for s in senders])  39.1 us
    pallas_call x1, Pallas kernels, on_device(): pl.pallas_call(functools.partial(final_kernel, last_col=last['last_col'])...  8.56 us
    unnamed x18, local copies, waits for them, and re-layouts  2.63 us
    pallas_call x1, Pallas kernels, on_device(): pl.pallas_call(functools.partial(prep_kernel, rows_n=rows_n, cols_n=cols_...  2.42 us
  transfers between devices with their start and end apart: 26, of which 11 were waited for; matrix products, arithmetic and copies ran while one was open for 2% of the time, Pallas kernels for 3%

profile of v7, /device:TPU:0, one launch (start us, length us, event | category | flops | bytes accessed | tf_op | source)
XLA Modules:
  0.0 102.3 jit_solution(10566580343505579199)
XLA Ops:
  2.6 2.4 %shard_map.55 = (s32[23,1024]{1,0:T(8,128)S(1)}, bf16[1024,128]{1,0:T(8,128)(2,1)S(1)}, bf16[1024,128]{1,0:T(8,128)(2,1)S(1)}, bf16[1024,128]{1,0:T(8,128)(2,1)S...) custom-call(s32[2,2]{1,0:T(2,128)S(1)} %copy-done.4, ...), custom_call_target="tpu_custom_call" | custom-call | tf_op jit(solution)/shard_map/pallas_call | solution.py:194
  5.0 3.0 %collective-permute-start.4 = (bf16[1024,128]{1,0:T(8,128)(2,1)S(1)}, bf16[1024,128]{1,0:T(8,128)(2,1)S(1)}, u32[]{:S(2)}, u32[]{:S(2)}) collective-permute-start(bf16[1024,128]{1,0:T(8,128)(2,1)S(1)} %get-tuple-element.43), channel_id=1, source_target_pairs={{0,4},{4,0},{8,12},{12,8},{16,20},{20,16},{24,28},{28,24},{1,5},{5... | collective-permute-start | bytes 786440 | tf_op jit(solution)/shard_map/ppermute | solution.py:27
  8.2 6.1 %collective-permute-done.4 = bf16[1024,128]{1,0:T(8,128)(2,1)S(1)} collective-permute-done((bf16[1024,128]{1,0:T(8,128)(2,1)S(1)}, bf16[1024,128]{1,0:T(8,128)(2,1)S(1)}, u32[]{:S(2)}, u32[]{:S(2)}) %collective-permute-start.4) | collective-permute-done | bytes 262176 | tf_op jit(solution)/shard_map/ppermute | solution.py:27
  15.1 1.9 %collective-permute-start.8 = (bf16[1024,128]{1,0:T(8,128)(2,1)S(1)}, bf16[1024,128]{1,0:T(8,128)(2,1)S(1)}, u32[]{:S(2)}, u32[]{:S(2)}) collective-permute-start(bf16[1024,128]{1,0:T(8,128)(2,1)S(1)} %broadcast_select_fusion.18), channel_id=1, source_target_pairs={{0,8},{4,12},{8,0},{12,4},{16,24},{20,28},{24,16},{28,20},{1,9},{5... | collective-permute-start | bytes 786440 | tf_op jit(solution)/shard_map/ppermute | solution.py:27
  17.0 1.6 %collective-permute-start.1 = (bf16[2,1024,128]{2,1,0:T(8,128)(2,1)S(1)}, bf16[2,1024,128]{2,1,0:T(8,128)(2,1)S(1)}, u32[]{:S(2)}, u32[]{:S(2)}) collective-permute-start(bf16[2,1024,128]{2,1,0:T(8,128)(2,1)S(1)} %broadcast_select_fusion.5), channel_id=1, source_target_pairs={{0,2},{1,3},{2,0},{3,1},{4,6},{5,7},{6,4},{7,5},{8,10},{9,11},{10,... | collective-permute-start | bytes 1572872 | tf_op jit(solution)/shard_map/ppermute | solution.py:27
  19.3 3.4 %collective-permute-done.8 = bf16[1024,128]{1,0:T(8,128)(2,1)S(1)} collective-permute-done((bf16[1024,128]{1,0:T(8,128)(2,1)S(1)}, bf16[1024,128]{1,0:T(8,128)(2,1)S(1)}, u32[]{:S(2)}, u32[]{:S(2)}) %collective-permute-start.8) | collective-permute-done | bytes 262176 | tf_op jit(solution)/shard_map/ppermute | solution.py:27
  22.7 1.5 %collective-permute-start.10 = (bf16[128,1024]{1,0:T(8,128)(2,1)S(1)}, bf16[128,1024]{1,0:T(8,128)(2,1)S(1)}, u32[]{:S(2)}, u32[]{:S(2)}) collective-permute-start(bf16[128,1024]{1,0:T(8,128)(2,1)S(1)} %get-tuple-element.49), channel_id=1, source_target_pairs={{0,4},{4,0},{8,12},{12,8},{16,20},{20,16},{24,28},{28,24},{1,5},{5... | collective-permute-start | bytes 786440 | tf_op jit(solution)/shard_map/ppermute | solution.py:27
  24.9 4.3 %collective-permute-start.9 = (bf16[1024,128]{1,0:T(8,128)(2,1)S(1)}, bf16[1024,128]{1,0:T(8,128)(2,1)S(1)}, u32[]{:S(2)}, u32[]{:S(2)}) collective-permute-start(bf16[1024,128]{1,0:T(8,128)(2,1)S(1)} %broadcast_select_fusion.16), channel_id=1, source_target_pairs={{0,16},{4,20},{8,24},{12,28},{16,0},{20,4},{24,8},{28,12},{1,17},{... | collective-permute-start | bytes 786440 | tf_op jit(solution)/shard_map/ppermute | solution.py:27
  29.3 1.3 %collective-permute-start.7 = (bf16[1024,128]{1,0:T(8,128)(2,1)S(1)}, bf16[1024,128]{1,0:T(8,128)(2,1)S(1)}, u32[]{:S(2)}, u32[]{:S(2)}) collective-permute-start(bf16[1024,128]{1,0:T(8,128)(2,1)S(1)} %broadcast_select_fusion.20), channel_id=1, source_target_pairs={{8,0},{12,4},{24,16},{28,20},{9,1},{13,5},{25,17},{29,21},{10,2},{... | collective-permute-start | bytes 786440 | tf_op jit(solution)/shard_map/ppermute | solution.py:27
  31.2 6.9 %collective-permute-start.20 = (bf16[128,1024]{1,0:T(8,128)(2,1)S(1)}, bf16[128,1024]{1,0:T(8,128)(2,1)S(1)}, u32[]{:S(2)}, u32[]{:S(2)}) collective-permute-start(bf16[128,1024]{1,0:T(8,128)(2,1)S(1)} %get-tuple-element.59), channel_id=1, source_target_pairs={{0,8},{4,12},{8,0},{12,4},{16,24},{20,28},{24,16},{28,20},{1,9},{5... | collective-permute-start | bytes 786440 | tf_op jit(solution)/shard_map/ppermute | solution.py:27
  38.8 8.4 %collective-permute-done.7 = bf16[1024,128]{1,0:T(8,128)(2,1)S(1)} collective-permute-done((bf16[1024,128]{1,0:T(8,128)(2,1)S(1)}, bf16[1024,128]{1,0:T(8,128)(2,1)S(1)}, u32[]{:S(2)}, u32[]{:S(2)}) %collective-permute-start.7) | collective-permute-done | bytes 262176 | tf_op jit(solution)/shard_map/ppermute | solution.py:27
  47.4 1.8 %shard_map.56.solved = bf16[2,1024,128]{2,1,0:T(8,128)(2,1)S(1)} custom-call(s32[2,2]{1,0:T(2,128)S(1)} %copy-done.4, bf16[2,1024,1024]{2,1,0:T(8,128)(2,1)S(1)} %copy-done, bf16[1024,128]{1,0:T(8,128)(2,1)S(1)} %broadcast_select_fusion.21.fixed, bf16[1024,128]{1,0:T(8,128)(2,1)S(1)} %broadcast_select_fusion.17.moving), custom_call_target="tpu_custom_call" | custom-call | tf_op jit(solution)/shard_map/pallas_call | solution.py:248
  50.2 1.3 %collective-permute-start.19 = (bf16[128,1024]{1,0:T(8,128)(2,1)S(1)}, bf16[128,1024]{1,0:T(8,128)(2,1)S(1)}, u32[]{:S(2)}, u32[]{:S(2)}) collective-permute-start(bf16[128,1024]{1,0:T(8,128)(2,1)S(1)} %broadcast_select_fusion.13), channel_id=1, source_target_pairs={{8,0},{12,4},{24,16},{28,20},{9,1},{13,5},{25,17},{29,21},{10,2},{... | collective-permute-start | bytes 786440 | tf_op jit(solution)/shard_map/ppermute | solution.py:27
  51.5 3.2 %collective-permute-start.21 = (bf16[128,1024]{1,0:T(8,128)(2,1)S(1)}, bf16[128,1024]{1,0:T(8,128)(2,1)S(1)}, u32[]{:S(2)}, u32[]{:S(2)}) collective-permute-start(bf16[128,1024]{1,0:T(8,128)(2,1)S(1)} %broadcast_select_fusion.10), channel_id=1, source_target_pairs={{0,16},{4,20},{8,24},{12,28},{16,0},{20,4},{24,8},{28,12},{1,17},{... | collective-permute-start | bytes 786440 | tf_op jit(solution)/shard_map/ppermute | solution.py:27
  54.7 1.6 %collective-permute-start.3 = (bf16[2,1024,128]{2,1,0:T(8,128)(2,1)S(1)}, bf16[2,1024,128]{2,1,0:T(8,128)(2,1)S(1)}, u32[]{:S(2)}, u32[]{:S(2)}) collective-permute-start(bf16[2,1024,128]{2,1,0:T(8,128)(2,1)S(1)} %broadcast_select_fusion.4), channel_id=1, source_target_pairs={{0,2},{1,3},{2,0},{3,1},{4,6},{5,7},{6,4},{7,5},{8,10},{9,11},{10,... | collective-permute-start | bytes 1572872 | tf_op jit(solution)/shard_map/ppermute | solution.py:27
  56.3 10.2 %collective-permute-done.19 = bf16[128,1024]{1,0:T(8,128)(2,1)S(1)} collective-permute-done((bf16[128,1024]{1,0:T(8,128)(2,1)S(1)}, bf16[128,1024]{1,0:T(8,128)(2,1)S(1)}, u32[]{:S(2)}, u32[]{:S(2)}) %collective-permute-start.19) | collective-permute-done | bytes 262176 | tf_op jit(solution)/shard_map/ppermute | solution.py:27
  67.1 1.3 %shard_map.57 = (bf16[2,512,128]{2,1,0:T(8,128)(2,1)S(1)}, bf16[2,128,128]{2,1,0:T(8,128)(2,1)S(1)}) custom-call(s32[2,2]{1,0:T(2,128)S(1)} %copy-done.4, bf16[2,1024,128]{2,1,0:T(8,128)(2,1)S(1)} %shard_map.56.solved, bf16[4,1024,128]{2,1,0:T(8,128)(2,1)S(1)} %get-tuple-element.72.first, bf16[4,1024,128]{2,1,0:T(8,128)(2,1)S(1)} %get-tuple-element.71.second), custom_call_target="tpu_custom_call" | custom-call | tf_op jit(solution)/shard_map/pallas_call | solution.py:255
  68.9 1.6 %collective-permute-start.14 = (bf16[2,128,128]{2,1,0:T(8,128)(2,1)S(1)}, bf16[2,128,128]{2,1,0:T(8,128)(2,1)S(1)}, u32[]{:S(2)}, u32[]{:S(2)}) collective-permute-start(bf16[2,128,128]{2,1,0:T(8,128)(2,1)S(1)} %get-tuple-element.51), channel_id=1, source_target_pairs={{0,16},{4,20},{8,24},{12,28},{16,0},{20,4},{24,8},{28,12},{1,17},{... | collective-permute-start | bytes 196616 | tf_op jit(solution)/shard_map/ppermute | solution.py:27
  70.5 2.4 %collective-permute-start.13 = (bf16[2,128,128]{2,1,0:T(8,128)(2,1)S(1)}, bf16[2,128,128]{2,1,0:T(8,128)(2,1)S(1)}, u32[]{:S(2)}, u32[]{:S(2)}) collective-permute-start(bf16[2,128,128]{2,1,0:T(8,128)(2,1)S(1)} %get-tuple-element.51), channel_id=1, source_target_pairs={{0,8},{4,12},{8,0},{12,4},{16,24},{20,28},{24,16},{28,20},{1,9},{5... | collective-permute-start | bytes 196616 | tf_op jit(solution)/shard_map/ppermute | solution.py:27
  72.9 1.8 %collective-permute-done.15 = bf16[2,128,128]{2,1,0:T(8,128)(2,1)S(1)} collective-permute-done((bf16[2,128,128]{2,1,0:T(8,128)(2,1)S(1)}, bf16[2,128,128]{2,1,0:T(8,128)(2,1)S(1)}, u32[]{:S(2)}, u32[]{:S(2)}) %collective-permute-start.15) | collective-permute-done | bytes 65568 | tf_op jit(solution)/shard_map/ppermute | solution.py:27
  78.2 5.6 %collective-permute-done.23.swapped = bf16[2,384,128]{2,1,0:T(8,128)(2,1)S(1)} collective-permute-done((bf16[2,384,128]{2,1,0:T(8,128)(2,1)S(1)}, bf16[2,384,128]{2,1,0:T(8,128)(2,1)S(1)}, u32[]{:S(2)}, u32[]{:S(2)}) %collective-permute-start.23) | collective-permute-done | bytes 196640 | tf_op jit(solution)/shard_map/ppermute | solution.py:27
  85.5 1.6 %collective-permute-start.25 = (bf16[640,128]{1,0:T(8,128)(2,1)S(1)}, bf16[640,128]{1,0:T(8,128)(2,1)S(1)}, u32[]{:S(2)}, u32[]{:S(2)}) collective-permute-start(bf16[640,128]{1,0:T(8,128)(2,1)S(1)} %select_select_fusion), channel_id=1, source_target_pairs={{0,2},{1,3},{2,0},{3,1},{4,6},{5,7},{6,4},{7,5},{8,10},{9,11},{10,... | collective-permute-start | bytes 491528 | tf_op jit(solution)/shard_map/ppermute | solution.py:27
  87.1 6.1 %collective-permute-done.22 = bf16[2,128,1024]{2,1,0:T(8,128)(2,1)S(1)} collective-permute-done((bf16[2,128,1024]{2,1,0:T(8,128)(2,1)S(1)}, bf16[2,128,1024]{2,1,0:T(8,128)(2,1)S(1)}, u32[]{:S(2)}, u32[]{:S(2)}) %collective-permute-start.22) | collective-permute-done | bytes 524320 | tf_op jit(solution)/shard_map/ppermute | solution.py:27
  93.8 8.6 %shard_map.58 = bf16[2,2,1024,1024]{3,2,1,0:T(8,128)(2,1)} custom-call(s32[2,2]{1,0:T(2,128)S(1)} %copy-done.4, s32[2,2]{1,0:T(2,128)S(1)} %copy-done.6, bf16[2,2,1024,128]{3,2,1,0:T(8,128)(2,1)S(1)} %copy-done.2, bf16[2,2,128,1024]{3,2,1,0:T(8,128)(2,1)S(1)} %copy-done.3, bf16[2,1024,128]{2,1,0:T(8,128)(2,1)S(1)} %get-tuple-element.76.first, ...), custom_call_target="tpu_custom_call" | custom-call | tf_op jit(solution)/shard_map/pallas_call | solution.py:287
  (90 shorter events, 14.1 us)
Async XLA Ops:
  5.0 9.3 %collective-permute-start.4 = (bf16[1024,128]{1,0:T(8,128)(2,1)S(1)}, bf16[1024,128]{1,0:T(8,128)(2,1)S(1)}, u32[]{:S(2)}, u32[]{:S(2)}) collective-permute-start(bf16[1024,128]{1,0:T(8,128)(2,1)S(1)} %get-tuple-element.43), channel_id=1, source_target_pairs={{0,4},{4,0},{8,12},{12,8},{16,20},{20,16},{24,28},{28,24},{1,5},{5... | collective-permute-start | bytes 786440 | tf_op jit(solution)/shard_map/ppermute | solution.py:27
  8.0 7.0 %collective-permute-start = (bf16[2,1024,128]{2,1,0:T(8,128)(2,1)S(1)}, bf16[2,1024,128]{2,1,0:T(8,128)(2,1)S(1)}, u32[]{:S(2)}, u32[]{:S(2)}) collective-permute-start(bf16[2,1024,128]{2,1,0:T(8,128)(2,1)S(1)} %get-tuple-element.38), channel_id=1, source_target_pairs={{0,1},{1,0},{2,3},{3,2},{4,5},{5,4},{6,7},{7,6},{8,9},{9,8},{10,11... | collective-permute-start | bytes 1572872 | tf_op jit(solution)/shard_map/ppermute | solution.py:27
  15.1 7.6 %collective-permute-start.8 = (bf16[1024,128]{1,0:T(8,128)(2,1)S(1)}, bf16[1024,128]{1,0:T(8,128)(2,1)S(1)}, u32[]{:S(2)}, u32[]{:S(2)}) collective-permute-start(bf16[1024,128]{1,0:T(8,128)(2,1)S(1)} %broadcast_select_fusion.18), channel_id=1, source_target_pairs={{0,8},{4,12},{8,0},{12,4},{16,24},{20,28},{24,16},{28,20},{1,9},{5... | collective-permute-start | bytes 786440 | tf_op jit(solution)/shard_map/ppermute | solution.py:27
  17.0 13.7 %collective-permute-start.1 = (bf16[2,1024,128]{2,1,0:T(8,128)(2,1)S(1)}, bf16[2,1024,128]{2,1,0:T(8,128)(2,1)S(1)}, u32[]{:S(2)}, u32[]{:S(2)}) collective-permute-start(bf16[2,1024,128]{2,1,0:T(8,128)(2,1)S(1)} %broadcast_select_fusion.5), channel_id=1, source_target_pairs={{0,2},{1,3},{2,0},{3,1},{4,6},{5,7},{6,4},{7,5},{8,10},{9,11},{10,... | collective-permute-start | bytes 1572872 | tf_op jit(solution)/shard_map/ppermute | solution.py:27
  18.6 10.6 %collective-permute-start.6 = (bf16[1024,128]{1,0:T(8,128)(2,1)S(1)}, bf16[1024,128]{1,0:T(8,128)(2,1)S(1)}, u32[]{:S(2)}, u32[]{:S(2)}) collective-permute-start(bf16[1024,128]{1,0:T(8,128)(2,1)S(1)} %broadcast_select_fusion.19), channel_id=1, source_target_pairs={{24,8},{28,12},{25,9},{29,13},{26,10},{30,14},{27,11},{31,15}} | collective-permute-start | bytes 786440 | tf_op jit(solution)/shard_map/ppermute | solution.py:27
  22.7 7.9 %collective-permute-start.10 = (bf16[128,1024]{1,0:T(8,128)(2,1)S(1)}, bf16[128,1024]{1,0:T(8,128)(2,1)S(1)}, u32[]{:S(2)}, u32[]{:S(2)}) collective-permute-start(bf16[128,1024]{1,0:T(8,128)(2,1)S(1)} %get-tuple-element.49), channel_id=1, source_target_pairs={{0,4},{4,0},{8,12},{12,8},{16,20},{20,16},{24,28},{28,24},{1,5},{5... | collective-permute-start | bytes 786440 | tf_op jit(solution)/shard_map/ppermute | solution.py:27
  24.2 6.4 %collective-permute-start.17 = (bf16[128,1024]{1,0:T(8,128)(2,1)S(1)}, bf16[128,1024]{1,0:T(8,128)(2,1)S(1)}, u32[]{:S(2)}, u32[]{:S(2)}) collective-permute-start(bf16[128,1024]{1,0:T(8,128)(2,1)S(1)} %get-tuple-element.55), channel_id=1, source_target_pairs={{28,24},{29,25},{30,26},{31,27}} | collective-permute-start | bytes 786440 | tf_op jit(solution)/shard_map/ppermute | solution.py:27
  24.9 22.4 %collective-permute-start.9 = (bf16[1024,128]{1,0:T(8,128)(2,1)S(1)}, bf16[1024,128]{1,0:T(8,128)(2,1)S(1)}, u32[]{:S(2)}, u32[]{:S(2)}) collective-permute-start(bf16[1024,128]{1,0:T(8,128)(2,1)S(1)} %broadcast_select_fusion.16), channel_id=1, source_target_pairs={{0,16},{4,20},{8,24},{12,28},{16,0},{20,4},{24,8},{28,12},{1,17},{... | collective-permute-start | bytes 786440 | tf_op jit(solution)/shard_map/ppermute | solution.py:27
  29.3 18.0 %collective-permute-start.7 = (bf16[1024,128]{1,0:T(8,128)(2,1)S(1)}, bf16[1024,128]{1,0:T(8,128)(2,1)S(1)}, u32[]{:S(2)}, u32[]{:S(2)}) collective-permute-start(bf16[1024,128]{1,0:T(8,128)(2,1)S(1)} %broadcast_select_fusion.20), channel_id=1, source_target_pairs={{8,0},{12,4},{24,16},{28,20},{9,1},{13,5},{25,17},{29,21},{10,2},{... | collective-permute-start | bytes 786440 | tf_op jit(solution)/shard_map/ppermute | solution.py:27
  30.8 18.4 %collective-permute-start.11 = (bf16[2,1024,128]{2,1,0:T(8,128)(2,1)S(1)}, bf16[2,1024,128]{2,1,0:T(8,128)(2,1)S(1)}, u32[]{:S(2)}, u32[]{:S(2)}) collective-permute-start(bf16[2,1024,128]{2,1,0:T(8,128)(2,1)S(1)} %broadcast_select_fusion.7), channel_id=1, source_target_pairs={{0,4},{4,0},{8,12},{12,8},{16,20},{20,16},{24,28},{28,24},{1,5},{5... | collective-permute-start | bytes 1572872 | tf_op jit(solution)/shard_map/ppermute | solution.py:27
  31.2 18.8 %collective-permute-start.20 = (bf16[128,1024]{1,0:T(8,128)(2,1)S(1)}, bf16[128,1024]{1,0:T(8,128)(2,1)S(1)}, u32[]{:S(2)}, u32[]{:S(2)}) collective-permute-start(bf16[128,1024]{1,0:T(8,128)(2,1)S(1)} %get-tuple-element.59), channel_id=1, source_target_pairs={{0,8},{4,12},{8,0},{12,4},{16,24},{20,28},{24,16},{28,20},{1,9},{5... | collective-permute-start | bytes 786440 | tf_op jit(solution)/shard_map/ppermute | solution.py:27
  38.1 12.0 %collective-permute-start.18 = (bf16[128,1024]{1,0:T(8,128)(2,1)S(1)}, bf16[128,1024]{1,0:T(8,128)(2,1)S(1)}, u32[]{:S(2)}, u32[]{:S(2)}) collective-permute-start(bf16[128,1024]{1,0:T(8,128)(2,1)S(1)} %get-tuple-element.56), channel_id=1, source_target_pairs={{24,8},{28,12},{25,9},{29,13},{26,10},{30,14},{27,11},{31,15}} | collective-permute-start | bytes 786440 | tf_op jit(solution)/shard_map/ppermute | solution.py:27
  47.3 7.4 %collective-permute-start.2 = (bf16[2,1024,128]{2,1,0:T(8,128)(2,1)S(1)}, bf16[2,1024,128]{2,1,0:T(8,128)(2,1)S(1)}, u32[]{:S(2)}, u32[]{:S(2)}) collective-permute-start(bf16[2,1024,128]{2,1,0:T(8,128)(2,1)S(1)} %get-tuple-element.39), channel_id=1, source_target_pairs={{0,1},{1,0},{2,3},{3,2},{4,5},{5,4},{6,7},{7,6},{8,9},{9,8},{10,11... | collective-permute-start | bytes 1572872 | tf_op jit(solution)/shard_map/ppermute | solution.py:27
  49.3 17.7 %collective-permute-start.12 = (bf16[4,1024,128]{2,1,0:T(8,128)(2,1)S(1)}, bf16[4,1024,128]{2,1,0:T(8,128)(2,1)S(1)}, u32[]{:S(2)}, u32[]{:S(2)}) collective-permute-start(bf16[4,1024,128]{2,1,0:T(8,128)(2,1)S(1)} %pad_maximum_fusion), channel_id=1, source_target_pairs={{0,1},{1,0},{2,3},{3,2},{4,5},{5,4},{6,7},{7,6},{8,9},{9,8},{10,11... | collective-permute-start | bytes 3145736 | tf_op jit(solution)/shard_map/ppermute | solution.py:27
  50.2 16.4 %collective-permute-start.19 = (bf16[128,1024]{1,0:T(8,128)(2,1)S(1)}, bf16[128,1024]{1,0:T(8,128)(2,1)S(1)}, u32[]{:S(2)}, u32[]{:S(2)}) collective-permute-start(bf16[128,1024]{1,0:T(8,128)(2,1)S(1)} %broadcast_select_fusion.13), channel_id=1, source_target_pairs={{8,0},{12,4},{24,16},{28,20},{9,1},{13,5},{25,17},{29,21},{10,2},{... | collective-permute-start | bytes 786440 | tf_op jit(solution)/shard_map/ppermute | solution.py:27
  51.5 15.4 %collective-permute-start.21 = (bf16[128,1024]{1,0:T(8,128)(2,1)S(1)}, bf16[128,1024]{1,0:T(8,128)(2,1)S(1)}, u32[]{:S(2)}, u32[]{:S(2)}) collective-permute-start(bf16[128,1024]{1,0:T(8,128)(2,1)S(1)} %broadcast_select_fusion.10), channel_id=1, source_target_pairs={{0,16},{4,20},{8,24},{12,28},{16,0},{20,4},{24,8},{28,12},{1,17},{... | collective-permute-start | bytes 786440 | tf_op jit(solution)/shard_map/ppermute | solution.py:27
  54.7 29.2 %collective-permute-start.3 = (bf16[2,1024,128]{2,1,0:T(8,128)(2,1)S(1)}, bf16[2,1024,128]{2,1,0:T(8,128)(2,1)S(1)}, u32[]{:S(2)}, u32[]{:S(2)}) collective-permute-start(bf16[2,1024,128]{2,1,0:T(8,128)(2,1)S(1)} %broadcast_select_fusion.4), channel_id=1, source_target_pairs={{0,2},{1,3},{2,0},{3,1},{4,6},{5,7},{6,4},{7,5},{8,10},{9,11},{10,... | collective-permute-start | bytes 1572872 | tf_op jit(solution)/shard_map/ppermute | solution.py:27
  68.5 6.3 %collective-permute-start.15 = (bf16[2,128,128]{2,1,0:T(8,128)(2,1)S(1)}, bf16[2,128,128]{2,1,0:T(8,128)(2,1)S(1)}, u32[]{:S(2)}, u32[]{:S(2)}) collective-permute-start(bf16[2,128,128]{2,1,0:T(8,128)(2,1)S(1)} %get-tuple-element.51), channel_id=1, source_target_pairs={{0,24},{4,28},{8,16},{12,20},{16,8},{20,12},{24,0},{28,4},{1,25},{... | collective-permute-start | bytes 196616 | tf_op jit(solution)/shard_map/ppermute | solution.py:27
  68.9 6.9 %collective-permute-start.14 = (bf16[2,128,128]{2,1,0:T(8,128)(2,1)S(1)}, bf16[2,128,128]{2,1,0:T(8,128)(2,1)S(1)}, u32[]{:S(2)}, u32[]{:S(2)}) collective-permute-start(bf16[2,128,128]{2,1,0:T(8,128)(2,1)S(1)} %get-tuple-element.51), channel_id=1, source_target_pairs={{0,16},{4,20},{8,24},{12,28},{16,0},{20,4},{24,8},{28,12},{1,17},{... | collective-permute-start | bytes 196616 | tf_op jit(solution)/shard_map/ppermute | solution.py:27
  70.5 5.3 %collective-permute-start.13 = (bf16[2,128,128]{2,1,0:T(8,128)(2,1)S(1)}, bf16[2,128,128]{2,1,0:T(8,128)(2,1)S(1)}, u32[]{:S(2)}, u32[]{:S(2)}) collective-permute-start(bf16[2,128,128]{2,1,0:T(8,128)(2,1)S(1)} %get-tuple-element.51), channel_id=1, source_target_pairs={{0,8},{4,12},{8,0},{12,4},{16,24},{20,28},{24,16},{28,20},{1,9},{5... | collective-permute-start | bytes 196616 | tf_op jit(solution)/shard_map/ppermute | solution.py:27
  75.9 7.9 %collective-permute-start.23 = (bf16[2,384,128]{2,1,0:T(8,128)(2,1)S(1)}, bf16[2,384,128]{2,1,0:T(8,128)(2,1)S(1)}, u32[]{:S(2)}, u32[]{:S(2)}) collective-permute-start(bf16[2,384,128]{2,1,0:T(8,128)(2,1)S(1)} %get-tuple-element.106), channel_id=1, source_target_pairs={{0,4},{4,0},{8,12},{12,8},{16,20},{20,16},{24,28},{28,24},{1,5},{5... | collective-permute-start | bytes 589832 | tf_op jit(solution)/shard_map/ppermute | solution.py:27
  77.2 16.0 %collective-permute-start.22 = (bf16[2,128,1024]{2,1,0:T(8,128)(2,1)S(1)}, bf16[2,128,1024]{2,1,0:T(8,128)(2,1)S(1)}, u32[]{:S(2)}, u32[]{:S(2)}) collective-permute-start(bf16[2,128,1024]{2,1,0:T(8,128)(2,1)S(1)} %pad_maximum_fusion.1), channel_id=1, source_target_pairs={{0,4},{4,0},{8,12},{12,8},{16,20},{20,16},{24,28},{28,24},{1,5},{5... | collective-permute-start | bytes 1572872 | tf_op jit(solution)/shard_map/ppermute | solution.py:27
  84.1 9.3 %collective-permute-start.16 = (bf16[2,1024,128]{2,1,0:T(8,128)(2,1)S(1)}, bf16[2,1024,128]{2,1,0:T(8,128)(2,1)S(1)}, u32[]{:S(2)}, u32[]{:S(2)}) collective-permute-start(bf16[2,1024,128]{2,1,0:T(8,128)(2,1)S(1)} %broadcast_select_fusion.6), channel_id=1, source_target_pairs={{0,1},{1,0},{2,3},{3,2},{4,5},{5,4},{6,7},{7,6},{8,9},{9,8},{10,11... | collective-permute-start | bytes 1572872 | tf_op jit(solution)/shard_map/ppermute | solution.py:27
  85.5 8.0 %collective-permute-start.25 = (bf16[640,128]{1,0:T(8,128)(2,1)S(1)}, bf16[640,128]{1,0:T(8,128)(2,1)S(1)}, u32[]{:S(2)}, u32[]{:S(2)}) collective-permute-start(bf16[640,128]{1,0:T(8,128)(2,1)S(1)} %select_select_fusion), channel_id=1, source_target_pairs={{0,2},{1,3},{2,0},{3,1},{4,6},{5,7},{6,4},{7,5},{8,10},{9,11},{10,... | collective-permute-start | bytes 491528 | tf_op jit(solution)/shard_map/ppermute | solution.py:27
  (9 other events, 129.0 us)

commit v8 on v7

--- a/solution.py
+++ b/solution.py
@@ -240,8 +240,9 @@
                 cu = Lane(cu_k, after(cu_g, cv.mine), "col", cols_n, same_both)
                 near = swap(after(cv.mine, v_lanes[0].mine), "row", rows_n, 1)
                 cv_first, cv_second = joined(jnp.concatenate([cv.mine, near]), "col", cols_n, "side_c")
-            for lane in v_lanes:
-                lane.step(k, *follow)
+            if k < len(upper_bits(rows_n)) - 1:
+                for lane in v_lanes:
+                    lane.step(k, *follow)
         for m in range(len(cu.bits)):
             cu.step(m)
         moving, fixed = mines(u_lanes)
@@ -259,6 +260,9 @@
             out_specs=[WHOLE] * 2,
             compiler_params=params(),
         )(panel_order, solved, cv_first, cv_second)
+        for lane in v_lanes:
+            lane.step(len(lane.bits) - 1, foot)
+
         def at_root(bit):
             return jnp.stack([flag(("p2", bit), foot), flag(("p1", bit), foot)])
 

time: 103 us -> 109 us (1.058)
  waiting for transfers between devices: 44.1 us -> 55.6 us
  starting transfers between devices: 39.1 us -> 34.4 us
    ppermute x26, waiting for transfers between devices: 44.1 us -> 55.6 us  [swap(): return lax.ppermute(block, axis, [(s, s ^ bit) for s in senders])]
    ppermute x26, starting transfers between devices: 39.1 us -> 34.4 us  [swap(): return lax.ppermute(block, axis, [(s, s ^ bit) for s in senders])]
  transfers between devices with their start and end apart: 26 -> 26, of which waited for: 11 -> 13; matrix products, arithmetic and copies ran while one was open for 2% -> 1% of each run, Pallas kernels for 3% -> 2%
where the time goes in v8:
time: 109 us
  waiting for transfers between devices  55.6 us (51%)
  starting transfers between devices  34.4 us (32%)
  Pallas kernels  14.1 us (13%)
  local copies, waits for them, and re-layouts  2.72 us (2%)
  other arithmetic  1.89 us (2%)
    ppermute x26, waiting for transfers between devices, swap(): return lax.ppermute(block, axis, [(s, s ^ bit) for s in senders])  55.6 us
    ppermute x26, starting transfers between devices, swap(): return lax.ppermute(block, axis, [(s, s ^ bit) for s in senders])  34.4 us
    pallas_call x1, Pallas kernels, on_device(): pl.pallas_call(functools.partial(final_kernel, last_col=last['last_col'])...  8.56 us
    unnamed x18, local copies, waits for them, and re-layouts  2.63 us
    pallas_call x1, Pallas kernels, on_device(): pl.pallas_call(functools.partial(prep_kernel, rows_n=rows_n, cols_n=cols_...  2.42 us
  transfers between devices with their start and end apart: 26, of which 13 were waited for; matrix products, arithmetic and copies ran while one was open for 1% of the time, Pallas kernels for 2%

profile of v8, /device:TPU:0, one launch (start us, length us, event | category | flops | bytes accessed | tf_op | source)
XLA Modules:
  0.0 109.1 jit_solution(8634055693459063092)
XLA Ops:
  2.6 2.4 %shard_map.55 = (s32[23,1024]{1,0:T(8,128)S(1)}, bf16[1024,128]{1,0:T(8,128)(2,1)S(1)}, bf16[1024,128]{1,0:T(8,128)(2,1)S(1)}, bf16[1024,128]{1,0:T(8,128)(2,1)S...) custom-call(s32[2,2]{1,0:T(2,128)S(1)} %copy-done.4, ...), custom_call_target="tpu_custom_call" | custom-call | tf_op jit(solution)/shard_map/pallas_call | solution.py:194
  5.0 3.0 %collective-permute-start.4 = (bf16[1024,128]{1,0:T(8,128)(2,1)S(1)}, bf16[1024,128]{1,0:T(8,128)(2,1)S(1)}, u32[]{:S(2)}, u32[]{:S(2)}) collective-permute-start(bf16[1024,128]{1,0:T(8,128)(2,1)S(1)} %get-tuple-element.43), channel_id=1, source_target_pairs={{0,4},{4,0},{8,12},{12,8},{16,20},{20,16},{24,28},{28,24},{1,5},{5... | collective-permute-start | bytes 786440 | tf_op jit(solution)/shard_map/ppermute | solution.py:27
  8.1 6.3 %collective-permute-done.4 = bf16[1024,128]{1,0:T(8,128)(2,1)S(1)} collective-permute-done((bf16[1024,128]{1,0:T(8,128)(2,1)S(1)}, bf16[1024,128]{1,0:T(8,128)(2,1)S(1)}, u32[]{:S(2)}, u32[]{:S(2)}) %collective-permute-start.4) | collective-permute-done | bytes 262176 | tf_op jit(solution)/shard_map/ppermute | solution.py:27
  14.4 1.9 %collective-permute-start.8 = (bf16[1024,128]{1,0:T(8,128)(2,1)S(1)}, bf16[1024,128]{1,0:T(8,128)(2,1)S(1)}, u32[]{:S(2)}, u32[]{:S(2)}) collective-permute-start(bf16[1024,128]{1,0:T(8,128)(2,1)S(1)} %broadcast_select_fusion.18), channel_id=1, source_target_pairs={{0,8},{4,12},{8,0},{12,4},{16,24},{20,28},{24,16},{28,20},{1,9},{5... | collective-permute-start | bytes 786440 | tf_op jit(solution)/shard_map/ppermute | solution.py:27
  17.1 1.6 %collective-permute-start.1 = (bf16[2,1024,128]{2,1,0:T(8,128)(2,1)S(1)}, bf16[2,1024,128]{2,1,0:T(8,128)(2,1)S(1)}, u32[]{:S(2)}, u32[]{:S(2)}) collective-permute-start(bf16[2,1024,128]{2,1,0:T(8,128)(2,1)S(1)} %broadcast_select_fusion.5), channel_id=1, source_target_pairs={{0,2},{1,3},{2,0},{3,1},{4,6},{5,7},{6,4},{7,5},{8,10},{9,11},{10,... | collective-permute-start | bytes 1572872 | tf_op jit(solution)/shard_map/ppermute | solution.py:27
  18.7 3.3 %collective-permute-done.8 = bf16[1024,128]{1,0:T(8,128)(2,1)S(1)} collective-permute-done((bf16[1024,128]{1,0:T(8,128)(2,1)S(1)}, bf16[1024,128]{1,0:T(8,128)(2,1)S(1)}, u32[]{:S(2)}, u32[]{:S(2)}) %collective-permute-start.8) | collective-permute-done | bytes 262176 | tf_op jit(solution)/shard_map/ppermute | solution.py:27
  22.0 1.5 %collective-permute-start.10 = (bf16[128,1024]{1,0:T(8,128)(2,1)S(1)}, bf16[128,1024]{1,0:T(8,128)(2,1)S(1)}, u32[]{:S(2)}, u32[]{:S(2)}) collective-permute-start(bf16[128,1024]{1,0:T(8,128)(2,1)S(1)} %get-tuple-element.49), channel_id=1, source_target_pairs={{0,4},{4,0},{8,12},{12,8},{16,20},{20,16},{24,28},{28,24},{1,5},{5... | collective-permute-start | bytes 786440 | tf_op jit(solution)/shard_map/ppermute | solution.py:27
  25.0 3.7 %collective-permute-done.10 = bf16[128,1024]{1,0:T(8,128)(2,1)S(1)} collective-permute-done((bf16[128,1024]{1,0:T(8,128)(2,1)S(1)}, bf16[128,1024]{1,0:T(8,128)(2,1)S(1)}, u32[]{:S(2)}, u32[]{:S(2)}) %collective-permute-start.10) | collective-permute-done | bytes 262176 | tf_op jit(solution)/shard_map/ppermute | solution.py:27
  29.8 1.6 %collective-permute-start.11 = (bf16[2,1024,128]{2,1,0:T(8,128)(2,1)S(1)}, bf16[2,1024,128]{2,1,0:T(8,128)(2,1)S(1)}, u32[]{:S(2)}, u32[]{:S(2)}) collective-permute-start(bf16[2,1024,128]{2,1,0:T(8,128)(2,1)S(1)} %broadcast_select_fusion.7), channel_id=1, source_target_pairs={{0,4},{4,0},{8,12},{12,8},{16,20},{20,16},{24,28},{28,24},{1,5},{5... | collective-permute-start | bytes 1572872 | tf_op jit(solution)/shard_map/ppermute | solution.py:27
  31.4 1.3 %collective-permute-start.7 = (bf16[1024,128]{1,0:T(8,128)(2,1)S(1)}, bf16[1024,128]{1,0:T(8,128)(2,1)S(1)}, u32[]{:S(2)}, u32[]{:S(2)}) collective-permute-start(bf16[1024,128]{1,0:T(8,128)(2,1)S(1)} %broadcast_select_fusion.20), channel_id=1, source_target_pairs={{8,0},{12,4},{24,16},{28,20},{9,1},{13,5},{25,17},{29,21},{10,2},{... | collective-permute-start | bytes 786440 | tf_op jit(solution)/shard_map/ppermute | solution.py:27
  32.8 2.7 %collective-permute-start.9 = (bf16[1024,128]{1,0:T(8,128)(2,1)S(1)}, bf16[1024,128]{1,0:T(8,128)(2,1)S(1)}, u32[]{:S(2)}, u32[]{:S(2)}) collective-permute-start(bf16[1024,128]{1,0:T(8,128)(2,1)S(1)} %broadcast_select_fusion.16), channel_id=1, source_target_pairs={{0,16},{4,20},{8,24},{12,28},{16,0},{20,4},{24,8},{28,12},{1,17},{... | collective-permute-start | bytes 786440 | tf_op jit(solution)/shard_map/ppermute | solution.py:27
  35.5 5.8 %collective-permute-start.20 = (bf16[128,1024]{1,0:T(8,128)(2,1)S(1)}, bf16[128,1024]{1,0:T(8,128)(2,1)S(1)}, u32[]{:S(2)}, u32[]{:S(2)}) collective-permute-start(bf16[128,1024]{1,0:T(8,128)(2,1)S(1)} %get-tuple-element.59), channel_id=1, source_target_pairs={{0,8},{4,12},{8,0},{12,4},{16,24},{20,28},{24,16},{28,20},{1,9},{5... | collective-permute-start | bytes 786440 | tf_op jit(solution)/shard_map/ppermute | solution.py:27
  41.3 6.7 %collective-permute-done.7 = bf16[1024,128]{1,0:T(8,128)(2,1)S(1)} collective-permute-done((bf16[1024,128]{1,0:T(8,128)(2,1)S(1)}, bf16[1024,128]{1,0:T(8,128)(2,1)S(1)}, u32[]{:S(2)}, u32[]{:S(2)}) %collective-permute-start.7) | collective-permute-done | bytes 262176 | tf_op jit(solution)/shard_map/ppermute | solution.py:27
  49.0 1.6 %collective-permute-start.3 = (bf16[2,1024,128]{2,1,0:T(8,128)(2,1)S(1)}, bf16[2,1024,128]{2,1,0:T(8,128)(2,1)S(1)}, u32[]{:S(2)}, u32[]{:S(2)}) collective-permute-start(bf16[2,1024,128]{2,1,0:T(8,128)(2,1)S(1)} %broadcast_select_fusion.4), channel_id=1, source_target_pairs={{0,2},{1,3},{2,0},{3,1},{4,6},{5,7},{6,4},{7,5},{8,10},{9,11},{10,... | collective-permute-start | bytes 1572872 | tf_op jit(solution)/shard_map/ppermute | solution.py:27
  50.6 1.8 %shard_map.56.solved = bf16[2,1024,128]{2,1,0:T(8,128)(2,1)S(1)} custom-call(s32[2,2]{1,0:T(2,128)S(1)} %copy-done.4, bf16[2,1024,1024]{2,1,0:T(8,128)(2,1)S(1)} %copy-done, bf16[1024,128]{1,0:T(8,128)(2,1)S(1)} %broadcast_select_fusion.21.fixed, bf16[1024,128]{1,0:T(8,128)(2,1)S(1)} %broadcast_select_fusion.17.moving), custom_call_target="tpu_custom_call" | custom-call | tf_op jit(solution)/shard_map/pallas_call | solution.py:249
  52.5 10.8 %collective-permute-done.3 = bf16[2,1024,128]{2,1,0:T(8,128)(2,1)S(1)} collective-permute-done((bf16[2,1024,128]{2,1,0:T(8,128)(2,1)S(1)}, bf16[2,1024,128]{2,1,0:T(8,128)(2,1)S(1)}, u32[]{:S(2)}, u32[]{:S(2)}) %collective-permute-start.3) | collective-permute-done | bytes 524320 | tf_op jit(solution)/shard_map/ppermute | solution.py:27
  64.9 3.2 %collective-permute-start.15 = (bf16[2,128,128]{2,1,0:T(8,128)(2,1)S(1)}, bf16[2,128,128]{2,1,0:T(8,128)(2,1)S(1)}, u32[]{:S(2)}, u32[]{:S(2)}) collective-permute-start(bf16[2,128,128]{2,1,0:T(8,128)(2,1)S(1)} %get-tuple-element.51), channel_id=1, source_target_pairs={{0,24},{4,28},{8,16},{12,20},{16,8},{20,12},{24,0},{28,4},{1,25},{... | collective-permute-start | bytes 196616 | tf_op jit(solution)/shard_map/ppermute | solution.py:27
  70.7 1.8 %collective-permute-start.21 = (bf16[128,1024]{1,0:T(8,128)(2,1)S(1)}, bf16[128,1024]{1,0:T(8,128)(2,1)S(1)}, u32[]{:S(2)}, u32[]{:S(2)}) collective-permute-start(bf16[128,1024]{1,0:T(8,128)(2,1)S(1)} %broadcast_select_fusion.10), channel_id=1, source_target_pairs={{0,16},{4,20},{8,24},{12,28},{16,0},{20,4},{24,8},{28,12},{1,17},{... | collective-permute-start | bytes 786440 | tf_op jit(solution)/shard_map/ppermute | solution.py:27
  73.6 6.2 %collective-permute-done.13 = bf16[2,128,128]{2,1,0:T(8,128)(2,1)S(1)} collective-permute-done((bf16[2,128,128]{2,1,0:T(8,128)(2,1)S(1)}, bf16[2,128,128]{2,1,0:T(8,128)(2,1)S(1)}, u32[]{:S(2)}, u32[]{:S(2)}) %collective-permute-start.13) | collective-permute-done | bytes 65568 | tf_op jit(solution)/shard_map/ppermute | solution.py:27
  80.6 4.4 %collective-permute-done.19 = bf16[128,1024]{1,0:T(8,128)(2,1)S(1)} collective-permute-done((bf16[128,1024]{1,0:T(8,128)(2,1)S(1)}, bf16[128,1024]{1,0:T(8,128)(2,1)S(1)}, u32[]{:S(2)}, u32[]{:S(2)}) %collective-permute-start.19) | collective-permute-done | bytes 262176 | tf_op jit(solution)/shard_map/ppermute | solution.py:27
  87.3 1.6 %collective-permute-start.25 = (bf16[640,128]{1,0:T(8,128)(2,1)S(1)}, bf16[640,128]{1,0:T(8,128)(2,1)S(1)}, u32[]{:S(2)}, u32[]{:S(2)}) collective-permute-start(bf16[640,128]{1,0:T(8,128)(2,1)S(1)} %select_select_fusion), channel_id=1, source_target_pairs={{0,2},{1,3},{2,0},{3,1},{4,6},{5,7},{6,4},{7,5},{8,10},{9,11},{10,... | collective-permute-start | bytes 491528 | tf_op jit(solution)/shard_map/ppermute | solution.py:27
  88.9 4.6 %collective-permute-done.25 = bf16[640,128]{1,0:T(8,128)(2,1)S(1)} collective-permute-done((bf16[640,128]{1,0:T(8,128)(2,1)S(1)}, bf16[640,128]{1,0:T(8,128)(2,1)S(1)}, u32[]{:S(2)}, u32[]{:S(2)}) %collective-permute-start.25) | collective-permute-done | bytes 163872 | tf_op jit(solution)/shard_map/ppermute | solution.py:27
  93.7 6.5 %collective-permute-done.22 = bf16[2,128,1024]{2,1,0:T(8,128)(2,1)S(1)} collective-permute-done((bf16[2,128,1024]{2,1,0:T(8,128)(2,1)S(1)}, bf16[2,128,1024]{2,1,0:T(8,128)(2,1)S(1)}, u32[]{:S(2)}, u32[]{:S(2)}) %collective-permute-start.22) | collective-permute-done | bytes 524320 | tf_op jit(solution)/shard_map/ppermute | solution.py:27
  100.6 8.6 %shard_map.58 = bf16[2,2,1024,1024]{3,2,1,0:T(8,128)(2,1)} custom-call(s32[2,2]{1,0:T(2,128)S(1)} %copy-done.4, s32[2,2]{1,0:T(2,128)S(1)} %copy-done.6, bf16[2,2,1024,128]{3,2,1,0:T(8,128)(2,1)S(1)} %copy-done.2, bf16[2,2,128,1024]{3,2,1,0:T(8,128)(2,1)S(1)} %copy-done.3, bf16[2,1024,128]{2,1,0:T(8,128)(2,1)S(1)} %get-tuple-element.76.first, ...), custom_call_target="tpu_custom_call" | custom-call | tf_op jit(solution)/shard_map/pallas_call | solution.py:291
  (90 shorter events, 16.0 us)
Async XLA Ops:
  5.0 9.3 %collective-permute-start.4 = (bf16[1024,128]{1,0:T(8,128)(2,1)S(1)}, bf16[1024,128]{1,0:T(8,128)(2,1)S(1)}, u32[]{:S(2)}, u32[]{:S(2)}) collective-permute-start(bf16[1024,128]{1,0:T(8,128)(2,1)S(1)} %get-tuple-element.43), channel_id=1, source_target_pairs={{0,4},{4,0},{8,12},{12,8},{16,20},{20,16},{24,28},{28,24},{1,5},{5... | collective-permute-start | bytes 786440 | tf_op jit(solution)/shard_map/ppermute | solution.py:27
  8.0 6.3 %collective-permute-start = (bf16[2,1024,128]{2,1,0:T(8,128)(2,1)S(1)}, bf16[2,1024,128]{2,1,0:T(8,128)(2,1)S(1)}, u32[]{:S(2)}, u32[]{:S(2)}) collective-permute-start(bf16[2,1024,128]{2,1,0:T(8,128)(2,1)S(1)} %get-tuple-element.38), channel_id=1, source_target_pairs={{0,1},{1,0},{2,3},{3,2},{4,5},{5,4},{6,7},{7,6},{8,9},{9,8},{10,11... | collective-permute-start | bytes 1572872 | tf_op jit(solution)/shard_map/ppermute | solution.py:27
  14.4 7.6 %collective-permute-start.8 = (bf16[1024,128]{1,0:T(8,128)(2,1)S(1)}, bf16[1024,128]{1,0:T(8,128)(2,1)S(1)}, u32[]{:S(2)}, u32[]{:S(2)}) collective-permute-start(bf16[1024,128]{1,0:T(8,128)(2,1)S(1)} %broadcast_select_fusion.18), channel_id=1, source_target_pairs={{0,8},{4,12},{8,0},{12,4},{16,24},{20,28},{24,16},{28,20},{1,9},{5... | collective-permute-start | bytes 786440 | tf_op jit(solution)/shard_map/ppermute | solution.py:27
  16.5 7.8 %collective-permute-start.5 = (bf16[1024,128]{1,0:T(8,128)(2,1)S(1)}, bf16[1024,128]{1,0:T(8,128)(2,1)S(1)}, u32[]{:S(2)}, u32[]{:S(2)}) collective-permute-start(bf16[1024,128]{1,0:T(8,128)(2,1)S(1)} %get-tuple-element.44), channel_id=1, source_target_pairs={{28,24},{29,25},{30,26},{31,27}} | collective-permute-start | bytes 786440 | tf_op jit(solution)/shard_map/ppermute | solution.py:27
  17.1 12.6 %collective-permute-start.1 = (bf16[2,1024,128]{2,1,0:T(8,128)(2,1)S(1)}, bf16[2,1024,128]{2,1,0:T(8,128)(2,1)S(1)}, u32[]{:S(2)}, u32[]{:S(2)}) collective-permute-start(bf16[2,1024,128]{2,1,0:T(8,128)(2,1)S(1)} %broadcast_select_fusion.5), channel_id=1, source_target_pairs={{0,2},{1,3},{2,0},{3,1},{4,6},{5,7},{6,4},{7,5},{8,10},{9,11},{10,... | collective-permute-start | bytes 1572872 | tf_op jit(solution)/shard_map/ppermute | solution.py:27
  22.0 6.6 %collective-permute-start.10 = (bf16[128,1024]{1,0:T(8,128)(2,1)S(1)}, bf16[128,1024]{1,0:T(8,128)(2,1)S(1)}, u32[]{:S(2)}, u32[]{:S(2)}) collective-permute-start(bf16[128,1024]{1,0:T(8,128)(2,1)S(1)} %get-tuple-element.49), channel_id=1, source_target_pairs={{0,4},{4,0},{8,12},{12,8},{16,20},{20,16},{24,28},{28,24},{1,5},{5... | collective-permute-start | bytes 786440 | tf_op jit(solution)/shard_map/ppermute | solution.py:27
  23.5 5.2 %collective-permute-start.17 = (bf16[128,1024]{1,0:T(8,128)(2,1)S(1)}, bf16[128,1024]{1,0:T(8,128)(2,1)S(1)}, u32[]{:S(2)}, u32[]{:S(2)}) collective-permute-start(bf16[128,1024]{1,0:T(8,128)(2,1)S(1)} %get-tuple-element.55), channel_id=1, source_target_pairs={{28,24},{29,25},{30,26},{31,27}} | collective-permute-start | bytes 786440 | tf_op jit(solution)/shard_map/ppermute | solution.py:27
  24.3 7.1 %collective-permute-start.6 = (bf16[1024,128]{1,0:T(8,128)(2,1)S(1)}, bf16[1024,128]{1,0:T(8,128)(2,1)S(1)}, u32[]{:S(2)}, u32[]{:S(2)}) collective-permute-start(bf16[1024,128]{1,0:T(8,128)(2,1)S(1)} %broadcast_select_fusion.19), channel_id=1, source_target_pairs={{24,8},{28,12},{25,9},{29,13},{26,10},{30,14},{27,11},{31,15}} | collective-permute-start | bytes 786440 | tf_op jit(solution)/shard_map/ppermute | solution.py:27
  29.8 18.9 %collective-permute-start.11 = (bf16[2,1024,128]{2,1,0:T(8,128)(2,1)S(1)}, bf16[2,1024,128]{2,1,0:T(8,128)(2,1)S(1)}, u32[]{:S(2)}, u32[]{:S(2)}) collective-permute-start(bf16[2,1024,128]{2,1,0:T(8,128)(2,1)S(1)} %broadcast_select_fusion.7), channel_id=1, source_target_pairs={{0,4},{4,0},{8,12},{12,8},{16,20},{20,16},{24,28},{28,24},{1,5},{5... | collective-permute-start | bytes 1572872 | tf_op jit(solution)/shard_map/ppermute | solution.py:27
  31.4 16.6 %collective-permute-start.7 = (bf16[1024,128]{1,0:T(8,128)(2,1)S(1)}, bf16[1024,128]{1,0:T(8,128)(2,1)S(1)}, u32[]{:S(2)}, u32[]{:S(2)}) collective-permute-start(bf16[1024,128]{1,0:T(8,128)(2,1)S(1)} %broadcast_select_fusion.20), channel_id=1, source_target_pairs={{8,0},{12,4},{24,16},{28,20},{9,1},{13,5},{25,17},{29,21},{10,2},{... | collective-permute-start | bytes 786440 | tf_op jit(solution)/shard_map/ppermute | solution.py:27
  32.7 16.2 %collective-permute-start.2 = (bf16[2,1024,128]{2,1,0:T(8,128)(2,1)S(1)}, bf16[2,1024,128]{2,1,0:T(8,128)(2,1)S(1)}, u32[]{:S(2)}, u32[]{:S(2)}) collective-permute-start(bf16[2,1024,128]{2,1,0:T(8,128)(2,1)S(1)} %get-tuple-element.39), channel_id=1, source_target_pairs={{0,1},{1,0},{2,3},{3,2},{4,5},{5,4},{6,7},{7,6},{8,9},{9,8},{10,11... | collective-permute-start | bytes 1572872 | tf_op jit(solution)/shard_map/ppermute | solution.py:27
  32.8 17.7 %collective-permute-start.9 = (bf16[1024,128]{1,0:T(8,128)(2,1)S(1)}, bf16[1024,128]{1,0:T(8,128)(2,1)S(1)}, u32[]{:S(2)}, u32[]{:S(2)}) collective-permute-start(bf16[1024,128]{1,0:T(8,128)(2,1)S(1)} %broadcast_select_fusion.16), channel_id=1, source_target_pairs={{0,16},{4,20},{8,24},{12,28},{16,0},{20,4},{24,8},{28,12},{1,17},{... | collective-permute-start | bytes 786440 | tf_op jit(solution)/shard_map/ppermute | solution.py:27
  35.5 16.9 %collective-permute-start.20 = (bf16[128,1024]{1,0:T(8,128)(2,1)S(1)}, bf16[128,1024]{1,0:T(8,128)(2,1)S(1)}, u32[]{:S(2)}, u32[]{:S(2)}) collective-permute-start(bf16[128,1024]{1,0:T(8,128)(2,1)S(1)} %get-tuple-element.59), channel_id=1, source_target_pairs={{0,8},{4,12},{8,0},{12,4},{16,24},{20,28},{24,16},{28,20},{1,9},{5... | collective-permute-start | bytes 786440 | tf_op jit(solution)/shard_map/ppermute | solution.py:27
  48.8 14.6 %collective-permute-start.12 = (bf16[4,1024,128]{2,1,0:T(8,128)(2,1)S(1)}, bf16[4,1024,128]{2,1,0:T(8,128)(2,1)S(1)}, u32[]{:S(2)}, u32[]{:S(2)}) collective-permute-start(bf16[4,1024,128]{2,1,0:T(8,128)(2,1)S(1)} %pad_maximum_fusion), channel_id=1, source_target_pairs={{0,1},{1,0},{2,3},{3,2},{4,5},{5,4},{6,7},{7,6},{8,9},{9,8},{10,11... | collective-permute-start | bytes 3145736 | tf_op jit(solution)/shard_map/ppermute | solution.py:27
  49.0 14.4 %collective-permute-start.3 = (bf16[2,1024,128]{2,1,0:T(8,128)(2,1)S(1)}, bf16[2,1024,128]{2,1,0:T(8,128)(2,1)S(1)}, u32[]{:S(2)}, u32[]{:S(2)}) collective-permute-start(bf16[2,1024,128]{2,1,0:T(8,128)(2,1)S(1)} %broadcast_select_fusion.4), channel_id=1, source_target_pairs={{0,2},{1,3},{2,0},{3,1},{4,6},{5,7},{6,4},{7,5},{8,10},{9,11},{10,... | collective-permute-start | bytes 1572872 | tf_op jit(solution)/shard_map/ppermute | solution.py:27
  64.9 7.5 %collective-permute-start.15 = (bf16[2,128,128]{2,1,0:T(8,128)(2,1)S(1)}, bf16[2,128,128]{2,1,0:T(8,128)(2,1)S(1)}, u32[]{:S(2)}, u32[]{:S(2)}) collective-permute-start(bf16[2,128,128]{2,1,0:T(8,128)(2,1)S(1)} %get-tuple-element.51), channel_id=1, source_target_pairs={{0,24},{4,28},{8,16},{12,20},{16,8},{20,12},{24,0},{28,4},{1,25},{... | collective-permute-start | bytes 196616 | tf_op jit(solution)/shard_map/ppermute | solution.py:27
  68.2 5.5 %collective-permute-start.14 = (bf16[2,128,128]{2,1,0:T(8,128)(2,1)S(1)}, bf16[2,128,128]{2,1,0:T(8,128)(2,1)S(1)}, u32[]{:S(2)}, u32[]{:S(2)}) collective-permute-start(bf16[2,128,128]{2,1,0:T(8,128)(2,1)S(1)} %get-tuple-element.51), channel_id=1, source_target_pairs={{0,16},{4,20},{8,24},{12,28},{16,0},{20,4},{24,8},{28,12},{1,17},{... | collective-permute-start | bytes 196616 | tf_op jit(solution)/shard_map/ppermute | solution.py:27
  68.2 11.6 %collective-permute-start.13 = (bf16[2,128,128]{2,1,0:T(8,128)(2,1)S(1)}, bf16[2,128,128]{2,1,0:T(8,128)(2,1)S(1)}, u32[]{:S(2)}, u32[]{:S(2)}) collective-permute-start(bf16[2,128,128]{2,1,0:T(8,128)(2,1)S(1)} %get-tuple-element.51), channel_id=1, source_target_pairs={{0,8},{4,12},{8,0},{12,4},{16,24},{20,28},{24,16},{28,20},{1,9},{5... | collective-permute-start | bytes 196616 | tf_op jit(solution)/shard_map/ppermute | solution.py:27
  69.4 15.6 %collective-permute-start.19 = (bf16[128,1024]{1,0:T(8,128)(2,1)S(1)}, bf16[128,1024]{1,0:T(8,128)(2,1)S(1)}, u32[]{:S(2)}, u32[]{:S(2)}) collective-permute-start(bf16[128,1024]{1,0:T(8,128)(2,1)S(1)} %broadcast_select_fusion.13), channel_id=1, source_target_pairs={{8,0},{12,4},{24,16},{28,20},{9,1},{13,5},{25,17},{29,21},{10,2},{... | collective-permute-start | bytes 786440 | tf_op jit(solution)/shard_map/ppermute | solution.py:27
  70.7 14.3 %collective-permute-start.21 = (bf16[128,1024]{1,0:T(8,128)(2,1)S(1)}, bf16[128,1024]{1,0:T(8,128)(2,1)S(1)}, u32[]{:S(2)}, u32[]{:S(2)}) collective-permute-start(bf16[128,1024]{1,0:T(8,128)(2,1)S(1)} %broadcast_select_fusion.10), channel_id=1, source_target_pairs={{0,16},{4,20},{8,24},{12,28},{16,0},{20,4},{24,8},{28,12},{1,17},{... | collective-permute-start | bytes 786440 | tf_op jit(solution)/shard_map/ppermute | solution.py:27
  79.8 5.7 %collective-permute-start.23 = (bf16[2,384,128]{2,1,0:T(8,128)(2,1)S(1)}, bf16[2,384,128]{2,1,0:T(8,128)(2,1)S(1)}, u32[]{:S(2)}, u32[]{:S(2)}) collective-permute-start(bf16[2,384,128]{2,1,0:T(8,128)(2,1)S(1)} %get-tuple-element.106), channel_id=1, source_target_pairs={{0,4},{4,0},{8,12},{12,8},{16,20},{20,16},{24,28},{28,24},{1,5},{5... | collective-permute-start | bytes 589832 | tf_op jit(solution)/shard_map/ppermute | solution.py:27
  80.6 8.3 %collective-permute-start.16 = (bf16[2,1024,128]{2,1,0:T(8,128)(2,1)S(1)}, bf16[2,1024,128]{2,1,0:T(8,128)(2,1)S(1)}, u32[]{:S(2)}, u32[]{:S(2)}) collective-permute-start(bf16[2,1024,128]{2,1,0:T(8,128)(2,1)S(1)} %broadcast_select_fusion.6), channel_id=1, source_target_pairs={{0,1},{1,0},{2,3},{3,2},{4,5},{5,4},{6,7},{7,6},{8,9},{9,8},{10,11... | collective-permute-start | bytes 1572872 | tf_op jit(solution)/shard_map/ppermute | solution.py:27
  85.9 14.4 %collective-permute-start.22 = (bf16[2,128,1024]{2,1,0:T(8,128)(2,1)S(1)}, bf16[2,128,1024]{2,1,0:T(8,128)(2,1)S(1)}, u32[]{:S(2)}, u32[]{:S(2)}) collective-permute-start(bf16[2,128,1024]{2,1,0:T(8,128)(2,1)S(1)} %pad_maximum_fusion.1), channel_id=1, source_target_pairs={{0,4},{4,0},{8,12},{12,8},{16,20},{20,16},{24,28},{28,24},{1,5},{5... | collective-permute-start | bytes 1572872 | tf_op jit(solution)/shard_map/ppermute | solution.py:27
  87.3 6.3 %collective-permute-start.25 = (bf16[640,128]{1,0:T(8,128)(2,1)S(1)}, bf16[640,128]{1,0:T(8,128)(2,1)S(1)}, u32[]{:S(2)}, u32[]{:S(2)}) collective-permute-start(bf16[640,128]{1,0:T(8,128)(2,1)S(1)} %select_select_fusion), channel_id=1, source_target_pairs={{0,2},{1,3},{2,0},{3,1},{4,6},{5,7},{6,4},{7,5},{8,10},{9,11},{10,... | collective-permute-start | bytes 491528 | tf_op jit(solution)/shard_map/ppermute | solution.py:27
  (9 other events, 163.4 us)

commit v9 on v7

--- a/solution.py
+++ b/solution.py
@@ -259,6 +259,8 @@
             out_specs=[WHOLE] * 2,
             compiler_params=params(),
         )(panel_order, solved, cv_first, cv_second)
+        made = foot
+
         def at_root(bit):
             return jnp.stack([flag(("p2", bit), foot), flag(("p1", bit), foot)])
 
@@ -279,7 +281,7 @@
             stays = jnp.where(early, flag(("q2", bit), edge), flag(("q1", bit), edge))
             edge = jnp.where(stays, edge, got)
 
-        moving, fixed = (after(x, foot) for x in mines(v_lanes))
+        moving, fixed = (after(x, made) for x in mines(v_lanes))
         mine = jnp.stack([choose("row_first", fixed, moving), choose("row_first", moving, fixed)])
         vj0, vj1 = joined(mine, "row", rows_n, "side_r")
         vp1, vp2 = (jnp.stack([vj0[s], vj1[s]]) for s in range(2))

time: 103 us -> 103 us (level)
  no operation moved by 1% of the time
where the time goes in v9:
time: 103 us; the launch traced here: 102 us
  waiting for transfers between devices  44.1 us (43%)
  starting transfers between devices  39.1 us (38%)
  Pallas kernels  14.1 us (14%)
  local copies, waits for them, and re-layouts  2.72 us (3%)
  other arithmetic  1.88 us (2%)
    ppermute x26, waiting for transfers between devices, swap(): return lax.ppermute(block, axis, [(s, s ^ bit) for s in senders])  44.1 us
    ppermute x26, starting transfers between devices, swap(): return lax.ppermute(block, axis, [(s, s ^ bit) for s in senders])  39.1 us
    pallas_call x1, Pallas kernels, on_device(): pl.pallas_call(functools.partial(final_kernel, last_col=last['last_col'])...  8.57 us
    unnamed x18, local copies, waits for them, and re-layouts  2.63 us
    pallas_call x1, Pallas kernels, on_device(): pl.pallas_call(functools.partial(prep_kernel, rows_n=rows_n, cols_n=cols_...  2.42 us
  transfers between devices with their start and end apart: 26, of which 11 were waited for; matrix products, arithmetic and copies ran while one was open for 2% of the time, Pallas kernels for 3%

profile of v9, /device:TPU:0, one launch (start us, length us, event | category | flops | bytes accessed | tf_op | source)
XLA Modules:
  0.0 102.3 jit_solution(14415460277544897050)
XLA Ops:
  2.6 2.4 %shard_map.55 = (s32[23,1024]{1,0:T(8,128)S(1)}, bf16[1024,128]{1,0:T(8,128)(2,1)S(1)}, bf16[1024,128]{1,0:T(8,128)(2,1)S(1)}, bf16[1024,128]{1,0:T(8,128)(2,1)S...) custom-call(s32[2,2]{1,0:T(2,128)S(1)} %copy-done.4, ...), custom_call_target="tpu_custom_call" | custom-call | tf_op jit(solution)/shard_map/pallas_call | solution.py:194
  5.0 3.0 %collective-permute-start.4 = (bf16[1024,128]{1,0:T(8,128)(2,1)S(1)}, bf16[1024,128]{1,0:T(8,128)(2,1)S(1)}, u32[]{:S(2)}, u32[]{:S(2)}) collective-permute-start(bf16[1024,128]{1,0:T(8,128)(2,1)S(1)} %get-tuple-element.43), channel_id=1, source_target_pairs={{0,4},{4,0},{8,12},{12,8},{16,20},{20,16},{24,28},{28,24},{1,5},{5... | collective-permute-start | bytes 786440 | tf_op jit(solution)/shard_map/ppermute | solution.py:27
  8.2 6.1 %collective-permute-done.4 = bf16[1024,128]{1,0:T(8,128)(2,1)S(1)} collective-permute-done((bf16[1024,128]{1,0:T(8,128)(2,1)S(1)}, bf16[1024,128]{1,0:T(8,128)(2,1)S(1)}, u32[]{:S(2)}, u32[]{:S(2)}) %collective-permute-start.4) | collective-permute-done | bytes 262176 | tf_op jit(solution)/shard_map/ppermute | solution.py:27
  15.1 1.9 %collective-permute-start.8 = (bf16[1024,128]{1,0:T(8,128)(2,1)S(1)}, bf16[1024,128]{1,0:T(8,128)(2,1)S(1)}, u32[]{:S(2)}, u32[]{:S(2)}) collective-permute-start(bf16[1024,128]{1,0:T(8,128)(2,1)S(1)} %broadcast_select_fusion.18), channel_id=1, source_target_pairs={{0,8},{4,12},{8,0},{12,4},{16,24},{20,28},{24,16},{28,20},{1,9},{5... | collective-permute-start | bytes 786440 | tf_op jit(solution)/shard_map/ppermute | solution.py:27
  17.0 1.6 %collective-permute-start.1 = (bf16[2,1024,128]{2,1,0:T(8,128)(2,1)S(1)}, bf16[2,1024,128]{2,1,0:T(8,128)(2,1)S(1)}, u32[]{:S(2)}, u32[]{:S(2)}) collective-permute-start(bf16[2,1024,128]{2,1,0:T(8,128)(2,1)S(1)} %broadcast_select_fusion.5), channel_id=1, source_target_pairs={{0,2},{1,3},{2,0},{3,1},{4,6},{5,7},{6,4},{7,5},{8,10},{9,11},{10,... | collective-permute-start | bytes 1572872 | tf_op jit(solution)/shard_map/ppermute | solution.py:27
  19.3 3.4 %collective-permute-done.8 = bf16[1024,128]{1,0:T(8,128)(2,1)S(1)} collective-permute-done((bf16[1024,128]{1,0:T(8,128)(2,1)S(1)}, bf16[1024,128]{1,0:T(8,128)(2,1)S(1)}, u32[]{:S(2)}, u32[]{:S(2)}) %collective-permute-start.8) | collective-permute-done | bytes 262176 | tf_op jit(solution)/shard_map/ppermute | solution.py:27
  22.7 1.5 %collective-permute-start.10 = (bf16[128,1024]{1,0:T(8,128)(2,1)S(1)}, bf16[128,1024]{1,0:T(8,128)(2,1)S(1)}, u32[]{:S(2)}, u32[]{:S(2)}) collective-permute-start(bf16[128,1024]{1,0:T(8,128)(2,1)S(1)} %get-tuple-element.49), channel_id=1, source_target_pairs={{0,4},{4,0},{8,12},{12,8},{16,20},{20,16},{24,28},{28,24},{1,5},{5... | collective-permute-start | bytes 786440 | tf_op jit(solution)/shard_map/ppermute | solution.py:27
  24.9 4.3 %collective-permute-start.9 = (bf16[1024,128]{1,0:T(8,128)(2,1)S(1)}, bf16[1024,128]{1,0:T(8,128)(2,1)S(1)}, u32[]{:S(2)}, u32[]{:S(2)}) collective-permute-start(bf16[1024,128]{1,0:T(8,128)(2,1)S(1)} %broadcast_select_fusion.16), channel_id=1, source_target_pairs={{0,16},{4,20},{8,24},{12,28},{16,0},{20,4},{24,8},{28,12},{1,17},{... | collective-permute-start | bytes 786440 | tf_op jit(solution)/shard_map/ppermute | solution.py:27
  29.3 1.3 %collective-permute-start.7 = (bf16[1024,128]{1,0:T(8,128)(2,1)S(1)}, bf16[1024,128]{1,0:T(8,128)(2,1)S(1)}, u32[]{:S(2)}, u32[]{:S(2)}) collective-permute-start(bf16[1024,128]{1,0:T(8,128)(2,1)S(1)} %broadcast_select_fusion.20), channel_id=1, source_target_pairs={{8,0},{12,4},{24,16},{28,20},{9,1},{13,5},{25,17},{29,21},{10,2},{... | collective-permute-start | bytes 786440 | tf_op jit(solution)/shard_map/ppermute | solution.py:27
  31.2 6.9 %collective-permute-start.20 = (bf16[128,1024]{1,0:T(8,128)(2,1)S(1)}, bf16[128,1024]{1,0:T(8,128)(2,1)S(1)}, u32[]{:S(2)}, u32[]{:S(2)}) collective-permute-start(bf16[128,1024]{1,0:T(8,128)(2,1)S(1)} %get-tuple-element.59), channel_id=1, source_target_pairs={{0,8},{4,12},{8,0},{12,4},{16,24},{20,28},{24,16},{28,20},{1,9},{5... | collective-permute-start | bytes 786440 | tf_op jit(solution)/shard_map/ppermute | solution.py:27
  38.8 8.4 %collective-permute-done.7 = bf16[1024,128]{1,0:T(8,128)(2,1)S(1)} collective-permute-done((bf16[1024,128]{1,0:T(8,128)(2,1)S(1)}, bf16[1024,128]{1,0:T(8,128)(2,1)S(1)}, u32[]{:S(2)}, u32[]{:S(2)}) %collective-permute-start.7) | collective-permute-done | bytes 262176 | tf_op jit(solution)/shard_map/ppermute | solution.py:27
  47.4 1.8 %shard_map.56.solved = bf16[2,1024,128]{2,1,0:T(8,128)(2,1)S(1)} custom-call(s32[2,2]{1,0:T(2,128)S(1)} %copy-done.4, bf16[2,1024,1024]{2,1,0:T(8,128)(2,1)S(1)} %copy-done, bf16[1024,128]{1,0:T(8,128)(2,1)S(1)} %broadcast_select_fusion.21.fixed, bf16[1024,128]{1,0:T(8,128)(2,1)S(1)} %broadcast_select_fusion.17.moving), custom_call_target="tpu_custom_call" | custom-call | tf_op jit(solution)/shard_map/pallas_call | solution.py:248
  50.2 1.3 %collective-permute-start.19 = (bf16[128,1024]{1,0:T(8,128)(2,1)S(1)}, bf16[128,1024]{1,0:T(8,128)(2,1)S(1)}, u32[]{:S(2)}, u32[]{:S(2)}) collective-permute-start(bf16[128,1024]{1,0:T(8,128)(2,1)S(1)} %broadcast_select_fusion.13), channel_id=1, source_target_pairs={{8,0},{12,4},{24,16},{28,20},{9,1},{13,5},{25,17},{29,21},{10,2},{... | collective-permute-start | bytes 786440 | tf_op jit(solution)/shard_map/ppermute | solution.py:27
  51.5 3.2 %collective-permute-start.21 = (bf16[128,1024]{1,0:T(8,128)(2,1)S(1)}, bf16[128,1024]{1,0:T(8,128)(2,1)S(1)}, u32[]{:S(2)}, u32[]{:S(2)}) collective-permute-start(bf16[128,1024]{1,0:T(8,128)(2,1)S(1)} %broadcast_select_fusion.10), channel_id=1, source_target_pairs={{0,16},{4,20},{8,24},{12,28},{16,0},{20,4},{24,8},{28,12},{1,17},{... | collective-permute-start | bytes 786440 | tf_op jit(solution)/shard_map/ppermute | solution.py:27
  54.7 1.6 %collective-permute-start.3 = (bf16[2,1024,128]{2,1,0:T(8,128)(2,1)S(1)}, bf16[2,1024,128]{2,1,0:T(8,128)(2,1)S(1)}, u32[]{:S(2)}, u32[]{:S(2)}) collective-permute-start(bf16[2,1024,128]{2,1,0:T(8,128)(2,1)S(1)} %broadcast_select_fusion.4), channel_id=1, source_target_pairs={{0,2},{1,3},{2,0},{3,1},{4,6},{5,7},{6,4},{7,5},{8,10},{9,11},{10,... | collective-permute-start | bytes 1572872 | tf_op jit(solution)/shard_map/ppermute | solution.py:27
  56.3 10.2 %collective-permute-done.19 = bf16[128,1024]{1,0:T(8,128)(2,1)S(1)} collective-permute-done((bf16[128,1024]{1,0:T(8,128)(2,1)S(1)}, bf16[128,1024]{1,0:T(8,128)(2,1)S(1)}, u32[]{:S(2)}, u32[]{:S(2)}) %collective-permute-start.19) | collective-permute-done | bytes 262176 | tf_op jit(solution)/shard_map/ppermute | solution.py:27
  67.1 1.3 %shard_map.57 = (bf16[2,512,128]{2,1,0:T(8,128)(2,1)S(1)}, bf16[2,128,128]{2,1,0:T(8,128)(2,1)S(1)}) custom-call(s32[2,2]{1,0:T(2,128)S(1)} %copy-done.4, bf16[2,1024,128]{2,1,0:T(8,128)(2,1)S(1)} %shard_map.56.solved, bf16[4,1024,128]{2,1,0:T(8,128)(2,1)S(1)} %get-tuple-element.72.first, bf16[4,1024,128]{2,1,0:T(8,128)(2,1)S(1)} %get-tuple-element.71.second), custom_call_target="tpu_custom_call" | custom-call | tf_op jit(solution)/shard_map/pallas_call | solution.py:255
  68.9 1.6 %collective-permute-start.14 = (bf16[2,128,128]{2,1,0:T(8,128)(2,1)S(1)}, bf16[2,128,128]{2,1,0:T(8,128)(2,1)S(1)}, u32[]{:S(2)}, u32[]{:S(2)}) collective-permute-start(bf16[2,128,128]{2,1,0:T(8,128)(2,1)S(1)} %get-tuple-element.51), channel_id=1, source_target_pairs={{0,16},{4,20},{8,24},{12,28},{16,0},{20,4},{24,8},{28,12},{1,17},{... | collective-permute-start | bytes 196616 | tf_op jit(solution)/shard_map/ppermute | solution.py:27
  70.5 2.4 %collective-permute-start.13 = (bf16[2,128,128]{2,1,0:T(8,128)(2,1)S(1)}, bf16[2,128,128]{2,1,0:T(8,128)(2,1)S(1)}, u32[]{:S(2)}, u32[]{:S(2)}) collective-permute-start(bf16[2,128,128]{2,1,0:T(8,128)(2,1)S(1)} %get-tuple-element.51), channel_id=1, source_target_pairs={{0,8},{4,12},{8,0},{12,4},{16,24},{20,28},{24,16},{28,20},{1,9},{5... | collective-permute-start | bytes 196616 | tf_op jit(solution)/shard_map/ppermute | solution.py:27
  72.9 1.8 %collective-permute-done.15 = bf16[2,128,128]{2,1,0:T(8,128)(2,1)S(1)} collective-permute-done((bf16[2,128,128]{2,1,0:T(8,128)(2,1)S(1)}, bf16[2,128,128]{2,1,0:T(8,128)(2,1)S(1)}, u32[]{:S(2)}, u32[]{:S(2)}) %collective-permute-start.15) | collective-permute-done | bytes 65568 | tf_op jit(solution)/shard_map/ppermute | solution.py:27
  78.2 5.6 %collective-permute-done.23.swapped = bf16[2,384,128]{2,1,0:T(8,128)(2,1)S(1)} collective-permute-done((bf16[2,384,128]{2,1,0:T(8,128)(2,1)S(1)}, bf16[2,384,128]{2,1,0:T(8,128)(2,1)S(1)}, u32[]{:S(2)}, u32[]{:S(2)}) %collective-permute-start.23) | collective-permute-done | bytes 196640 | tf_op jit(solution)/shard_map/ppermute | solution.py:27
  85.5 1.6 %collective-permute-start.25 = (bf16[640,128]{1,0:T(8,128)(2,1)S(1)}, bf16[640,128]{1,0:T(8,128)(2,1)S(1)}, u32[]{:S(2)}, u32[]{:S(2)}) collective-permute-start(bf16[640,128]{1,0:T(8,128)(2,1)S(1)} %select_select_fusion), channel_id=1, source_target_pairs={{0,2},{1,3},{2,0},{3,1},{4,6},{5,7},{6,4},{7,5},{8,10},{9,11},{10,... | collective-permute-start | bytes 491528 | tf_op jit(solution)/shard_map/ppermute | solution.py:27
  87.1 6.1 %collective-permute-done.22 = bf16[2,128,1024]{2,1,0:T(8,128)(2,1)S(1)} collective-permute-done((bf16[2,128,1024]{2,1,0:T(8,128)(2,1)S(1)}, bf16[2,128,1024]{2,1,0:T(8,128)(2,1)S(1)}, u32[]{:S(2)}, u32[]{:S(2)}) %collective-permute-start.22) | collective-permute-done | bytes 524320 | tf_op jit(solution)/shard_map/ppermute | solution.py:27
  93.8 8.6 %shard_map.58 = bf16[2,2,1024,1024]{3,2,1,0:T(8,128)(2,1)} custom-call(s32[2,2]{1,0:T(2,128)S(1)} %copy-done.4, s32[2,2]{1,0:T(2,128)S(1)} %copy-done.6, bf16[2,2,1024,128]{3,2,1,0:T(8,128)(2,1)S(1)} %copy-done.2, bf16[2,2,128,1024]{3,2,1,0:T(8,128)(2,1)S(1)} %copy-done.3, bf16[2,1024,128]{2,1,0:T(8,128)(2,1)S(1)} %get-tuple-element.76.first, ...), custom_call_target="tpu_custom_call" | custom-call | tf_op jit(solution)/shard_map/pallas_call | solution.py:289
  (90 shorter events, 14.1 us)
Async XLA Ops:
  5.0 9.3 %collective-permute-start.4 = (bf16[1024,128]{1,0:T(8,128)(2,1)S(1)}, bf16[1024,128]{1,0:T(8,128)(2,1)S(1)}, u32[]{:S(2)}, u32[]{:S(2)}) collective-permute-start(bf16[1024,128]{1,0:T(8,128)(2,1)S(1)} %get-tuple-element.43), channel_id=1, source_target_pairs={{0,4},{4,0},{8,12},{12,8},{16,20},{20,16},{24,28},{28,24},{1,5},{5... | collective-permute-start | bytes 786440 | tf_op jit(solution)/shard_map/ppermute | solution.py:27
  8.0 7.0 %collective-permute-start = (bf16[2,1024,128]{2,1,0:T(8,128)(2,1)S(1)}, bf16[2,1024,128]{2,1,0:T(8,128)(2,1)S(1)}, u32[]{:S(2)}, u32[]{:S(2)}) collective-permute-start(bf16[2,1024,128]{2,1,0:T(8,128)(2,1)S(1)} %get-tuple-element.38), channel_id=1, source_target_pairs={{0,1},{1,0},{2,3},{3,2},{4,5},{5,4},{6,7},{7,6},{8,9},{9,8},{10,11... | collective-permute-start | bytes 1572872 | tf_op jit(solution)/shard_map/ppermute | solution.py:27
  15.1 7.6 %collective-permute-start.8 = (bf16[1024,128]{1,0:T(8,128)(2,1)S(1)}, bf16[1024,128]{1,0:T(8,128)(2,1)S(1)}, u32[]{:S(2)}, u32[]{:S(2)}) collective-permute-start(bf16[1024,128]{1,0:T(8,128)(2,1)S(1)} %broadcast_select_fusion.18), channel_id=1, source_target_pairs={{0,8},{4,12},{8,0},{12,4},{16,24},{20,28},{24,16},{28,20},{1,9},{5... | collective-permute-start | bytes 786440 | tf_op jit(solution)/shard_map/ppermute | solution.py:27
  17.0 13.7 %collective-permute-start.1 = (bf16[2,1024,128]{2,1,0:T(8,128)(2,1)S(1)}, bf16[2,1024,128]{2,1,0:T(8,128)(2,1)S(1)}, u32[]{:S(2)}, u32[]{:S(2)}) collective-permute-start(bf16[2,1024,128]{2,1,0:T(8,128)(2,1)S(1)} %broadcast_select_fusion.5), channel_id=1, source_target_pairs={{0,2},{1,3},{2,0},{3,1},{4,6},{5,7},{6,4},{7,5},{8,10},{9,11},{10,... | collective-permute-start | bytes 1572872 | tf_op jit(solution)/shard_map/ppermute | solution.py:27
  18.6 10.6 %collective-permute-start.6 = (bf16[1024,128]{1,0:T(8,128)(2,1)S(1)}, bf16[1024,128]{1,0:T(8,128)(2,1)S(1)}, u32[]{:S(2)}, u32[]{:S(2)}) collective-permute-start(bf16[1024,128]{1,0:T(8,128)(2,1)S(1)} %broadcast_select_fusion.19), channel_id=1, source_target_pairs={{24,8},{28,12},{25,9},{29,13},{26,10},{30,14},{27,11},{31,15}} | collective-permute-start | bytes 786440 | tf_op jit(solution)/shard_map/ppermute | solution.py:27
  22.7 7.9 %collective-permute-start.10 = (bf16[128,1024]{1,0:T(8,128)(2,1)S(1)}, bf16[128,1024]{1,0:T(8,128)(2,1)S(1)}, u32[]{:S(2)}, u32[]{:S(2)}) collective-permute-start(bf16[128,1024]{1,0:T(8,128)(2,1)S(1)} %get-tuple-element.49), channel_id=1, source_target_pairs={{0,4},{4,0},{8,12},{12,8},{16,20},{20,16},{24,28},{28,24},{1,5},{5... | collective-permute-start | bytes 786440 | tf_op jit(solution)/shard_map/ppermute | solution.py:27
  24.2 6.4 %collective-permute-start.17 = (bf16[128,1024]{1,0:T(8,128)(2,1)S(1)}, bf16[128,1024]{1,0:T(8,128)(2,1)S(1)}, u32[]{:S(2)}, u32[]{:S(2)}) collective-permute-start(bf16[128,1024]{1,0:T(8,128)(2,1)S(1)} %get-tuple-element.55), channel_id=1, source_target_pairs={{28,24},{29,25},{30,26},{31,27}} | collective-permute-start | bytes 786440 | tf_op jit(solution)/shard_map/ppermute | solution.py:27
  24.9 22.4 %collective-permute-start.9 = (bf16[1024,128]{1,0:T(8,128)(2,1)S(1)}, bf16[1024,128]{1,0:T(8,128)(2,1)S(1)}, u32[]{:S(2)}, u32[]{:S(2)}) collective-permute-start(bf16[1024,128]{1,0:T(8,128)(2,1)S(1)} %broadcast_select_fusion.16), channel_id=1, source_target_pairs={{0,16},{4,20},{8,24},{12,28},{16,0},{20,4},{24,8},{28,12},{1,17},{... | collective-permute-start | bytes 786440 | tf_op jit(solution)/shard_map/ppermute | solution.py:27
  29.3 18.0 %collective-permute-start.7 = (bf16[1024,128]{1,0:T(8,128)(2,1)S(1)}, bf16[1024,128]{1,0:T(8,128)(2,1)S(1)}, u32[]{:S(2)}, u32[]{:S(2)}) collective-permute-start(bf16[1024,128]{1,0:T(8,128)(2,1)S(1)} %broadcast_select_fusion.20), channel_id=1, source_target_pairs={{8,0},{12,4},{24,16},{28,20},{9,1},{13,5},{25,17},{29,21},{10,2},{... | collective-permute-start | bytes 786440 | tf_op jit(solution)/shard_map/ppermute | solution.py:27
  30.8 18.4 %collective-permute-start.11 = (bf16[2,1024,128]{2,1,0:T(8,128)(2,1)S(1)}, bf16[2,1024,128]{2,1,0:T(8,128)(2,1)S(1)}, u32[]{:S(2)}, u32[]{:S(2)}) collective-permute-start(bf16[2,1024,128]{2,1,0:T(8,128)(2,1)S(1)} %broadcast_select_fusion.7), channel_id=1, source_target_pairs={{0,4},{4,0},{8,12},{12,8},{16,20},{20,16},{24,28},{28,24},{1,5},{5... | collective-permute-start | bytes 1572872 | tf_op jit(solution)/shard_map/ppermute | solution.py:27
  31.2 18.8 %collective-permute-start.20 = (bf16[128,1024]{1,0:T(8,128)(2,1)S(1)}, bf16[128,1024]{1,0:T(8,128)(2,1)S(1)}, u32[]{:S(2)}, u32[]{:S(2)}) collective-permute-start(bf16[128,1024]{1,0:T(8,128)(2,1)S(1)} %get-tuple-element.59), channel_id=1, source_target_pairs={{0,8},{4,12},{8,0},{12,4},{16,24},{20,28},{24,16},{28,20},{1,9},{5... | collective-permute-start | bytes 786440 | tf_op jit(solution)/shard_map/ppermute | solution.py:27
  38.1 12.0 %collective-permute-start.18 = (bf16[128,1024]{1,0:T(8,128)(2,1)S(1)}, bf16[128,1024]{1,0:T(8,128)(2,1)S(1)}, u32[]{:S(2)}, u32[]{:S(2)}) collective-permute-start(bf16[128,1024]{1,0:T(8,128)(2,1)S(1)} %get-tuple-element.56), channel_id=1, source_target_pairs={{24,8},{28,12},{25,9},{29,13},{26,10},{30,14},{27,11},{31,15}} | collective-permute-start | bytes 786440 | tf_op jit(solution)/shard_map/ppermute | solution.py:27
  47.3 7.4 %collective-permute-start.2 = (bf16[2,1024,128]{2,1,0:T(8,128)(2,1)S(1)}, bf16[2,1024,128]{2,1,0:T(8,128)(2,1)S(1)}, u32[]{:S(2)}, u32[]{:S(2)}) collective-permute-start(bf16[2,1024,128]{2,1,0:T(8,128)(2,1)S(1)} %get-tuple-element.39), channel_id=1, source_target_pairs={{0,1},{1,0},{2,3},{3,2},{4,5},{5,4},{6,7},{7,6},{8,9},{9,8},{10,11... | collective-permute-start | bytes 1572872 | tf_op jit(solution)/shard_map/ppermute | solution.py:27
  49.3 17.7 %collective-permute-start.12 = (bf16[4,1024,128]{2,1,0:T(8,128)(2,1)S(1)}, bf16[4,1024,128]{2,1,0:T(8,128)(2,1)S(1)}, u32[]{:S(2)}, u32[]{:S(2)}) collective-permute-start(bf16[4,1024,128]{2,1,0:T(8,128)(2,1)S(1)} %pad_maximum_fusion), channel_id=1, source_target_pairs={{0,1},{1,0},{2,3},{3,2},{4,5},{5,4},{6,7},{7,6},{8,9},{9,8},{10,11... | collective-permute-start | bytes 3145736 | tf_op jit(solution)/shard_map/ppermute | solution.py:27
  50.2 16.4 %collective-permute-start.19 = (bf16[128,1024]{1,0:T(8,128)(2,1)S(1)}, bf16[128,1024]{1,0:T(8,128)(2,1)S(1)}, u32[]{:S(2)}, u32[]{:S(2)}) collective-permute-start(bf16[128,1024]{1,0:T(8,128)(2,1)S(1)} %broadcast_select_fusion.13), channel_id=1, source_target_pairs={{8,0},{12,4},{24,16},{28,20},{9,1},{13,5},{25,17},{29,21},{10,2},{... | collective-permute-start | bytes 786440 | tf_op jit(solution)/shard_map/ppermute | solution.py:27
  51.5 15.4 %collective-permute-start.21 = (bf16[128,1024]{1,0:T(8,128)(2,1)S(1)}, bf16[128,1024]{1,0:T(8,128)(2,1)S(1)}, u32[]{:S(2)}, u32[]{:S(2)}) collective-permute-start(bf16[128,1024]{1,0:T(8,128)(2,1)S(1)} %broadcast_select_fusion.10), channel_id=1, source_target_pairs={{0,16},{4,20},{8,24},{12,28},{16,0},{20,4},{24,8},{28,12},{1,17},{... | collective-permute-start | bytes 786440 | tf_op jit(solution)/shard_map/ppermute | solution.py:27
  54.7 29.2 %collective-permute-start.3 = (bf16[2,1024,128]{2,1,0:T(8,128)(2,1)S(1)}, bf16[2,1024,128]{2,1,0:T(8,128)(2,1)S(1)}, u32[]{:S(2)}, u32[]{:S(2)}) collective-permute-start(bf16[2,1024,128]{2,1,0:T(8,128)(2,1)S(1)} %broadcast_select_fusion.4), channel_id=1, source_target_pairs={{0,2},{1,3},{2,0},{3,1},{4,6},{5,7},{6,4},{7,5},{8,10},{9,11},{10,... | collective-permute-start | bytes 1572872 | tf_op jit(solution)/shard_map/ppermute | solution.py:27
  68.5 6.3 %collective-permute-start.15 = (bf16[2,128,128]{2,1,0:T(8,128)(2,1)S(1)}, bf16[2,128,128]{2,1,0:T(8,128)(2,1)S(1)}, u32[]{:S(2)}, u32[]{:S(2)}) collective-permute-start(bf16[2,128,128]{2,1,0:T(8,128)(2,1)S(1)} %get-tuple-element.51), channel_id=1, source_target_pairs={{0,24},{4,28},{8,16},{12,20},{16,8},{20,12},{24,0},{28,4},{1,25},{... | collective-permute-start | bytes 196616 | tf_op jit(solution)/shard_map/ppermute | solution.py:27
  68.9 6.9 %collective-permute-start.14 = (bf16[2,128,128]{2,1,0:T(8,128)(2,1)S(1)}, bf16[2,128,128]{2,1,0:T(8,128)(2,1)S(1)}, u32[]{:S(2)}, u32[]{:S(2)}) collective-permute-start(bf16[2,128,128]{2,1,0:T(8,128)(2,1)S(1)} %get-tuple-element.51), channel_id=1, source_target_pairs={{0,16},{4,20},{8,24},{12,28},{16,0},{20,4},{24,8},{28,12},{1,17},{... | collective-permute-start | bytes 196616 | tf_op jit(solution)/shard_map/ppermute | solution.py:27
  70.5 5.3 %collective-permute-start.13 = (bf16[2,128,128]{2,1,0:T(8,128)(2,1)S(1)}, bf16[2,128,128]{2,1,0:T(8,128)(2,1)S(1)}, u32[]{:S(2)}, u32[]{:S(2)}) collective-permute-start(bf16[2,128,128]{2,1,0:T(8,128)(2,1)S(1)} %get-tuple-element.51), channel_id=1, source_target_pairs={{0,8},{4,12},{8,0},{12,4},{16,24},{20,28},{24,16},{28,20},{1,9},{5... | collective-permute-start | bytes 196616 | tf_op jit(solution)/shard_map/ppermute | solution.py:27
  75.9 7.9 %collective-permute-start.23 = (bf16[2,384,128]{2,1,0:T(8,128)(2,1)S(1)}, bf16[2,384,128]{2,1,0:T(8,128)(2,1)S(1)}, u32[]{:S(2)}, u32[]{:S(2)}) collective-permute-start(bf16[2,384,128]{2,1,0:T(8,128)(2,1)S(1)} %get-tuple-element.106), channel_id=1, source_target_pairs={{0,4},{4,0},{8,12},{12,8},{16,20},{20,16},{24,28},{28,24},{1,5},{5... | collective-permute-start | bytes 589832 | tf_op jit(solution)/shard_map/ppermute | solution.py:27
  77.2 16.0 %collective-permute-start.22 = (bf16[2,128,1024]{2,1,0:T(8,128)(2,1)S(1)}, bf16[2,128,1024]{2,1,0:T(8,128)(2,1)S(1)}, u32[]{:S(2)}, u32[]{:S(2)}) collective-permute-start(bf16[2,128,1024]{2,1,0:T(8,128)(2,1)S(1)} %pad_maximum_fusion.1), channel_id=1, source_target_pairs={{0,4},{4,0},{8,12},{12,8},{16,20},{20,16},{24,28},{28,24},{1,5},{5... | collective-permute-start | bytes 1572872 | tf_op jit(solution)/shard_map/ppermute | solution.py:27
  84.1 9.4 %collective-permute-start.16 = (bf16[2,1024,128]{2,1,0:T(8,128)(2,1)S(1)}, bf16[2,1024,128]{2,1,0:T(8,128)(2,1)S(1)}, u32[]{:S(2)}, u32[]{:S(2)}) collective-permute-start(bf16[2,1024,128]{2,1,0:T(8,128)(2,1)S(1)} %broadcast_select_fusion.6), channel_id=1, source_target_pairs={{0,1},{1,0},{2,3},{3,2},{4,5},{5,4},{6,7},{7,6},{8,9},{9,8},{10,11... | collective-permute-start | bytes 1572872 | tf_op jit(solution)/shard_map/ppermute | solution.py:27
  85.5 8.0 %collective-permute-start.25 = (bf16[640,128]{1,0:T(8,128)(2,1)S(1)}, bf16[640,128]{1,0:T(8,128)(2,1)S(1)}, u32[]{:S(2)}, u32[]{:S(2)}) collective-permute-start(bf16[640,128]{1,0:T(8,128)(2,1)S(1)} %select_select_fusion), channel_id=1, source_target_pairs={{0,2},{1,3},{2,0},{3,1},{4,6},{5,7},{6,4},{7,5},{8,10},{9,11},{10,... | collective-permute-start | bytes 491528 | tf_op jit(solution)/shard_map/ppermute | solution.py:27
  (9 other events, 129.0 us)
